TPU v7x, 256 devices: a whole 4x4x8 slice. The times are simulated.
256 devices in a mesh: tile: 64 (over z, y_hi, x), copy: 4 (over y_lo, core).
Axes of the slice: x: 4, y: 4 (y_hi: 2, y_lo: 2; y = y_hi * 2 + y_lo), z: 8, core: 2. Of those that a mesh axis runs over, the one named last changes fastest.
Arguments:
- pair_rep: bfloat16 [1536, 1536, 128], P('tile', 'copy'), may hold values from -6 to 6
- single: bfloat16 [1536, 384], P('tile'), may hold values from -6 to 6
- atom_feat: bfloat16 [12288, 128], P('tile'), may hold values from -6 to 6
- coords: float32 [8, 3, 12288], P('copy', None, 'tile'), may hold values from -96 to 96
- levels: int32 [8], P('copy'), may hold values from 0 to 199
- window_offset: int32 [384], P('tile'), may hold values from 0 to 32
- atom_token: int32 [12288], P('tile'), may hold values from 0 to 1535, as said below
- trans_in: bfloat16 [128, 1024], replicated, may hold values from -0.5 to 0.5
- trans_out: bfloat16 [512, 128], replicated, may hold values from -0.25 to 0.25
- bias_weight: bfloat16 [128, 16], replicated, may hold values from -0.5 to 0.5
- single_weight: bfloat16 [384, 768], replicated, may hold values from -0.3125 to 0.3125
- coord_weight: float32 [3, 128], replicated, may hold values from -3.5 to 3.5
- atom_weight: bfloat16 [128, 384], replicated, as said below
- agg_weight: bfloat16 [128, 768], replicated, may hold values from -0.5 to 0.5
- token_weight: bfloat16 [768, 2304], replicated, as said below
- noise_weight: float32 [768], replicated, may hold values from -6 to 6
- cotangent: bfloat16 [8, 1536, 768], P('copy', 'tile'), may hold values from -6 to 6
Outputs:
- token_update: bfloat16 [8, 1536, 768], P('copy', 'tile')
- grad_pair: bfloat16 [1536, 1536, 128], P('tile', 'copy')
Inputs may be any that keep to these rules, and one draw needn't show every extreme that they name: atom_token never falls; atoms k * 192 to (k + 1) * 192 - 1 belong to tokens k * 24 to (k + 1) * 24 - 1, and every token has one atom or more. `atom_weight`: columns are queries, keys and values in this order. `token_weight`: columns are queries, keys and values in this order.
All inputs are finite; a program needn't handle non-finite values.
Results may differ from a plain program's by a relative error of at most 0.007.
The roundings to bfloat16 on the way count: a program that leaves them out, or rounds other values in their place, can miss the bound.
Values may be sent and summed in bfloat16 or wider, within the bound.
No kernel may reach another device: no remote copies, remote signals or barrier semaphores. Data moves between devices by JAX's collectives and lax.ppermute only.
A program may use at most 128 MiB of HBM per device.

v0:
```python
import math

import jax
import jax.numpy as jnp
from jax import lax
from jax.sharding import PartitionSpec as P

A_HEAD = 32
Q_BLOCK = 32
K_WIN = 128
LEVELS = 200


epsilon = 1e-05
sigma_data = 16.0
sigma_top = 160.0
sigma_low = 0.0004
rho_power = 7.0
excluded = -1e30
highest_precision = lax.Precision.HIGHEST


def with_halo(block, sides, width):
    for axis, dim in sides:
        count = lax.axis_size(axis)
        forward = [(i, i + 1) for i in range(count - 1)]
        backward = [(target, source) for source, target in forward]
        low = lax.ppermute(
            lax.slice_in_dim(block, block.shape[dim] - width, None, axis=dim), axis, forward
        )
        high = lax.ppermute(lax.slice_in_dim(block, 0, width, axis=dim), axis, backward)
        block = jnp.concatenate([low, block, high], axis=dim)
    return block


def norm_parts(value):
    average = jnp.mean(value, axis=-1, keepdims=True)
    centred = value - average
    spread = jnp.mean(centred * centred, axis=-1, keepdims=True)
    scale = lax.rsqrt(spread + epsilon)
    return (centred * scale, scale)


def noise_scales(levels):
    fraction = levels.astype(jnp.float32) / LEVELS
    highest = sigma_top ** (1.0 / rho_power)
    lowest = sigma_low ** (1.0 / rho_power)
    sigma = sigma_data * (highest + fraction * (lowest - highest)) ** rho_power
    input_scale = lax.rsqrt(sigma * sigma + sigma_data * sigma_data)
    noise_code = 0.25 * jnp.log(sigma / sigma_data)
    return (input_scale, noise_code)


def soft_weights(scores):
    highest = jnp.max(scores, axis=-1, keepdims=True)
    spread = jnp.exp(scores - highest)
    return spread / jnp.sum(spread, axis=-1, keepdims=True)


def condition_pair(row_block, trans_in, trans_out):
    normal, _ = norm_parts(row_block.astype(jnp.float32))
    gate_up = jnp.einsum(
        "ijc,cf->ijf", normal.astype(jnp.bfloat16), trans_in, preferred_element_type=jnp.float32
    )
    inner = trans_out.shape[0]
    hidden = (jax.nn.silu(gate_up[..., :inner]) * gate_up[..., inner:]).astype(jnp.bfloat16)
    pair_delta = jnp.einsum("ijf,fc->ijc", hidden, trans_out, preferred_element_type=jnp.float32)
    return (row_block.astype(jnp.float32) + pair_delta).astype(jnp.bfloat16)


def on_device(
    pair_rep,
    single,
    atom_feat,
    coords,
    levels,
    window_offset,
    atom_token,
    trans_in,
    trans_out,
    bias_weight,
    single_weight,
    coord_weight,
    atom_weight,
    agg_weight,
    token_weight,
    noise_weight,
    cotangent,
):
    tile_index = lax.axis_index("tile")
    copies, tok_rows, width = cotangent.shape
    atom_rows, atom_width = atom_feat.shape
    heads = bias_weight.shape[1]
    head_size = width // heads
    atom_heads = atom_width // A_HEAD
    rim_width = K_WIN // 2
    blocks = atom_rows // Q_BLOCK
    token_float = token_weight.astype(jnp.float32)
    input_scale, noise_code = noise_scales(levels)
    scaled = coords * input_scale[:, None, None]
    atoms = atom_feat.astype(jnp.float32)[None]
    for axis_index in range(3):
        atoms = atoms + scaled[:, axis_index, :, None] * coord_weight[axis_index][None, None, :]
    atom_normal, _ = norm_parts(atoms)
    atom_proj = jnp.einsum(
        "nac,cf->naf",
        atom_normal.astype(jnp.bfloat16),
        atom_weight,
        preferred_element_type=jnp.float32,
    )
    queries = atom_proj[..., :atom_width].reshape(copies, blocks, Q_BLOCK, atom_heads, A_HEAD)
    extended = with_halo(atom_proj[..., atom_width:], (("tile", 1),), rim_width)
    window_index = (
        Q_BLOCK * jnp.arange(blocks, dtype=jnp.int32)[:, None]
        + window_offset[:, None]
        + jnp.arange(K_WIN, dtype=jnp.int32)[None, :]
    )
    position = window_index - rim_width + tile_index * atom_rows
    total_atoms = atom_rows * lax.axis_size("tile")
    inside = (position >= 0) & (position < total_atoms)
    window = extended[:, window_index]
    window_keys = window[..., :atom_width].reshape(copies, blocks, K_WIN, atom_heads, A_HEAD)
    values = window[..., atom_width:].reshape(copies, blocks, K_WIN, atom_heads, A_HEAD)
    scores = jnp.einsum(
        "nbqhd,nbkhd->nbhqk", queries, window_keys, precision=highest_precision
    ) / math.sqrt(A_HEAD)
    scores = jnp.where(inside[None, :, None, None, :], scores, excluded)
    soft_probs = soft_weights(scores).astype(jnp.bfloat16)
    attended = jnp.einsum(
        "nbhqk,nbkhd->nbqhd", soft_probs.astype(jnp.float32), values, precision=highest_precision
    ).reshape(copies, atom_rows, atom_width)
    atom_out = (atoms + attended).astype(jnp.bfloat16)
    hidden = jax.nn.relu(
        jnp.einsum("nac,cf->naf", atom_out, agg_weight, preferred_element_type=jnp.float32)
    )
    local_token = atom_token - tile_index * tok_rows
    member = (local_token[None, :] == jnp.arange(tok_rows, dtype=jnp.int32)[:, None]).astype(
        jnp.float32
    )
    token_sums = jnp.einsum("ta,naf->ntf", member, hidden, precision=highest_precision)
    counts = jnp.sum(member, axis=1)
    token_feat = token_sums / counts[None, :, None]
    single_term = jnp.dot(single, single_weight, preferred_element_type=jnp.float32)
    token_normal, _ = norm_parts(token_feat)
    token_in = (
        token_normal + single_term[None] + noise_code[:, None, None] * noise_weight[None, None, :]
    )
    token_proj = jnp.einsum("ntc,cf->ntf", token_in, token_float, precision=highest_precision)
    query_rows = token_proj[..., :width]
    key_values = lax.all_gather(token_proj[..., width:], "tile", axis=1, tiled=True)
    rows_block = math.gcd(tok_rows, 8)
    pair_blocks = pair_rep.reshape(
        tok_rows // rows_block, rows_block, pair_rep.shape[1], pair_rep.shape[2]
    )

    def condition_block(row_block):
        return condition_pair(row_block, trans_in, trans_out)

    pair_cond = lax.map(condition_block, pair_blocks).reshape(pair_rep.shape)
    cond_normal, cond_scale = norm_parts(pair_cond.astype(jnp.float32))
    cond_normed = cond_normal.astype(jnp.bfloat16)
    cot_float = cotangent.astype(jnp.float32)
    local_bias = jnp.einsum(
        "ijc,ch->hij", cond_normed, bias_weight, preferred_element_type=jnp.float32
    )
    head_bias = lax.all_gather(local_bias, "copy", axis=2, tiled=True)
    all_tokens = key_values.shape[1]
    query_heads = query_rows.reshape(copies, tok_rows, heads, head_size)
    key_heads = key_values[..., :width].reshape(copies, all_tokens, heads, head_size)
    value_heads = key_values[..., width:].reshape(copies, all_tokens, heads, head_size)
    scores = jnp.einsum(
        "nihd,njhd->nhij", query_heads, key_heads, precision=highest_precision
    ) / math.sqrt(head_size)
    scores = scores + head_bias[None]
    exact = soft_weights(scores)
    soft_probs = exact.astype(jnp.bfloat16)
    update = jnp.einsum(
        "nhij,njhd->nihd", soft_probs.astype(jnp.float32), value_heads, precision=highest_precision
    )
    update = update.reshape(copies, tok_rows, width).astype(jnp.bfloat16)
    cot_heads = cot_float.reshape(copies, tok_rows, heads, head_size)
    prob_grad = jnp.einsum("nihd,njhd->nhij", cot_heads, value_heads, precision=highest_precision)
    inner = jnp.sum(exact * prob_grad, axis=-1, keepdims=True)
    partial_grad = jnp.sum(exact * (prob_grad - inner), axis=0)
    bias_grad = lax.psum_scatter(partial_grad, "copy", scatter_dimension=2, tiled=True)
    grad_normal = jnp.einsum(
        "hij,ch->ijc", bias_grad, bias_weight.astype(jnp.float32), precision=highest_precision
    )
    gradient = (
        grad_normal
        - jnp.mean(grad_normal, axis=-1, keepdims=True)
        - cond_normal * jnp.mean(grad_normal * cond_normal, axis=-1, keepdims=True)
    )
    return (update, (gradient * cond_scale).astype(jnp.bfloat16))


def solution(mesh):
    placed = (
        P("tile", "copy", None),
        P("tile", None),
        P("tile", None),
        P("copy", None, "tile"),
        P("copy"),
        P("tile"),
        P("tile"),
        P(),
        P(),
        P(),
        P(),
        P(),
        P(),
        P(),
        P(),
        P(),
        P("copy", "tile", None),
    )
    return jax.shard_map(
        on_device,
        mesh=mesh,
        in_specs=placed,
        out_specs=(P("copy", "tile", None), P("tile", "copy", None)),
        check_vma=False,
    )
```

profile of v0, /device:TPU:1, one launch (start us, length us, event | category | flops | bytes accessed | tf_op | source)
XLA Modules:
  0.0 446.6 jit_solution(11869408031589089903)
XLA Ops:
  14.6 4.6 %collective-permute-start = (f32[2,64,256]{2,1,0:T(8,128)}, f32[2,64,256]{2,1,0:T(8,128)}, u32[]{:S(2)}, u32[]{:S(2)}) collective-permute-start(f32[2,64,256]{2,1,0:T(8,128)} %get-tuple-element.52), channel_id=1, source_target_pairs={{0,4},{4,8},{8,12},{12,16},{16,20},{20,24},{24,28},{28,32},{32,36}... | collective-permute-start | bytes 393224 | tf_op jit(solution)/shard_map/ppermute | solution.py:28
  20.5 32.5 %while.10 = (s32[]{:T(128)}, bf16[3,8,384,128]{3,2,1,0:T(8,128)(2,1)}, bf16[3,8,384,128]{3,2,1,0:T(8,128)(2,1)}, bf16[128,1024]{1,0:T(8,128)(2,1)}, bf16[512,128]{1,0:T(8,128)(2,1)}, /*index=5*/s32[]{:T(128)}) while((s32[]{:T(128)}, bf16[3,8,384,128]{3,2,1,0:T(8,128)(2,1)}, bf16[3,8,384,128]{3,2,1,0:T(8,128)(2,1)}, ...), condition=%wide.region_10.11_spmd, body=%wide.region_7.10_spmd.sunk | while | flops 1222511616 | bytes 30126200 | solution.py:159
  20.5 1.4 convert_reduce_fusion.4
  21.9 2.0 fusion.129
  24.0 3.6 fusion.130
  27.6 3.7 fusion.131
  31.3 1.4 convert_reduce_fusion.4
  32.8 2.0 fusion.129
  34.8 3.6 fusion.130
  38.4 3.7 fusion.131
  42.1 1.4 convert_reduce_fusion.4
  43.6 2.0 fusion.129
  45.6 3.6 fusion.130
  49.2 3.7 fusion.131
  53.0 3.0 convert_reduce_fusion.1
  55.9 4.6 %copy.51 = f32[3,8,384,128]{2,3,1,0:T(8,128)} copy(bf16[3,8,384,128]{3,2,1,0:T(8,128)(2,1)} %get-tuple-element.29) | data formatting | bytes 7077888 | tf_op jit(solution)/shard_map/convert_element_type | solution.py:160
  61.3 4.1 multiply_reduce_fusion.1
  66.0 3.0 fusion.34
  73.3 1.4 broadcast_multiply_fusion.5
  74.6 1.9 fusion.107
  77.1 1.6 slice.83
  78.8 1.8 slice.80
  80.5 2.2 reshape.220
  85.2 1.4 copy.44
  86.6 5.0 %gather_fusion = f32[768,2,256]{2,1,0:T(2,128)} fusion(f32[2,320,256]{2,0,1:T(2,128)} %copy.44, s32[1024]{0:T(1024)} %pad_clamp_fusion), kind=kCustom, calls=%fused_computation | custom fusion | bytes 3148800 | tf_op jit(solution)/shard_map/gather | solution.py:121
  91.6 3.6 copy.45
  95.2 1.5 fusion.102
  96.8 2.1 fusion.44
  98.9 8.1 %fusion.104 = (f32[2,6,4,32]{3,2,1,0:T(4,128)S(1)}, f32[2,6,4,32,128]{4,3,2,1,0:T(8,128)S(1)}) fusion(f32[2,6,4,32,128]{4,3,2,1,0:T(8,128)S(1)} %fusion.44), kind=kOutput, calls=%fused_computation.145 | output fusion | flops 393343 | bytes 1579008 | tf_op jit(solution)/shard_map/sub | solution.py:56
  107.0 1.7 convolution_bitcast_fusion
  108.7 2.3 copy.47
  111.0 2.2 reshape.222
  113.2 1.5 convolution_maximum_fusion
  116.2 2.9 fusion.35
  123.1 3.0 copy.53
  126.1 214.0 %all-gather.3.cloned.1.call-done = f32[2,1536,1536]{2,1,0:T(8,128)} async-done(((f32[2,24,1536]{2,1,0:T(8,128)}), f32[2,1536,1536]{2,1,0:T(8,128)}) %all-gather.3.cloned.1.call-update) | async-done | bytes 18874384 | tf_op jit(solution)/shard_map/all_gather | solution.py:150
  340.2 13.3 %fusion.101 = (f32[2,1536,768]{2,1,0:T(8,128)}, f32[2,1536,768]{2,1,0:T(8,128)}) fusion(f32[2,1536,1536]{2,1,0:T(8,128)} %all-gather.3.cloned.1.call-done), kind=kLoop, calls=%fused_computation.142 | loop fusion | bytes 37748736 | tf_op jit(solution)/shard_map/slice | solution.py:169
  353.5 9.6 %copy.49 = f32[2,1536,768]{1,2,0:T(8,128)} copy(f32[2,1536,768]{2,1,0:T(8,128)} %get-tuple-element.48) | data formatting | bytes 18874368 | tf_op jit(solution)/shard_map/slice | solution.py:169
  363.1 9.6 %copy.48 = f32[2,1536,768]{1,2,0:T(8,128)} copy(f32[2,1536,768]{2,1,0:T(8,128)} %get-tuple-element.49) | data formatting | bytes 18874368 | tf_op jit(solution)/shard_map/slice | solution.py:170
  372.7 7.8 %fusion.55 = f32[2,16,24,1536]{3,2,1,0:T(8,128)S(1)} fusion(f32[2,1536,16,48]{1,3,2,0:T(8,128)} %bitcast.136, f32[2,24,16,48]{3,2,1,0:T(8,128)S(1)} %reshape.224), kind=kOutput, calls=%fused_computation.66 | convolution fusion | flops 679477248 | bytes 14303232 | tf_op jit(solution)/shard_map/nihd,njhd->nhij/dot_general | solution.py:171
  380.5 3.7 fusion.106
  384.3 3.9 fusion.59
  388.2 5.9 %fusion.31 = f32[16,24,1536]{2,1,0:T(8,128)} fusion(f32[2,16,1536,24]{2,3,1,0:T(8,128)S(1)} %fusion.59, f32[2,16,24,1536]{3,2,1,0:T(8,128)S(1)} %get-tuple-element.69, f32[2,16,24]{2,1,0:T(8,128)S(1)} %get-tuple-element.68), kind=kOutput, calls=%fused_computation.31 | output fusion | flops 6490367 | bytes 11799552 | tf_op jit(solution)/shard_map/sub | solution.py:184
  394.2 10.0 %fusion.48 = bf16[2,24,16,48]{3,1,2,0:T(8,128)(2,1)S(1)} fusion(f32[2,1536,16,48]{1,3,2,0:T(8,128)} %bitcast.132, f32[2,16,24,1536]{3,2,1,0:T(8,128)} %copy-done.2, f32[2,16,24]{2,1,0:T(8,128)S(1)} %get-tuple-element.68), kind=kOutput, calls=%fused_computation.58 | convolution fusion | flops 681873408 | bytes 14232576 | tf_op jit(solution)/shard_map/nhij,njhd->nihd/dot_general | solution.py:177
  405.0 19.7 %reduce-scatter.2.cloned.1.call-done = f32[16,24,384]{2,1,0:T(8,128)} async-done(((f32[16,24,1536]{2,1,0:T(8,128)}), f32[16,24,384]{2,1,0:T(8,128)}) %reduce-scatter.2.cloned.1.call-update) | async-done | bytes 589840 | tf_op jit(solution)/shard_map/reduce_scatter | solution.py:185
  424.7 5.5 %fusion.100 = (f32[24,384]{1,0:T(8,128)S(1)}, f32[24,384]{1,0:T(8,128)S(1)}, f32[24,384,128]{1,2,0:T(8,128)S(1)}) fusion(f32[24,384]{1,0:T(8,128)S(1)} %copy-done.10, f32[24,384]{1,0:T(8,128)S(1)} %copy-done.7, f32[3,8,384,128]{2,3,1,0:T(8,128)} %copy.51, bf16[128,16]{0,1:T(8,128)(2,1)S(1)} %copy-done.12, f32[16,24,384]{2,1,0:T(8,128)} %reduce-scatter.2.cloned.1.call-done), kind=kOutput, calls=%fused_computation.141 | convolution fusion | flops 232372224 | bytes 10178560 | tf_op jit(solution)/shard_map/hij,ch->ijc/dot_general | solution.py:186
  430.2 5.6 %multiply_convert_fusion = bf16[24,384,128]{1,2,0:T(8,128)(2,1)} fusion(f32[24,384,128]{1,2,0:T(8,128)S(1)} %get-tuple-element.70, f32[3,8,384,128]{2,3,1,0:T(8,128)} %copy.51, f32[24,384]{1,0:T(8,128)S(1)} %get-tuple-element.71, f32[24,384]{1,0:T(8,128)S(1)} %get-tuple-element.72, f32[24,384]{1,0:T(8,128)S(1)} %copy-done.11, f32[24,384]{1,0:T(8,128)S(1)} %copy-done.8), kind=kLoop, calls=%fused_computation.34 | loop fusion | flops 8257536 | bytes 11943936 | tf_op jit(solution)/shard_map/convert_element_type | solution.py:194
  435.8 4.3 copy.57
  (94 shorter events, 23.8 us)
Async XLA Ops:
  7.2 109.0 %copy-start = (bf16[768,2304]{1,0:T(8,128)(2,1)S(1)}, bf16[768,2304]{1,0:T(8,128)(2,1)}, u32[]{:S(2)}) copy-start(bf16[768,2304]{1,0:T(8,128)(2,1)} %param.33) | copy-start | bytes 10616836
  7.2 115.9 %all-gather.5.cloned.1.call-start = ((), (), s32[]{:S(2)}) async-start(), calls=%async_computation.2 | async-start | bytes 2949120 | tf_op jit(solution)/shard_map/all_gather | solution.py:166
  9.3 5.3 %copy-start.13 = (f32[128]{0:T(128)}, f32[128]{0:T(128)S(1)}, u32[]{:S(2)}) copy-start(f32[128]{0:T(128)S(1)} %get-tuple-element.59) | copy-start | bytes 1540
  9.3 9.9 %copy-start.14 = (f32[128]{0:T(128)}, f32[128]{0:T(128)S(1)}, u32[]{:S(2)}) copy-start(f32[128]{0:T(128)S(1)} %get-tuple-element.60) | copy-start | bytes 1540
  9.3 9.9 %copy-start.15 = (f32[128]{0:T(128)}, f32[128]{0:T(128)S(1)}, u32[]{:S(2)}) copy-start(f32[128]{0:T(128)S(1)} %get-tuple-element.61) | copy-start | bytes 1540
  10.9 3.7 copy-start.4
  13.1 0.8 copy-start.3
  14.6 69.5 %collective-permute-start = (f32[2,64,256]{2,1,0:T(8,128)}, f32[2,64,256]{2,1,0:T(8,128)}, u32[]{:S(2)}, u32[]{:S(2)}) collective-permute-start(f32[2,64,256]{2,1,0:T(8,128)} %get-tuple-element.52), channel_id=1, source_target_pairs={{0,4},{4,8},{8,12},{12,16},{16,20},{20,24},{24,28},{28,32},{32,36}... | collective-permute-start | bytes 393224 | tf_op jit(solution)/shard_map/ppermute | solution.py:28
  19.2 64.9 %collective-permute-start.1 = (f32[2,64,256]{2,1,0:T(8,128)}, f32[2,64,256]{2,1,0:T(8,128)}, u32[]{:S(2)}, u32[]{:S(2)}) collective-permute-start(f32[2,64,256]{2,1,0:T(8,128)} %get-tuple-element.53), channel_id=1, source_target_pairs={{4,0},{8,4},{12,8},{16,12},{20,16},{24,20},{28,24},{32,28},{36,32}... | collective-permute-start | bytes 393224 | tf_op jit(solution)/shard_map/ppermute | solution.py:31
  24.0 3.6 copy-start.16
  34.8 3.6 copy-start.16
  45.6 3.6 copy-start.16
  61.3 7.8 %copy-start.6 = (f32[24,384]{1,0:T(8,128)}, f32[24,384]{1,0:T(8,128)S(1)}, u32[]{:S(2)}) copy-start(f32[24,384]{1,0:T(8,128)S(1)} %get-tuple-element.54) | copy-start | bytes 110596
  61.3 7.8 %copy-start.12 = (bf16[128,16]{0,1:T(8,128)(2,1)S(1)}, bf16[128,16]{0,1:T(8,128)(2,1)}, u32[]{:S(2)}) copy-start(bf16[128,16]{0,1:T(8,128)(2,1)} %param.28) | copy-start | bytes 12292
  65.4 0.6 copy-start.9
  70.4 269.8 %all-gather.3.cloned.1.call-start = ((), (), s32[]{:S(2)}) async-start(), calls=%async_computation.1 | async-start | bytes 19169280 | tf_op jit(solution)/shard_map/all_gather | solution.py:150
  119.1 0.8 copy-start.5
  120.6 304.1 %reduce-scatter.2.cloned.1.call-start = ((), (), s32[]{:S(2)}) async-start(), calls=%async_computation.3 | async-start | bytes 2949120 | tf_op jit(solution)/shard_map/reduce_scatter | solution.py:185
  372.7 11.5 %slice-start = ((s8[9437184]{0:T(1024)(128)(4,1)}), s8[4194304]{0:T(1024)(128)(4,1)S(1)}, s32[]{:S(2)}) async-start(s8[9437184]{0:T(1024)(128)(4,1)} %bitcast.133), calls=%async_computation.4 | async-start | bytes 8388608
  372.7 11.5 %slice-start.1 = ((s8[9437184]{0:T(1024)(128)(4,1)}), s8[4194304]{0:T(1024)(128)(4,1)S(1)}, s32[]{:S(2)}) async-start(s8[9437184]{0:T(1024)(128)(4,1)} %bitcast.133), calls=%async_computation.5 | async-start | bytes 8388608
  380.5 3.7 slice-start.2
  384.2 4.0 copy-start.2
  394.2 30.6 %copy-start.7 = (f32[24,384]{1,0:T(8,128)S(1)}, f32[24,384]{1,0:T(8,128)}, u32[]{:S(2)}) copy-start(f32[24,384]{1,0:T(8,128)} %copy-done.6) | copy-start | bytes 110596
  394.2 30.5 %copy-start.10 = (f32[24,384]{1,0:T(8,128)S(1)}, f32[24,384]{1,0:T(8,128)}, u32[]{:S(2)}) copy-start(f32[24,384]{1,0:T(8,128)} %copy-done.9) | copy-start | bytes 110596
  424.7 5.5 %copy-start.8 = (f32[24,384]{1,0:T(8,128)S(1)}, f32[24,384]{1,0:T(8,128)}, u32[]{:S(2)}) copy-start(f32[24,384]{1,0:T(8,128)} %copy-done.6) | copy-start | bytes 110596
  424.7 5.5 %copy-start.11 = (f32[24,384]{1,0:T(8,128)S(1)}, f32[24,384]{1,0:T(8,128)}, u32[]{:S(2)}) copy-start(f32[24,384]{1,0:T(8,128)} %copy-done.9) | copy-start | bytes 110596
  430.2 9.9 %copy-start.1 = (bf16[768,2304]{1,0:T(8,128)(2,1)S(1)}, bf16[768,2304]{1,0:T(8,128)(2,1)}, u32[]{:S(2)}) copy-start(bf16[768,2304]{1,0:T(8,128)(2,1)} %param.33) | copy-start | bytes 10616836
Sparse Core Ops, SparseCore 0:
  70.5 39.6 all-gather.4
  120.7 219.4 all-gather.2
  394.3 30.3 reduce-scatter.1
where the time goes:
time: 449 us; the launch traced here: 447 us
  waiting for transfers between devices  234 us (52%)
  local copies, waits for them, and re-layouts  73.6 us (16%)
  matrix products  63.1 us (14%)
  other arithmetic  55.5 us (12%)
  between operations  14.1 us (3%)
  starting transfers between devices  6.39 us (1%)
    all_gather x1, waiting for transfers between devices, on_device(): lax.all_gather(token_proj[..., width:], 'tile', axis=1, tiled=True)  214 us
    slice x2, local copies, waits for them, and re-layouts, on_device(): key_values[..., :width].reshape(copies, all_tokens, heads, head_size)  22.9 us
    reduce_scatter x1, waiting for transfers between devices, on_device(): lax.psum_scatter(partial_grad, 'copy', scatter_dimension=2, tiled=True)  19.7 us
    sub x2, other arithmetic, soft_weights(): spread = jnp.exp(scores - highest)  11.8 us
    dot_general x3, matrix products, condition_pair(): jnp.einsum('ijf,fc->ijc', hidden, trans_out, preferred_element_type=jnp.f...  11.2 us
    reduce_sum x6, other arithmetic, norm_parts(): spread = jnp.mean(centred * centred, axis=-1, keepdims=True)  10.8 us
    dot_general x3, matrix products, condition_pair(): jnp.einsum('ijc,cf->ijf', normal.astype(jnp.bfloat16), trans_in, preferre...  10.7 us
    dot_general x1, matrix products, on_device(): jnp.einsum('nhij,njhd->nihd', soft_probs.astype(jnp.float32), value_heads...  9.96 us
  transfers between devices with their start and end apart: 5, of which 2 were waited for; matrix products, arithmetic and copies ran while one was open for 26% of the time, Pallas kernels for 0%

commit v1 on v0

v1 whole, which is shorter than its diff:
```python
import math

import jax
import jax.numpy as jnp
from jax import lax
from jax.experimental import pallas as pl
from jax.experimental.pallas import tpu as pltpu
from jax.sharding import Mesh, PartitionSpec as P

A_HEAD = 32
A_HEADS = 4
Q_BLOCK = 32
K_WIN = 128
LEVELS = 200
HEAD = 48
H = 16

epsilon = 1e-05
sigma_data = 16.0
sigma_top = 160.0
sigma_low = 0.0004
rho_power = 7.0
excluded = -1e30
TILE = ("z", "g")
COPY = ("ylo", "core")
PLANE = ("g", "ylo")
BF = jnp.bfloat16
F32 = jnp.float32
NT = (((1,), (1,)), ((), ()))
NN = (((1,), (0,)), ((), ()))
TN = (((0,), (0,)), ((), ()))


def norm_parts(value):
    average = jnp.mean(value, axis=-1, keepdims=True)
    centred = value - average
    spread = jnp.mean(centred * centred, axis=-1, keepdims=True)
    scale = lax.rsqrt(spread + epsilon)
    return (centred * scale, scale)


def noise_scales(levels):
    fraction = levels.astype(F32) / LEVELS
    highest = sigma_top ** (1.0 / rho_power)
    lowest = sigma_low ** (1.0 / rho_power)
    sigma = sigma_data * (highest + fraction * (lowest - highest)) ** rho_power
    input_scale = lax.rsqrt(sigma * sigma + sigma_data * sigma_data)
    noise_code = 0.25 * jnp.log(sigma / sigma_data)
    return (input_scale, noise_code)


def dot(a, b, dims=NN):
    return lax.dot_general(a, b, dims, preferred_element_type=F32)


def two_parts(value):
    high = value.astype(BF)
    low = (value - high.astype(F32)).astype(BF)
    return high, low


def three_parts(value):
    high = value.astype(BF)
    rest = value - high.astype(F32)
    middle = rest.astype(BF)
    low = (rest - middle.astype(F32)).astype(BF)
    return high, middle, low


def atom_kernel(
    place, offsets, noise, low, high, normed, atoms, atom_weight, agg_weight, local_token,
    single, single_weight, noise_weight, token_weight, cotangent, out
):
    tile = place[0]
    copies, rows, width = normed.shape
    blocks = rows // Q_BLOCK
    span = K_WIN + Q_BLOCK
    rim = K_WIN // 2
    total = 64 * rows
    tok_rows = single.shape[0]
    head_of = lax.broadcasted_iota(jnp.int32, (Q_BLOCK, width), 1) // A_HEAD
    reach = lax.broadcasted_iota(jnp.int32, (1, span), 1)
    member = (
        lax.broadcasted_iota(jnp.int32, (tok_rows, rows), 0) == local_token[...]
    ).astype(F32)
    counts = jnp.sum(member, axis=1, keepdims=True)
    member = member.astype(BF)
    single_term = dot(single[...], single_weight[...])
    token_in = []
    for n in range(copies):
        ext = jnp.concatenate([low[n], normed[n], high[n]], axis=0)
        proj = dot(ext, atom_weight[...])
        queries = proj[rim : rim + rows, :width] * (1.0 / math.sqrt(A_HEAD))
        key_high, key_low = two_parts(proj[:, width : 2 * width])
        val_high, val_low = two_parts(proj[:, 2 * width :])
        keys = jnp.concatenate([key_high, key_low], axis=1)
        vals = jnp.concatenate([val_high, val_low], axis=1)
        parts = []
        for b in range(blocks):
            first = b * Q_BLOCK
            block = queries[first : first + Q_BLOCK]
            spread = jnp.concatenate(
                [jnp.where(head_of == h, block, 0.0) for h in range(A_HEADS)], axis=0
            )
            q_high, q_low = two_parts(spread)
            scores = dot(
                jnp.concatenate([q_high, q_high], axis=1), keys[first : first + span], NT
            ) + dot(q_low, key_high[first : first + span], NT)
            offset = offsets[b]
            position = tile * rows + first - rim + reach
            inside = (
                (reach >= offset)
                & (reach < offset + K_WIN)
                & (position >= 0)
                & (position < total)
            )
            scores = jnp.where(inside, scores, excluded)
            top = jnp.max(scores, axis=-1, keepdims=True)
            weights = jnp.exp(scores - top)
            weights = weights / jnp.sum(weights, axis=-1, keepdims=True)
            mixed = dot(weights.astype(BF), vals[first : first + span])
            mixed = mixed[:, :width] + mixed[:, width:]
            gathered = jnp.where(head_of == 0, mixed[:Q_BLOCK], 0.0)
            for h in range(1, A_HEADS):
                gathered += jnp.where(
                    head_of == h, mixed[h * Q_BLOCK : (h + 1) * Q_BLOCK], 0.0
                )
            parts.append(gathered)
        atom_out = (atoms[n] + jnp.concatenate(parts, axis=0)).astype(BF)
        hidden = jnp.maximum(dot(atom_out, agg_weight[...]), 0.0)
        sums = 0.0
        for part in three_parts(hidden):
            sums = sums + dot(member, part)
        token_normal, _ = norm_parts(sums / counts)
        token_in.append(token_normal + single_term + noise[n] * noise_weight[...])
    token_in = jnp.concatenate(token_in, axis=0)
    count = token_in.shape[0]
    stacked = jnp.concatenate(three_parts(token_in), axis=0)
    proj = dot(stacked, token_weight[...])
    proj = proj[:count] + proj[count : 2 * count] + proj[2 * count :]
    wide = H * HEAD
    cot = jnp.concatenate([cotangent[n].astype(F32) for n in range(copies)], axis=0)
    blank = jnp.zeros((count, 128 - 2 * HEAD), F32)
    for h in range(H):
        at = h * HEAD
        out[h, :, :128] = jnp.concatenate(
            [proj[:, at : at + HEAD] * (1.0 / math.sqrt(HEAD)), cot[:, at : at + HEAD], blank], axis=1
        )
        out[h, :, 128:] = jnp.concatenate(
            [
                proj[:, wide + at : wide + at + HEAD],
                proj[:, 2 * wide + at : 2 * wide + at + HEAD],
                blank,
            ],
            axis=1,
        )


def pair_kernel(pair, trans_in, trans_out, bias_weight_t, cond_out, bias_out):
    inner = trans_out.shape[0]
    for i in range(pair.shape[0]):
        row = pair[i].astype(F32)
        normal, _ = norm_parts(row)
        gate_up = dot(normal.astype(BF), trans_in[...])
        gate = gate_up[:, :inner]
        half = 0.5 * gate
        hidden = ((half + half * jnp.tanh(half)) * gate_up[:, inner:]).astype(BF)
        cond = (row + dot(hidden, trans_out[...])).astype(BF)
        cond_out[i] = cond
        normal, _ = norm_parts(cond.astype(F32))
        bias_out[:, i, :] = dot(bias_weight_t[...], normal.astype(BF), NT)


def attend_kernel(place, queries, kv, bias_mine, bias_other, update, grad_mine, grad_other):
    core = place[0]
    blocks = [core, 2 + core, 1 - core, 3 - core]
    rows = 192
    cols = 384
    tok = 24
    lane = lax.broadcasted_iota(jnp.int32, (1, 128), 1)
    is_key = lane < HEAD
    is_value = (lane >= HEAD) & (lane < 2 * HEAD)
    bias = jnp.concatenate(
        [
            jnp.concatenate(
                [
                    (bias_mine if c < 2 else bias_other)[2 * g + c % 2]
                    for c in range(4)
                ],
                axis=1,
            )
            for g in range(8)
        ],
        axis=0,
    )
    grad = None
    for y in range(2):
        for p in range(2):
            query = jnp.concatenate(
                [queries[2 * g + y, p * tok : (p + 1) * tok, :128] for g in range(8)], axis=0
            )
            q_high, q_low = two_parts(jnp.where(is_key, query, 0.0))
            cot = jnp.where(is_value, query, 0.0).astype(BF)
            tokens = []
            for c in blocks:
                for z in range(2):
                    for g in range(8):
                        tokens.append(kv[2 * c + z, 2 * g + y, p * tok : (p + 1) * tok, :])
            high, low = two_parts(jnp.concatenate(tokens, axis=0))
            both = jnp.concatenate([high, low], axis=1)
            scores = (
                dot(jnp.concatenate([q_high, q_high], axis=1), both, NT)
                + dot(q_low, high, NT)
                + bias
            )
            top = jnp.max(scores, axis=-1, keepdims=True)
            weights = jnp.exp(scores - top)
            weights = weights * (1.0 / jnp.sum(weights, axis=-1, keepdims=True))
            mixed = dot(weights.astype(BF), both)
            mixed = mixed[:, :128] + mixed[:, 128:]
            for g in range(8):
                update[2 * g + y, p * tok : (p + 1) * tok, :] = mixed[g * tok : (g + 1) * tok]
            term = weights * dot(jnp.concatenate([cot, cot], axis=1), both, NT)
            term = term - weights * jnp.sum(term, axis=-1, keepdims=True)
            grad = term if grad is None else grad + term
    for g in range(8):
        for c in range(4):
            (grad_mine if c < 2 else grad_other)[2 * g + c % 2] = grad[
                g * tok : (g + 1) * tok, c * cols : (c + 1) * cols
            ]


def grad_kernel(grad, cond, weight_parts, out):
    for i in range(cond.shape[0]):
        high, middle, low = three_parts(grad[:, i, :])
        stacked = jnp.concatenate([high, middle, low, high, middle], axis=0)
        grad_normal = dot(stacked, weight_parts[...], TN)
        normal, scale = norm_parts(cond[i].astype(F32))
        shared = jnp.mean(grad_normal * normal, axis=-1, keepdims=True)
        out[i] = ((grad_normal - normal * shared) * scale).astype(BF)


def params(**more):
    return pltpu.CompilerParams(vmem_limit_bytes=56 * 1024 * 1024, **more)


VMEM = pl.BlockSpec(memory_space=pltpu.VMEM)
SMEM = pl.BlockSpec(memory_space=pltpu.SMEM)


def on_device(
    pair_rep,
    single,
    atom_feat,
    coords,
    levels,
    window_offset,
    atom_token,
    trans_in,
    trans_out,
    bias_weight,
    single_weight,
    coord_weight,
    atom_weight,
    agg_weight,
    token_weight,
    noise_weight,
    cotangent,
):
    tile_index = lax.axis_index(TILE).astype(jnp.int32)
    core_index = lax.axis_index("core").astype(jnp.int32)
    copies, tok_rows, width = cotangent.shape
    atom_rows, atom_width = atom_feat.shape
    cols = pair_rep.shape[1]
    rim = K_WIN // 2
    input_scale, noise_code = noise_scales(levels)
    scaled = coords * input_scale[:, None, None]
    atoms = atom_feat.astype(F32)[None]
    for axis_index in range(3):
        atoms = atoms + scaled[:, axis_index, :, None] * coord_weight[axis_index][None, None, :]
    atom_normal, _ = norm_parts(atoms)
    normed = atom_normal.astype(BF)
    forward = [(i, i + 1) for i in range(63)]
    backward = [(i + 1, i) for i in range(63)]
    low = lax.ppermute(normed[:, atom_rows - rim :], TILE, forward)
    high = lax.ppermute(normed[:, :rim], TILE, backward)
    local_token = (atom_token - tile_index * tok_rows)[None, :]
    packed = pl.pallas_call(
        atom_kernel,
        out_shape=jax.ShapeDtypeStruct((H, copies * tok_rows, 256), F32),
        in_specs=[SMEM] * 3 + [VMEM] * 12,
        out_specs=VMEM,
        compiler_params=params(),
        cost_estimate=pl.CostEstimate(flops=3_000_000_000, bytes_accessed=6_000_000, transcendentals=0),
        name="atom_stage",
    )(
        tile_index[None], window_offset, noise_code, low, high, normed, atoms, atom_weight, agg_weight,
        local_token, single, single_weight, noise_weight[None, :], token_weight, cotangent,
    )
    packed = lax.all_to_all(packed, PLANE, 0, 0, tiled=True)
    kv = lax.all_gather(packed[:, :, 128:], "z", axis=0)

    step = 8
    bias_t = bias_weight.T
    cond, bias = pl.pallas_call(
        pair_kernel,
        grid=(tok_rows // step,),
        out_shape=(
            jax.ShapeDtypeStruct(pair_rep.shape, BF),
            jax.ShapeDtypeStruct((H, tok_rows, cols), F32),
        ),
        in_specs=[
            pl.BlockSpec((step, cols, 128), lambda i: (i, 0, 0)),
            pl.BlockSpec(trans_in.shape, lambda i: (0, 0)),
            pl.BlockSpec(trans_out.shape, lambda i: (0, 0)),
            pl.BlockSpec(bias_t.shape, lambda i: (0, 0)),
        ],
        out_specs=(
            pl.BlockSpec((step, cols, 128), lambda i: (i, 0, 0)),
            pl.BlockSpec((H, step, cols), lambda i: (0, i, 0)),
        ),
        compiler_params=params(),
        cost_estimate=pl.CostEstimate(flops=4_000_000_000, bytes_accessed=6_000_000, transcendentals=5_000_000),
        name="pair_transition",
    )(pair_rep, trans_in, trans_out, bias_t)
    bias_mine = lax.all_to_all(bias, PLANE, 0, 0, tiled=True)
    swap = [(0, 1), (1, 0)]
    bias_other = lax.ppermute(bias_mine, "core", swap)

    update, grad_mine, grad_other = pl.pallas_call(
        attend_kernel,
        out_shape=(
            jax.ShapeDtypeStruct((H, copies * tok_rows, 128), F32),
            jax.ShapeDtypeStruct((H, tok_rows, cols), F32),
            jax.ShapeDtypeStruct((H, tok_rows, cols), F32),
        ),
        in_specs=[SMEM] + [VMEM] * 4,
        out_specs=(VMEM, VMEM, VMEM),
        compiler_params=params(),
        cost_estimate=pl.CostEstimate(flops=4_000_000_000, bytes_accessed=8_000_000, transcendentals=1_200_000),
        name="token_attention",
    )(core_index[None], packed, kv, bias_mine, bias_other)
    grad = grad_mine + lax.ppermute(grad_other, "core", swap)
    grad = lax.all_to_all(grad, PLANE, 0, 0, tiled=True)
    update = update[:, :, HEAD : 2 * HEAD].astype(BF)
    update = lax.all_to_all(update, PLANE, 0, 0, tiled=True)
    update = update.reshape(H, copies, tok_rows, HEAD).transpose(1, 2, 0, 3)
    update = update.reshape(copies, tok_rows, width)

    weight = bias_weight.astype(F32)
    weight = (weight - jnp.mean(weight, axis=0, keepdims=True)).T
    w_high, w_low = two_parts(weight)
    weight_parts = jnp.concatenate([w_high, w_high, w_high, w_low, w_low], axis=0)
    gradient = pl.pallas_call(
        grad_kernel,
        grid=(tok_rows // step,),
        out_shape=jax.ShapeDtypeStruct(pair_rep.shape, BF),
        in_specs=[
            pl.BlockSpec((H, step, cols), lambda i: (0, i, 0)),
            pl.BlockSpec((step, cols, 128), lambda i: (i, 0, 0)),
            pl.BlockSpec(weight_parts.shape, lambda i: (0, 0)),
        ],
        out_specs=pl.BlockSpec((step, cols, 128), lambda i: (i, 0, 0)),
        compiler_params=params(),
        cost_estimate=pl.CostEstimate(flops=400_000_000, bytes_accessed=6_000_000, transcendentals=0),
        name="pair_gradient",
    )(grad, cond, weight_parts)
    return (update, gradient)


def solution(mesh):
    fine = Mesh(mesh.devices.reshape(8, 8, 2, 2), ("z", "g", "ylo", "core"))
    placed = (
        P(TILE, COPY, None),
        P(TILE, None),
        P(TILE, None),
        P(COPY, None, TILE),
        P(COPY),
        P(TILE),
        P(TILE),
        P(),
        P(),
        P(),
        P(),
        P(),
        P(),
        P(),
        P(),
        P(),
        P(COPY, TILE, None),
    )
    return jax.shard_map(
        on_device,
        mesh=fine,
        in_specs=placed,
        out_specs=(P(COPY, TILE, None), P(TILE, COPY, None)),
        check_vma=False,
    )
```

time: 449 us -> 161 us (0.36)
  waiting for transfers between devices: 234 us -> 20.4 us
  local copies, waits for them, and re-layouts: 73.6 us -> 7.51 us
  matrix products: 63.1 us -> 0 us
  Pallas kernels: 0 us -> 52.8 us
  other arithmetic: 55.5 us -> 8.1 us
  blocking collectives: 0 us -> 36.4 us
  starting transfers between devices: 6.39 us -> 21.1 us
    all_gather x2 -> x1, waiting for transfers between devices: 214 us -> 4.43 us  [on_device(): kv = lax.all_gather(packed[:, :, 128:], 'z', axis=0)]
    dot_general x18 -> x0, matrix products: 63.1 us -> none  [the longest x3 11.2 us: condition_pair(): jnp.einsum('ijf,fc->ijc', hidden, trans_out, preferred_element_type=jnp.f...]
    pallas_call x0 -> x4, Pallas kernels: none -> 52.8 us  [the longest x1 23.3 us: on_device(): pl.pallas_call(pair_kernel, grid=(tok_rows // step,), out_shape=(jax.Shap...]
    slice x9 -> x3, local copies, waits for them, and re-layouts: 39.8 us -> 1.94 us  [the longest x1 1.11 us: on_device(): update = update[:, :, HEAD:2 * HEAD].astype(BF)]
    all_to_all x0 -> x2, blocking collectives: none -> 36.4 us  [the longest x1 23.5 us: on_device(): packed = lax.all_to_all(packed, PLANE, 0, 0, tiled=True)]
    reduce_scatter x1 -> x0, waiting for transfers between devices: 19.7 us -> none  [on_device(): lax.psum_scatter(partial_grad, 'copy', scatter_dimension=2, tiled=True)]
    sub x4 -> x1, other arithmetic: 19 us -> 1.22 us  [on_device(): local_token = (atom_token - tile_index * tok_rows)[None, :]]
    all_to_all x0 -> x2, waiting for transfers between devices: none -> 13.6 us  [the longest x1 9.1 us: on_device(): grad = lax.all_to_all(grad, PLANE, 0, 0, tiled=True)]
  transfers between devices with their start and end apart: 5 -> 7, of which waited for: 2 -> 5; matrix products, arithmetic and copies ran while one was open for 26% -> 5% of each run, Pallas kernels for 0% -> 15%
where the time goes in v1:
time: 161 us; the launch traced here: 160 us
  Pallas kernels  52.8 us (33%)
  blocking collectives  36.4 us (23%)
  starting transfers between devices  21.1 us (13%)
  waiting for transfers between devices  20.4 us (13%)
  between operations  14.1 us (9%)
  other arithmetic  8.1 us (5%)
  local copies, waits for them, and re-layouts  7.51 us (5%)
    all_to_all x1, blocking collectives, on_device(): packed = lax.all_to_all(packed, PLANE, 0, 0, tiled=True)  23.5 us
    pallas_call x1, Pallas kernels, on_device(): pl.pallas_call(pair_kernel, grid=(tok_rows // step,), out_shape=(jax.Shap...  23.3 us
    all_to_all x1, blocking collectives, on_device(): bias_mine = lax.all_to_all(bias, PLANE, 0, 0, tiled=True)  12.9 us
    pallas_call x1, Pallas kernels, on_device(): pl.pallas_call(grad_kernel, grid=(tok_rows // step,), out_shape=jax.Shape...  10.5 us
    pallas_call x1, Pallas kernels, on_device(): pl.pallas_call(atom_kernel, out_shape=jax.ShapeDtypeStruct((H, copies * t...  9.89 us
    all_to_all x1, waiting for transfers between devices, on_device(): grad = lax.all_to_all(grad, PLANE, 0, 0, tiled=True)  9.1 us
    pallas_call x1, Pallas kernels, on_device(): pl.pallas_call(attend_kernel, out_shape=(jax.ShapeDtypeStruct((H, copies...  9 us
    all_to_all x1, starting transfers between devices, on_device(): update = lax.all_to_all(update, PLANE, 0, 0, tiled=True)  6.51 us
  transfers between devices with their start and end apart: 7, of which 5 were waited for; matrix products, arithmetic and copies ran while one was open for 5% of the time, Pallas kernels for 15%

profile of v1, /device:TPU:1, one launch (start us, length us, event | category | flops | bytes accessed | tf_op | source)
XLA Modules:
  0.0 160.4 jit_solution(13361495476780381720)
XLA Ops:
  7.2 0.0 all-gather.3.cloned.1.call-start
  7.2 1.2 add_rsqrt_fusion.1
  8.4 0.8 broadcast_multiply_fusion
  9.2 0.8 slice_bitcast_fusion.5
  10.0 0.8 convert_element_type.23
  10.8 0.9 multiply_add_fusion
  11.7 0.4 multiply_reduce_fusion
  12.1 0.3 multiply_convert_fusion.normed
  12.5 3.9 %collective-permute-start = (bf16[2,64,128]{2,1,0:T(8,128)(2,1)S(1)}, bf16[2,64,128]{2,1,0:T(8,128)(2,1)S(1)}, u32[]{:S(2)}, u32[]{:S(2)}) collective-permute-start(bf16[2,64,128]{2,1,0:T(8,128)(2,1)S(1)} %get-tuple-element.15), channel_id=1, source_target_pairs={{0,4},{4,8},{8,12},{12,16},{16,20},{20,24},{24,28},{28,32},{32,36}... | collective-permute-start | bytes 98312 | tf_op jit(solution)/shard_map/ppermute | solution.py:285
  16.4 1.3 collective-permute-start.1
  17.7 1.2 broadcast_subtract_fusion
  19.0 1.3 broadcast_in_dim.20.noise_weight
  20.2 0.0 collective-permute-done.low
  20.2 0.9 collective-permute-done.1.high
  21.1 0.0 copy-done.3
  21.1 0.6 copy-done.8
  21.7 9.9 %atom_stage.1 = f32[16,48,256]{2,1,0:T(8,128)} custom-call(s32[1]{0:T(128)} %bitcast.1.place, s32[6]{0:T(128)} %offsets.1, f32[2]{0:T(128)} %get-tuple-element.23.noise, bf16[2,64,128]{2,1,0:T(8,128)(2,1)} %copy-done.7, bf16[2,64,128]{2,1,0:T(8,128)(2,1)} %copy-done.8, bf16[2,192,128]{2,1,0:T(8,128)(2,1)} %copy-done.3, ...), custom_call_target="tpu_custom_call" | custom-call | flops 3000000000 | bytes 6000000 | tf_op jit(solution)/shard_map/atom_stage/pallas_call | solution.py:288
  31.6 23.5 %all_to_all.20.queries = f32[16,48,256]{2,1,0:T(8,128)S(1)} all-to-all(f32[16,48,256]{2,1,0:T(8,128)} %atom_stage.1), channel_id=1, replica_groups=mesh['z'=8,'g'=8,'ylo'=2,'core'=2] {'g','ylo'}, dimensions={0} | all-to-all | bytes 1572864 | tf_op jit(solution)/shard_map/all_to_all | solution.py:300
  55.1 0.8 slice.46
  55.9 0.0 all-gather.3.cloned.1.call-update
  56.0 0.0 copy-start.4
  56.0 23.3 %pair_transition.1 = (bf16[24,384,128]{2,1,0:T(8,128)(2,1)}, f32[16,24,384]{2,1,0:T(8,128)}) custom-call(bf16[24,384,128]{2,1,0:T(8,128)(2,1)} %pair.1, bf16[128,1024]{1,0:T(8,128)(2,1)} %trans_in.1, bf16[512,128]{1,0:T(8,128)(2,1)} %trans_out.1, bf16[16,128]{1,0:T(8,128)(2,1)} %bitcast.45), custom_call_target="tpu_custom_call" | custom-call | flops 4000000000 | bytes 6000000 | tf_op jit(solution)/shard_map/pair_transition/pallas_call | solution.py:305
  79.3 12.9 %all_to_all.21.bias_mine = f32[16,24,384]{2,1,0:T(8,128)S(1)} all-to-all(f32[16,24,384]{2,1,0:T(8,128)} %get-tuple-element.7), channel_id=1, replica_groups=mesh['z'=8,'g'=8,'ylo'=2,'core'=2] {'g','ylo'}, dimensions={0} | all-to-all | bytes 1179648 | tf_op jit(solution)/shard_map/all_to_all | solution.py:326
  92.2 4.6 %collective-permute-start.2 = (f32[16,24,384]{2,1,0:T(8,128)S(1)}, f32[16,24,384]{2,1,0:T(8,128)S(1)}, u32[]{:S(2)}, u32[]{:S(2)}) collective-permute-start(f32[16,24,384]{2,1,0:T(8,128)S(1)} %all_to_all.21.bias_mine), channel_id=1, source_target_pairs={{0,1},{1,0},{2,3},{3,2},{4,5},{5,4},{6,7},{7,6},{8,9},{9,8},{10,11... | collective-permute-start | bytes 1769480 | tf_op jit(solution)/shard_map/ppermute | solution.py:328
  96.8 0.0 copy-done.4
  96.8 0.1 convert_reduce_fusion
  96.9 1.5 collective-permute-done.2.bias_other
  98.4 4.4 %all-gather.3.cloned.1.call-done = f32[128,48,128]{2,1,0:T(8,128)} async-done(((f32[16,48,128]{2,1,0:T(8,128)}), f32[128,48,128]{2,1,0:T(8,128)}) %all-gather.3.cloned.1.call-update) | async-done | bytes 3145744 | tf_op jit(solution)/shard_map/all_gather | solution.py:301
  102.9 9.0 %token_attention.1 = (f32[16,48,128]{2,1,0:T(8,128)}, f32[16,24,384]{2,1,0:T(8,128)}, f32[16,24,384]{2,1,0:T(8,128)}) custom-call(s32[1]{0:T(128)} %bitcast.place, f32[16,48,256]{2,1,0:T(8,128)} %copy-done.1, f32[8,16,48,128]{3,2,1,0:T(8,128)} %bitcast.47, f32[16,24,384]{2,1,0:T(8,128)} %copy-done.2, f32[16,24,384]{2,1,0:T(8,128)} %copy-done.6), custom_call_target="tpu_custom_call" | custom-call | flops 4000000000 | bytes 8000000 | tf_op jit(solution)/shard_map/token_attention/pallas_call | solution.py:330
  111.8 1.1 collective-permute-start.3
  113.0 0.1 constant_dynamic-update-slice_fusion.4
  113.1 1.1 slice.55
  114.2 0.9 reshape.37
  115.1 6.5 %all-to-all-start.2 = ((bf16[16,2,1152]{2,1,0:T(2,128)(2,1)}), bf16[16,2,1152]{2,1,0:T(2,128)(2,1)S(1)}, u32[]{:S(2)}, u32[]{:S(2)}) async-start(bf16[16,2,1152]{2,1,0:T(2,128)(2,1)} %reshape.37), calls=%async_computation.2 | async-start | bytes 147456 | tf_op jit(solution)/shard_map/all_to_all | solution.py:346
  121.6 0.1 constant_dynamic-update-slice_fusion.3
  121.7 0.0 collective-permute-done.3
  121.7 1.9 %add.46 = f32[16,24,384]{2,1,0:T(8,128)} add(f32[16,24,384]{2,1,0:T(8,128)} %get-tuple-element.9, f32[16,24,384]{2,1,0:T(8,128)S(1)} %collective-permute-done.3) | non-fusion elementwise | flops 147456 | bytes 1769472 | tf_op jit(solution)/shard_map/add | solution.py:343
  123.6 4.5 %all-to-all-done.2 = bf16[16,2,1152]{2,1,0:T(2,128)(2,1)S(1)} async-done(((bf16[16,2,1152]{2,1,0:T(2,128)(2,1)}), bf16[16,2,1152]{2,1,0:T(2,128)(2,1)S(1)}, u32[]{:S(2)}, u32[]{:S(2)}) %all-to-all-start.2) | async-done | bytes 73760 | tf_op jit(solution)/shard_map/all_to_all | solution.py:346
  128.1 3.6 %all-to-all-start.3 = ((f32[16,24,384]{2,1,0:T(8,128)}), f32[16,24,384]{2,1,0:T(8,128)S(1)}, u32[]{:S(2)}, u32[]{:S(2)}) async-start(f32[16,24,384]{2,1,0:T(8,128)} %add.46), calls=%async_computation.3 | async-start | bytes 1179648 | tf_op jit(solution)/shard_map/all_to_all | solution.py:344
  131.7 0.1 constant_dynamic-update-slice_fusion.2
  131.8 0.1 constant_dynamic-update-slice_fusion.1
  131.8 0.1 constant_dynamic-update-slice_fusion.weight_parts
  131.9 0.2 reshape.38
  132.1 0.1 copy.20
  132.2 0.8 reshape.35
  133.1 9.1 %all-to-all-done.3.grad = f32[16,24,384]{2,1,0:T(8,128)S(1)} async-done(((f32[16,24,384]{2,1,0:T(8,128)}), f32[16,24,384]{2,1,0:T(8,128)S(1)}, u32[]{:S(2)}, u32[]{:S(2)}) %all-to-all-start.3) | async-done | bytes 589856 | tf_op jit(solution)/shard_map/all_to_all | solution.py:344
  142.2 0.8 copy-done
  143.0 10.5 %pair_gradient.1 = bf16[24,384,128]{2,1,0:T(8,128)(2,1)} custom-call(f32[16,24,384]{2,1,0:T(8,128)} %copy-done, bf16[24,384,128]{2,1,0:T(8,128)(2,1)} %get-tuple-element.11.cond, bf16[80,128]{1,0:T(8,128)(2,1)} %copy-done.5), custom_call_target="tpu_custom_call" | custom-call | flops 400000000 | bytes 6000000 | tf_op jit(solution)/shard_map/pair_gradient/pallas_call | solution.py:354
  (18 shorter events, 0.1 us)
Async XLA Ops:
  7.2 95.7 %all-gather.3.cloned.1.call-start = ((), (), s32[]{:S(2)}) async-start(), calls=%async_computation.4 | async-start | bytes 3538944 | tf_op jit(solution)/shard_map/all_gather | solution.py:301
  12.5 8.6 %copy-start.3 = (bf16[2,192,128]{2,1,0:T(8,128)(2,1)}, bf16[2,192,128]{2,1,0:T(8,128)(2,1)S(1)}, u32[]{:S(2)}) copy-start(bf16[2,192,128]{2,1,0:T(8,128)(2,1)S(1)} %multiply_convert_fusion.normed) | copy-start | bytes 294916
  12.5 7.8 %collective-permute-start = (bf16[2,64,128]{2,1,0:T(8,128)(2,1)S(1)}, bf16[2,64,128]{2,1,0:T(8,128)(2,1)S(1)}, u32[]{:S(2)}, u32[]{:S(2)}) collective-permute-start(bf16[2,64,128]{2,1,0:T(8,128)(2,1)S(1)} %get-tuple-element.15), channel_id=1, source_target_pairs={{0,4},{4,8},{8,12},{12,16},{16,20},{20,24},{24,28},{28,32},{32,36}... | collective-permute-start | bytes 98312 | tf_op jit(solution)/shard_map/ppermute | solution.py:285
  16.4 4.7 %collective-permute-start.1 = (bf16[2,64,128]{2,1,0:T(8,128)(2,1)S(1)}, bf16[2,64,128]{2,1,0:T(8,128)(2,1)S(1)}, u32[]{:S(2)}, u32[]{:S(2)}) collective-permute-start(bf16[2,64,128]{2,1,0:T(8,128)(2,1)S(1)} %get-tuple-element.14), channel_id=1, source_target_pairs={{4,0},{8,4},{12,8},{16,12},{20,16},{24,20},{28,24},{32,28},{36,32}... | collective-permute-start | bytes 98312 | tf_op jit(solution)/shard_map/ppermute | solution.py:286
  20.2 0.9 copy-start.7
  21.1 0.6 copy-start.8
  55.1 24.2 %copy-start.1 = (f32[16,48,256]{2,1,0:T(8,128)}, f32[16,48,256]{2,1,0:T(8,128)S(1)}, u32[]{:S(2)}) copy-start(f32[16,48,256]{2,1,0:T(8,128)S(1)} %all_to_all.20.queries) | copy-start | bytes 2359300
  56.0 40.8 %copy-start.4 = (bf16[128,16]{0,1:T(8,128)(2,1)S(1)}, bf16[128,16]{0,1:T(8,128)(2,1)}, u32[]{:S(2)}) copy-start(bf16[128,16]{0,1:T(8,128)(2,1)} %param.26) | copy-start | bytes 12292
  92.2 10.7 %copy-start.2 = (f32[16,24,384]{2,1,0:T(8,128)}, f32[16,24,384]{2,1,0:T(8,128)S(1)}, u32[]{:S(2)}) copy-start(f32[16,24,384]{2,1,0:T(8,128)S(1)} %all_to_all.21.bias_mine) | copy-start | bytes 1769476
  92.2 6.2 %collective-permute-start.2 = (f32[16,24,384]{2,1,0:T(8,128)S(1)}, f32[16,24,384]{2,1,0:T(8,128)S(1)}, u32[]{:S(2)}, u32[]{:S(2)}) collective-permute-start(f32[16,24,384]{2,1,0:T(8,128)S(1)} %all_to_all.21.bias_mine), channel_id=1, source_target_pairs={{0,1},{1,0},{2,3},{3,2},{4,5},{5,4},{6,7},{7,6},{8,9},{9,8},{10,11... | collective-permute-start | bytes 1769480 | tf_op jit(solution)/shard_map/ppermute | solution.py:328
  98.4 4.4 %copy-start.6 = (f32[16,24,384]{2,1,0:T(8,128)}, f32[16,24,384]{2,1,0:T(8,128)S(1)}, u32[]{:S(2)}) copy-start(f32[16,24,384]{2,1,0:T(8,128)S(1)} %collective-permute-done.2.bias_other) | copy-start | bytes 1769476
  111.8 9.8 %collective-permute-start.3 = (f32[16,24,384]{2,1,0:T(8,128)}, f32[16,24,384]{2,1,0:T(8,128)S(1)}, u32[]{:S(2)}, u32[]{:S(2)}) collective-permute-start(f32[16,24,384]{2,1,0:T(8,128)} %get-tuple-element.10), channel_id=1, source_target_pairs={{0,1},{1,0},{2,3},{3,2},{4,5},{5,4},{6,7},{7,6},{8,9},{9,8},{10,11... | collective-permute-start | bytes 1769480 | tf_op jit(solution)/shard_map/ppermute | solution.py:343
  115.1 13.0 %all-to-all-start.2 = ((bf16[16,2,1152]{2,1,0:T(2,128)(2,1)}), bf16[16,2,1152]{2,1,0:T(2,128)(2,1)S(1)}, u32[]{:S(2)}, u32[]{:S(2)}) async-start(bf16[16,2,1152]{2,1,0:T(2,128)(2,1)} %reshape.37), calls=%async_computation.2 | async-start | bytes 147456 | tf_op jit(solution)/shard_map/all_to_all | solution.py:346
  128.1 14.1 %all-to-all-start.3 = ((f32[16,24,384]{2,1,0:T(8,128)}), f32[16,24,384]{2,1,0:T(8,128)S(1)}, u32[]{:S(2)}, u32[]{:S(2)}) async-start(f32[16,24,384]{2,1,0:T(8,128)} %add.46), calls=%async_computation.3 | async-start | bytes 1179648 | tf_op jit(solution)/shard_map/all_to_all | solution.py:344
  131.9 10.2 %copy-start.5 = (bf16[80,128]{1,0:T(8,128)(2,1)}, bf16[80,128]{1,0:T(8,128)(2,1)S(1)}, u32[]{:S(2)}) copy-start(bf16[80,128]{1,0:T(8,128)(2,1)S(1)} %constant_dynamic-update-slice_fusion.weight_parts) | copy-start | bytes 61444
  142.1 0.8 copy-start
Sparse Core Ops, SparseCore 0:
  56.1 46.7 all-gather.2

commit v2 on v1

v2 whole, which is shorter than its diff:
```python
import math

import jax
import jax.numpy as jnp
from jax import lax
from jax.experimental import pallas as pl
from jax.experimental.pallas import tpu as pltpu
from jax.sharding import Mesh, PartitionSpec as P

A_HEAD = 32
A_HEADS = 4
Q_BLOCK = 32
K_WIN = 128
LEVELS = 200
HEAD = 48
H = 16

epsilon = 1e-05
sigma_data = 16.0
sigma_top = 160.0
sigma_low = 0.0004
rho_power = 7.0
excluded = -1e30
TILE = ("z", "g")
COPY = ("ylo", "core")
PLANE = ("g", "ylo")
BF = jnp.bfloat16
F32 = jnp.float32
NT = (((1,), (1,)), ((), ()))
NN = (((1,), (0,)), ((), ()))
TN = (((0,), (0,)), ((), ()))


def norm_parts(value):
    average = jnp.mean(value, axis=-1, keepdims=True)
    centred = value - average
    spread = jnp.mean(centred * centred, axis=-1, keepdims=True)
    scale = lax.rsqrt(spread + epsilon)
    return (centred * scale, scale)


def noise_parts(level):
    fraction = jnp.full((1, 128), level, jnp.int32).astype(F32) / LEVELS
    highest = sigma_top ** (1.0 / rho_power)
    lowest = sigma_low ** (1.0 / rho_power)
    root = highest + fraction * (lowest - highest)
    square = root * root
    sigma = sigma_data * (square * square * square * root)
    input_scale = lax.rsqrt(sigma * sigma + sigma_data * sigma_data)
    noise_code = 0.25 * jnp.log(sigma / sigma_data)
    return (input_scale, noise_code)


def dot(a, b, dims=NN):
    return lax.dot_general(a, b, dims, preferred_element_type=F32)


def two_parts(value):
    high = value.astype(BF)
    low = (value - high.astype(F32)).astype(BF)
    return high, low


def three_parts(value):
    high = value.astype(BF)
    rest = value - high.astype(F32)
    middle = rest.astype(BF)
    low = (rest - middle.astype(F32)).astype(BF)
    return high, middle, low


def grid_scale(top):
    top = jnp.maximum(top, 1e-30)
    power = jnp.ceil(jnp.log2(top))
    steps = jnp.ceil(top * jnp.exp2(13.0 - power)) + 1.0
    return steps, power


def scale_value(steps, power):
    return steps * jnp.exp2(power - 13.0) * (1.0 / 32767.0)


def whole(value):
    return jnp.round(value).astype(jnp.int32)


def start_kernel(levels, feat, coords, coord_weight, atoms_out, normed_out, first_out, last_out):
    rows = feat.shape[0]
    rim = K_WIN // 2
    for n in range(coords.shape[0]):
        input_scale, _ = noise_parts(levels[n])
        scaled = coords[n] * input_scale[:, :1]
        atoms = feat[...].astype(F32) + lax.dot_general(
            scaled, coord_weight[...], TN, precision=lax.Precision.HIGHEST, preferred_element_type=F32
        )
        normal, _ = norm_parts(atoms)
        normal = normal.astype(BF)
        atoms_out[n] = atoms
        normed_out[n] = normal
        first_out[n] = normal[:rim]
        last_out[n] = normal[rows - rim :]


def atom_kernel(
    place, offsets, levels, low, high, normed, atoms, atom_weight, agg_weight, atom_token,
    single, single_weight, noise_weight, token_weight, cotangent, out
):
    tile = place[0]
    copies, rows, width = normed.shape
    blocks = rows // Q_BLOCK
    span = K_WIN + Q_BLOCK
    rim = K_WIN // 2
    total = 64 * rows
    tok_rows = single.shape[0]
    head_of = lax.broadcasted_iota(jnp.int32, (Q_BLOCK, width), 1) // A_HEAD
    reach = lax.broadcasted_iota(jnp.int32, (1, span), 1)
    local_token = atom_token[...].reshape(1, rows) - tile * tok_rows
    member = (lax.broadcasted_iota(jnp.int32, (tok_rows, rows), 0) == local_token).astype(F32)
    counts = jnp.sum(member, axis=1, keepdims=True)
    member = member.astype(BF)
    single_term = dot(single[...], single_weight[...])
    noise_row = noise_weight[...].reshape(1, noise_weight.shape[0])
    token_in = []
    for n in range(copies):
        ext = jnp.concatenate([low[n], normed[n], high[n]], axis=0)
        proj = dot(ext, atom_weight[...])
        queries = proj[rim : rim + rows, :width] * (1.0 / math.sqrt(A_HEAD))
        key_high, key_low = two_parts(proj[:, width : 2 * width])
        val_high, val_low = two_parts(proj[:, 2 * width :])
        keys = jnp.concatenate([key_high, key_low], axis=1)
        vals = jnp.concatenate([val_high, val_low], axis=1)
        parts = []
        for b in range(blocks):
            first = b * Q_BLOCK
            block = queries[first : first + Q_BLOCK]
            spread = jnp.concatenate(
                [jnp.where(head_of == h, block, 0.0) for h in range(A_HEADS)], axis=0
            )
            q_high, q_low = two_parts(spread)
            stacked = jnp.concatenate(
                [
                    jnp.concatenate([q_high, q_high], axis=1),
                    jnp.concatenate([q_low, jnp.zeros_like(q_low)], axis=1),
                ],
                axis=0,
            )
            scores = dot(stacked, keys[first : first + span], NT)
            scores = scores[: A_HEADS * Q_BLOCK] + scores[A_HEADS * Q_BLOCK :]
            offset = offsets[b]
            position = tile * rows + first - rim + reach
            inside = (
                (reach >= offset)
                & (reach < offset + K_WIN)
                & (position >= 0)
                & (position < total)
            )
            scores = jnp.where(inside, scores, excluded)
            top = jnp.max(scores, axis=-1, keepdims=True)
            weights = jnp.exp(scores - top)
            weights = weights * (1.0 / jnp.sum(weights, axis=-1, keepdims=True))
            mixed = dot(weights.astype(BF), vals[first : first + span])
            mixed = mixed[:, :width] + mixed[:, width:]
            gathered = jnp.where(head_of == 0, mixed[:Q_BLOCK], 0.0)
            for h in range(1, A_HEADS):
                gathered += jnp.where(
                    head_of == h, mixed[h * Q_BLOCK : (h + 1) * Q_BLOCK], 0.0
                )
            parts.append(gathered)
        atom_out = (atoms[n] + jnp.concatenate(parts, axis=0)).astype(BF)
        hidden = jnp.maximum(dot(atom_out, agg_weight[...]), 0.0)
        sums = 0.0
        for part in two_parts(hidden):
            sums = sums + dot(member, part)
        token_normal, _ = norm_parts(sums / counts)
        _, noise_code = noise_parts(levels[n])
        token_in.append(token_normal + single_term + noise_code[:, :1] * noise_row)
    token_in = jnp.concatenate(token_in, axis=0)
    count = token_in.shape[0]
    stacked = jnp.concatenate(two_parts(token_in), axis=0)
    proj = dot(stacked, token_weight[...])
    proj = proj[:count] + proj[count:]
    wide = H * HEAD
    cot = jnp.concatenate([cotangent[n].astype(F32) for n in range(copies)], axis=0)
    lane = lax.broadcasted_iota(jnp.int32, (1, 128 - 2 * HEAD), 1)
    for h in range(H):
        at = h * HEAD
        pieces = [
            proj[:, at : at + HEAD] * (1.0 / math.sqrt(HEAD)),
            cot[:, at : at + HEAD],
            proj[:, wide + at : wide + at + HEAD],
            proj[:, 2 * wide + at : 2 * wide + at + HEAD],
        ]
        for half in range(2):
            row = []
            codes = jnp.zeros((1, 128 - 2 * HEAD), F32)
            for at_piece in range(2):
                piece = pieces[2 * half + at_piece]
                top = jnp.max(jnp.max(jnp.abs(piece), axis=0, keepdims=True), axis=1, keepdims=True)
                steps, power = grid_scale(top)
                codes = jnp.where(lane == 2 * at_piece, steps, codes)
                codes = jnp.where(lane == 2 * at_piece + 1, power, codes)
                row.append(piece * (1.0 / scale_value(steps, power)))
            row.append(jnp.broadcast_to(codes, (count, 128 - 2 * HEAD)))
            out[h, :, half * 128 : (half + 1) * 128] = whole(
                jnp.concatenate(row, axis=1)
            ).astype(jnp.int16)


def pair_kernel(pair, trans_in, trans_out, bias_weight_t, unit, cond_out, bias_out, held):
    inner = trans_out.shape[0]
    cols = pair.shape[1]
    step = pl.program_id(0)
    lanes = 128
    row_at = lax.broadcasted_iota(jnp.int32, (256, 256), 0)
    col_at = lax.broadcasted_iota(jnp.int32, (256, 256), 1)
    same = (row_at // lanes) == (col_at // lanes)
    ones = jnp.where(same, 1.0 / lanes, 0.0).astype(BF)
    centre = jnp.where(
        same, jnp.where(row_at == col_at, 1.0 - 1.0 / lanes, -1.0 / lanes), 0.0
    ).astype(BF)

    def normalise(value):
        half = value.shape[0] // 2
        centred = dot(jnp.concatenate([value[:half], value[half:]], axis=1), centre)
        high, low = two_parts(centred * centred)
        spread = dot(high, ones) + dot(low, ones)
        normal = (centred * lax.rsqrt(spread + epsilon)).astype(BF)
        return jnp.concatenate([normal[:, :lanes], normal[:, lanes:]], axis=0)

    group = 4
    chunk = 256
    for part in range(pair.shape[0] // group):
        value = pair[part * group : (part + 1) * group].reshape(group * cols, lanes)
        normed = normalise(value)
        delta = value.astype(F32)
        hidden = []
        for f in range(inner // chunk):
            half = dot(normed, trans_in[:, f * chunk : (f + 1) * chunk] * 0.5)
            up = dot(normed, trans_in[:, inner + f * chunk : inner + (f + 1) * chunk])
            hidden.append(((half + half * jnp.tanh(half)) * up).astype(BF))
        delta = delta + dot(jnp.concatenate(hidden, axis=1), trans_out[...])
        cond = delta.astype(BF)
        cond_out[part * group : (part + 1) * group] = cond.reshape(group, cols, lanes)
        bias = dot(bias_weight_t[...], normalise(cond), NT) * (1.0 / unit[...])
        for i in range(group):
            held[step, :, part * group + i, :] = bias[:, i * cols : (i + 1) * cols]

    @pl.when(step == pl.num_programs(0) - 1)
    def _():
        for s in range(held.shape[0]):
            rows = held.shape[2]
            bias_out[:, s * rows : (s + 1) * rows, :] = whole(held[s]).astype(jnp.int16)


def attend_kernel(place, unit, queries, kv, bias_mine, bias_other, update_mine, grad_other):
    core = place[0]
    blocks = [core, 2 + core, 1 - core, 3 - core]
    cols = 384
    tok = 24
    rows = 8 * tok
    lane = lax.broadcasted_iota(jnp.int32, (1, 128), 1)
    is_key = lane < HEAD
    is_value = (lane >= HEAD) & (lane < 2 * HEAD)

    def decode(block):
        block = block.astype(jnp.int32).astype(F32)
        codes = block[0:1]
        at = 2 * HEAD
        first = scale_value(codes[:, at : at + 1], codes[:, at + 1 : at + 2])
        second = scale_value(codes[:, at + 2 : at + 3], codes[:, at + 3 : at + 4])
        return block * jnp.where(is_key, first, jnp.where(is_value, second, 0.0))

    bias = jnp.concatenate(
        [
            jnp.concatenate(
                [
                    (bias_mine if c < 2 else bias_other)[2 * g + c % 2].astype(jnp.int32).astype(F32)
                    for c in range(4)
                ],
                axis=1,
            )
            for g in range(8)
        ],
        axis=0,
    ) * unit[0]
    grad = None
    for y in range(2):
        query_blocks = [decode(queries[2 * g + y, :, :128]) for g in range(8)]
        token_blocks = [
            decode(kv[2 * c + z, 2 * g + y]) for c in blocks for z in range(2) for g in range(8)
        ]
        for p in range(2):
            query = jnp.concatenate([b[p * tok : (p + 1) * tok] for b in query_blocks], axis=0)
            q_high, q_low = two_parts(jnp.where(is_key, query, 0.0))
            c_high, c_low = two_parts(jnp.where(is_value, query, 0.0))
            high, low = two_parts(
                jnp.concatenate([b[p * tok : (p + 1) * tok] for b in token_blocks], axis=0)
            )
            both = jnp.concatenate([high, low], axis=1)
            none = jnp.zeros_like(q_low)
            stacked = jnp.concatenate(
                [
                    jnp.concatenate([q_high, q_high], axis=1),
                    jnp.concatenate([q_low, none], axis=1),
                    jnp.concatenate([c_high, c_high], axis=1),
                    jnp.concatenate([c_low, none], axis=1),
                ],
                axis=0,
            )
            products = dot(stacked, both, NT)
            scores = products[:rows] + products[rows : 2 * rows] + bias
            prob_grad = products[2 * rows : 3 * rows] + products[3 * rows :]
            top = jnp.max(scores, axis=-1, keepdims=True)
            weights = jnp.exp(scores - top)
            weights = weights * (1.0 / jnp.sum(weights, axis=-1, keepdims=True))
            mixed = dot(weights.astype(BF), both)
            mixed = mixed[:, :128] + mixed[:, 128:]
            for g in range(8):
                update_mine[2 * g + y, :, cols + p * HEAD : cols + (p + 1) * HEAD] = mixed[
                    g * tok : (g + 1) * tok, HEAD : 2 * HEAD
                ]
            term = weights * prob_grad
            term = term - weights * jnp.sum(term, axis=-1, keepdims=True)
            grad = term if grad is None else grad + term
    for g in range(8):
        for c in range(4):
            (update_mine if c < 2 else grad_other)[2 * g + c % 2, :, :cols] = grad[
                g * tok : (g + 1) * tok, c * cols : (c + 1) * cols
            ]


def merge_kernel(mine, other, out):
    cols = other.shape[2]
    used = 2 * HEAD
    lane = lax.broadcasted_iota(jnp.int32, (1, 128), 1)
    for h in range(mine.shape[0]):
        grad = mine[h, :, :cols] + other[h]
        update = jnp.where(lane < used, mine[h, :, cols:], 0.0)
        codes = update
        scaled = []
        for at, part in ((0, grad), (2, update)):
            steps, power = grid_scale(jnp.max(jnp.abs(part), axis=-1, keepdims=True))
            scaled.append(part * (1.0 / scale_value(steps, power)))
            codes = jnp.where(lane == used + at, steps, codes)
            codes = jnp.where(lane == used + at + 1, power, codes)
        last = jnp.where(lane < used, scaled[1], codes)
        out[h] = jnp.concatenate(
            [
                whole(scaled[0][:, :256]),
                whole(jnp.concatenate([scaled[0][:, 256:], last], axis=1)),
            ],
            axis=0,
        ).astype(jnp.int16)


def grad_kernel(packed, cond, bias_weight, out, update_out, held):
    step = pl.program_id(0)
    lanes = 128
    heads, _, rows, cols = held.shape[1], 0, held.shape[2], held.shape[3]
    tok = packed.shape[1] // 2

    @pl.when(step == 0)
    def _():
        pieces = [[], []]
        for h in range(heads):
            block = packed[h].astype(jnp.int32).astype(F32)
            low, high = block[:tok], block[tok:]
            at = lanes + 2 * HEAD
            grad_scale = scale_value(high[:, at : at + 1], high[:, at + 1 : at + 2])
            update_scale = scale_value(high[:, at + 2 : at + 3], high[:, at + 3 : at + 4])
            grad = jnp.concatenate([low, high[:, :lanes]], axis=1) * grad_scale
            for s in range(held.shape[0]):
                held[s, h] = grad[s * rows : (s + 1) * rows]
            for p in range(2):
                pieces[p].append(
                    high[:, lanes + p * HEAD : lanes + (p + 1) * HEAD] * update_scale
                )
        for p in range(2):
            update_out[p] = jnp.concatenate(pieces[p], axis=1).astype(BF)

    row_at = lax.broadcasted_iota(jnp.int32, (256, 256), 0)
    col_at = lax.broadcasted_iota(jnp.int32, (256, 256), 1)
    same = (row_at // lanes) == (col_at // lanes)
    ones = jnp.where(same, 1.0 / lanes, 0.0).astype(BF)
    centre = jnp.where(
        same, jnp.where(row_at == col_at, 1.0 - 1.0 / lanes, -1.0 / lanes), 0.0
    ).astype(BF)
    weight = bias_weight[...].astype(F32)
    w_high, w_low = two_parts(weight - jnp.mean(weight, axis=-1, keepdims=True))
    parts = jnp.concatenate([w_high, w_high, w_high, w_low, w_low], axis=0)
    group = 4
    count = group * cols
    half = count // 2

    def paired(value):
        return jnp.concatenate([value[:half], value[half:]], axis=1)

    def mean(value):
        high, low = two_parts(value)
        return dot(high, ones) + dot(low, ones)

    for part in range(rows // group):
        normals = []
        for i in range(group):
            high, middle, low = three_parts(held[step, :, part * group + i, :])
            stacked = jnp.concatenate([high, middle, low, high, middle], axis=0)
            normals.append(dot(stacked, parts, TN))
        grad_normal = paired(jnp.concatenate(normals, axis=0))
        value = cond[part * group : (part + 1) * group].reshape(count, lanes)
        centred = dot(paired(value), centre)
        scale = lax.rsqrt(mean(centred * centred) + epsilon)
        normal = centred * scale
        result = ((grad_normal - normal * mean(grad_normal * normal)) * scale).astype(BF)
        result = jnp.concatenate([result[:, :lanes], result[:, lanes:]], axis=0)
        out[part * group : (part + 1) * group] = result.reshape(group, cols, lanes)


def params(**more):
    return pltpu.CompilerParams(vmem_limit_bytes=56 * 1024 * 1024, **more)


VMEM = pl.BlockSpec(memory_space=pltpu.VMEM)
SMEM = pl.BlockSpec(memory_space=pltpu.SMEM)


def on_device(
    pair_rep,
    single,
    atom_feat,
    coords,
    levels,
    window_offset,
    atom_token,
    trans_in,
    trans_out,
    bias_weight,
    single_weight,
    coord_weight,
    atom_weight,
    agg_weight,
    token_weight,
    noise_weight,
    cotangent,
):
    tile_index = lax.axis_index(TILE).astype(jnp.int32)
    core_index = lax.axis_index("core").astype(jnp.int32)
    copies, tok_rows, width = cotangent.shape
    atom_rows, atom_width = atom_feat.shape
    cols = pair_rep.shape[1]
    rim = K_WIN // 2
    atoms, normed, first, last = pl.pallas_call(
        start_kernel,
        out_shape=(
            jax.ShapeDtypeStruct((copies, atom_rows, atom_width), F32),
            jax.ShapeDtypeStruct((copies, atom_rows, atom_width), BF),
            jax.ShapeDtypeStruct((copies, rim, atom_width), BF),
            jax.ShapeDtypeStruct((copies, rim, atom_width), BF),
        ),
        in_specs=[SMEM] + [VMEM] * 3,
        out_specs=(VMEM,) * 4,
        compiler_params=params(),
        cost_estimate=pl.CostEstimate(flops=1_000_000, bytes_accessed=500_000, transcendentals=0),
        name="atom_start",
    )(levels, atom_feat, coords, coord_weight)
    forward = [(i, i + 1) for i in range(63)]
    backward = [(i + 1, i) for i in range(63)]
    low = lax.ppermute(last, TILE, forward)
    high = lax.ppermute(first, TILE, backward)
    packed = pl.pallas_call(
        atom_kernel,
        out_shape=jax.ShapeDtypeStruct((H, copies * tok_rows, 256), jnp.int16),
        in_specs=[SMEM] * 3 + [VMEM] * 12,
        out_specs=VMEM,
        compiler_params=params(),
        cost_estimate=pl.CostEstimate(flops=3_000_000_000, bytes_accessed=6_000_000, transcendentals=0),
        name="atom_stage",
    )(
        tile_index[None], window_offset, levels, low, high, normed, atoms, atom_weight, agg_weight,
        atom_token, single, single_weight, noise_weight, token_weight, cotangent,
    )
    packed = lax.all_to_all(packed, PLANE, 0, 0, tiled=True)
    kv = lax.all_gather(packed[:, :, 128:], "z", axis=0)

    step = 8
    steps = tok_rows // step
    bias_t = bias_weight.T
    reach = jnp.sqrt(jnp.sum(jnp.square(bias_weight.astype(F32)), axis=0))
    unit = (reach * (math.sqrt(128.0) * 1.01 / 32767.0) + 1e-30).astype(F32)
    cond, bias = pl.pallas_call(
        pair_kernel,
        grid=(steps,),
        out_shape=(
            jax.ShapeDtypeStruct(pair_rep.shape, BF),
            jax.ShapeDtypeStruct((H, tok_rows, cols), jnp.int16),
        ),
        in_specs=[
            pl.BlockSpec((step, cols, 128), lambda i: (i, 0, 0)),
            pl.BlockSpec(trans_in.shape, lambda i: (0, 0)),
            pl.BlockSpec(trans_out.shape, lambda i: (0, 0)),
            pl.BlockSpec(bias_t.shape, lambda i: (0, 0)),
            pl.BlockSpec((H, 1), lambda i: (0, 0)),
        ],
        out_specs=(
            pl.BlockSpec((step, cols, 128), lambda i: (i, 0, 0)),
            pl.BlockSpec((H, tok_rows, cols), lambda i: (0, 0, 0)),
        ),
        scratch_shapes=[pltpu.VMEM((steps, H, step, cols), F32)],
        compiler_params=params(),
        cost_estimate=pl.CostEstimate(flops=4_000_000_000, bytes_accessed=6_000_000, transcendentals=5_000_000),
        name="pair_transition",
    )(pair_rep, trans_in, trans_out, bias_t, unit[:, None])
    bias_mine = lax.all_to_all(bias, PLANE, 0, 0, tiled=True)
    swap = [(0, 1), (1, 0)]
    bias_other = lax.ppermute(bias_mine, "core", swap)

    head_index = lax.axis_index(PLANE)
    grad_mine, grad_other = pl.pallas_call(
        attend_kernel,
        out_shape=(
            jax.ShapeDtypeStruct((H, tok_rows, cols + 128), F32),
            jax.ShapeDtypeStruct((H, tok_rows, cols), F32),
        ),
        in_specs=[SMEM] * 2 + [VMEM] * 4,
        out_specs=(VMEM, VMEM),
        compiler_params=params(),
        cost_estimate=pl.CostEstimate(flops=4_000_000_000, bytes_accessed=8_000_000, transcendentals=1_200_000),
        name="token_attention",
    )(core_index[None], lax.dynamic_slice(unit, (head_index,), (1,)), packed, kv, bias_mine, bias_other)
    merged = pl.pallas_call(
        merge_kernel,
        out_shape=jax.ShapeDtypeStruct((H, 2 * tok_rows, 256), jnp.int16),
        in_specs=[VMEM] * 2,
        out_specs=VMEM,
        compiler_params=params(),
        cost_estimate=pl.CostEstimate(flops=2_000_000, bytes_accessed=2_000_000, transcendentals=0),
        name="gradient_merge",
    )(grad_mine, lax.ppermute(grad_other, "core", swap))
    merged = lax.all_to_all(merged, PLANE, 0, 0, tiled=True)
    gradient, update = pl.pallas_call(
        grad_kernel,
        grid=(steps,),
        out_shape=(
            jax.ShapeDtypeStruct(pair_rep.shape, BF),
            jax.ShapeDtypeStruct(cotangent.shape, BF),
        ),
        in_specs=[
            pl.BlockSpec(merged.shape, lambda i: (0, 0, 0)),
            pl.BlockSpec((step, cols, 128), lambda i: (i, 0, 0)),
            pl.BlockSpec(bias_t.shape, lambda i: (0, 0)),
        ],
        out_specs=(
            pl.BlockSpec((step, cols, 128), lambda i: (i, 0, 0)),
            pl.BlockSpec(cotangent.shape, lambda i: (0, 0, 0)),
        ),
        scratch_shapes=[pltpu.VMEM((steps, H, step, cols), F32)],
        compiler_params=params(),
        cost_estimate=pl.CostEstimate(flops=400_000_000, bytes_accessed=6_000_000, transcendentals=0),
        name="pair_gradient",
    )(merged, cond, bias_t)
    return (update, gradient)


def solution(mesh):
    fine = Mesh(mesh.devices.reshape(8, 8, 2, 2), ("z", "g", "ylo", "core"))
    placed = (
        P(TILE, COPY, None),
        P(TILE, None),
        P(TILE, None),
        P(COPY, None, TILE),
        P(COPY),
        P(TILE),
        P(TILE),
        P(),
        P(),
        P(),
        P(),
        P(),
        P(),
        P(),
        P(),
        P(),
        P(COPY, TILE, None),
    )
    return jax.shard_map(
        on_device,
        mesh=fine,
        in_specs=placed,
        out_specs=(P(COPY, TILE, None), P(TILE, COPY, None)),
        check_vma=False,
    )
```

time: 161 us -> 143 us (0.89)
  between operations: 14.1 us -> 0.74 us
  waiting for transfers between devices: 20.4 us -> 7.38 us
  starting transfers between devices: 21.1 us -> 30.9 us
  other arithmetic: 8.1 us -> 0.81 us
  blocking collectives: 36.4 us -> 43.3 us
  local copies, waits for them, and re-layouts: 7.51 us -> 4.74 us
    all_gather x0 -> x1, blocking collectives: none -> 29.5 us  [on_device(): kv = lax.all_gather(packed[:, :, 128:], 'z', axis=0)]
    all_to_all x2 -> x1, blocking collectives: 36.4 us -> 13.8 us  [on_device(): merged = lax.all_to_all(merged, PLANE, 0, 0, tiled=True)]
    all_to_all x2, waiting for transfers between devices: 13.6 us -> 5.54 us  [the longest x1 5.53 us: on_device(): packed = lax.all_to_all(packed, PLANE, 0, 0, tiled=True)]
    ppermute x3, starting transfers between devices: 6.36 us -> 13.4 us  [the longest x1 8.14 us: on_device(): lax.ppermute(grad_other, 'core', swap)]
    all_to_all x2, starting transfers between devices: 10.1 us -> 15.4 us  [the longest x1 8.77 us: on_device(): bias_mine = lax.all_to_all(bias, PLANE, 0, 0, tiled=True)]
    all_gather x1 -> x0, waiting for transfers between devices: 4.43 us -> none  [on_device(): kv = lax.all_gather(packed[:, :, 128:], 'z', axis=0)]
    add x2 -> x1, other arithmetic: 2.85 us -> 0.01 us  [on_device(): unit = (reach * (math.sqrt(128.0) * 1.01 / 32767.0) + 1e-30).astype(F32)]
    ppermute x1, starting transfers between devices: 4.59 us -> 2.09 us  [on_device(): bias_other = lax.ppermute(bias_mine, 'core', swap)]
  transfers between devices with their start and end apart: 7 -> 6, of which waited for: 5 -> 2; matrix products, arithmetic and copies ran while one was open for 5% -> 1% of each run, Pallas kernels for 15% -> 20%
where the time goes in v2:
time: 143 us; the launch traced here: 142 us
  Pallas kernels  54.3 us (38%)
  blocking collectives  43.3 us (30%)
  starting transfers between devices  30.9 us (22%)
  waiting for transfers between devices  7.38 us (5%)
  local copies, waits for them, and re-layouts  4.74 us (3%)
    all_gather x1, blocking collectives, on_device(): kv = lax.all_gather(packed[:, :, 128:], 'z', axis=0)  29.5 us
    pallas_call x1, Pallas kernels, on_device(): pl.pallas_call(pair_kernel, grid=(steps,), out_shape=(jax.ShapeDtypeStruc...  18.2 us
    all_to_all x1, blocking collectives, on_device(): merged = lax.all_to_all(merged, PLANE, 0, 0, tiled=True)  13.8 us
    pallas_call x1, Pallas kernels, on_device(): pl.pallas_call(grad_kernel, grid=(steps,), out_shape=(jax.ShapeDtypeStruc...  12 us
    pallas_call x1, Pallas kernels, on_device(): pl.pallas_call(atom_kernel, out_shape=jax.ShapeDtypeStruct((H, copies * t...  10.5 us
    pallas_call x1, Pallas kernels, on_device(): pl.pallas_call(attend_kernel, out_shape=(jax.ShapeDtypeStruct((H, tok_row...  9.08 us
    all_to_all x1, starting transfers between devices, on_device(): bias_mine = lax.all_to_all(bias, PLANE, 0, 0, tiled=True)  8.77 us
    ppermute x1, starting transfers between devices, on_device(): lax.ppermute(grad_other, 'core', swap)  8.14 us
  transfers between devices with their start and end apart: 6, of which 2 were waited for; matrix products, arithmetic and copies ran while one was open for 1% of the time, Pallas kernels for 20%

profile of v2, /device:TPU:1, one launch (start us, length us, event | category | flops | bytes accessed | tf_op | source)
XLA Modules:
  0.0 142.2 jit_solution(5732274589163275356)
XLA Ops:
  0.6 1.3 copy.21.coords
  1.9 2.1 %atom_start.1 = (f32[2,192,128]{2,1,0:T(8,128)}, bf16[2,192,128]{2,1,0:T(8,128)(2,1)}, bf16[2,64,128]{2,1,0:T(8,128)(2,1)}, bf16[2,64,128]{2,1,0:T(8,128)(2,1)}) custom-call(s32[2]{0:T(128)} %levels.3, bf16[192,128]{1,0:T(8,128)(2,1)} %feat.1, f32[2,3,192]{2,1,0:T(4,128)} %copy.21.coords, f32[3,128]{1,0:T(4,128)} %coord_weight.1), custom_call_target="tpu_custom_call" | custom-call | flops 1000000 | bytes 500000 | tf_op jit(solution)/shard_map/atom_start/pallas_call | solution.py:451
  4.0 3.9 %collective-permute-start = (bf16[2,64,128]{2,1,0:T(8,128)(2,1)}, bf16[2,64,128]{2,1,0:T(8,128)(2,1)S(1)}, u32[]{:S(2)}, u32[]{:S(2)}) collective-permute-start(bf16[2,64,128]{2,1,0:T(8,128)(2,1)} %get-tuple-element.12), channel_id=1, source_target_pairs={{0,4},{4,8},{8,12},{12,16},{16,20},{20,24},{24,28},{28,32},{32,36}... | collective-permute-start | bytes 98312 | tf_op jit(solution)/shard_map/ppermute | solution.py:467
  8.0 1.3 collective-permute-start.1
  9.3 0.8 multiply_reduce_fusion
  10.1 0.7 copy.22.unit
  10.8 18.2 %pair_transition.1 = (bf16[24,384,128]{2,1,0:T(8,128)(2,1)}, s16[16,24,384]{2,1,0:T(8,128)(2,1)}) custom-call(bf16[24,384,128]{2,1,0:T(8,128)(2,1)} %pair.1, bf16[128,1024]{1,0:T(8,128)(2,1)} %trans_in.1, bf16[512,128]{1,0:T(8,128)(2,1)} %trans_out.1, bf16[16,128]{1,0:T(8,128)(2,1)} %bitcast.7, f32[16,1]{1,0:T(8,128)} %copy.22.unit), custom_call_target="tpu_custom_call" | custom-call | flops 4000000000 | bytes 6000000 | tf_op jit(solution)/shard_map/pair_transition/pallas_call | solution.py:489
  28.9 8.8 %all-to-all-start.1 = ((s16[16,24,384]{2,1,0:T(8,128)(2,1)}), s16[16,24,384]{2,1,0:T(8,128)(2,1)S(1)}, u32[]{:S(2)}, u32[]{:S(2)}) async-start(s16[16,24,384]{2,1,0:T(8,128)(2,1)} %get-tuple-element.16), calls=%async_computation.1 | async-start | bytes 589824 | tf_op jit(solution)/shard_map/all_to_all | solution.py:512
  37.7 0.0 collective-permute-done.low
  37.7 0.0 copy-start.4
  37.7 0.0 collective-permute-done.1.high
  37.7 0.0 copy-start.5
  37.8 0.6 copy-done.4
  38.3 0.0 copy-done.5
  38.4 10.5 %atom_stage.1 = s16[16,48,256]{2,1,0:T(8,128)(2,1)} custom-call(s32[1]{0:T(128)} %bitcast.1.place, s32[6]{0:T(128)} %offsets.1, s32[2]{0:T(128)} %levels.3, bf16[2,64,128]{2,1,0:T(8,128)(2,1)} %copy-done.4, bf16[2,64,128]{2,1,0:T(8,128)(2,1)} %copy-done.5, bf16[2,192,128]{2,1,0:T(8,128)(2,1)} %get-tuple-element.14.normed, ...), custom_call_target="tpu_custom_call" | custom-call | flops 3000000000 | bytes 6000000 | tf_op jit(solution)/shard_map/atom_stage/pallas_call | solution.py:469
  48.9 0.0 all-to-all-done.1.bias_mine
  48.9 0.0 copy-start.2
  48.9 6.6 %all-to-all-start = ((s16[16,48,256]{2,1,0:T(8,128)(2,1)}), s16[16,48,256]{2,1,0:T(8,128)(2,1)S(1)}, u32[]{:S(2)}, u32[]{:S(2)}) async-start(s16[16,48,256]{2,1,0:T(8,128)(2,1)} %atom_stage.1), calls=%async_computation | async-start | bytes 786432 | tf_op jit(solution)/shard_map/all_to_all | solution.py:481
  55.6 0.6 dynamic_slice.3.unit
  56.2 2.1 %collective-permute-start.2 = (s16[16,24,384]{2,1,0:T(8,128)(2,1)S(1)}, s16[16,24,384]{2,1,0:T(8,128)(2,1)S(1)}, u32[]{:S(2)}, u32[]{:S(2)}) collective-permute-start(s16[16,24,384]{2,1,0:T(8,128)(2,1)S(1)} %all-to-all-done.1.bias_mine), channel_id=1, source_target_pairs={{0,1},{1,0},{2,3},{3,2},{4,5},{5,4},{6,7},{7,6},{8,9},{9,8},{10,11... | collective-permute-start | bytes 884744 | tf_op jit(solution)/shard_map/ppermute | solution.py:514
  58.2 5.5 %all-to-all-done.queries = s16[16,48,256]{2,1,0:T(8,128)(2,1)S(1)} async-done(((s16[16,48,256]{2,1,0:T(8,128)(2,1)}), s16[16,48,256]{2,1,0:T(8,128)(2,1)S(1)}, u32[]{:S(2)}, u32[]{:S(2)}) %all-to-all-start) | async-done | bytes 393248 | tf_op jit(solution)/shard_map/all_to_all | solution.py:481
  63.8 0.0 copy-start
  63.8 29.5 %all-gather.2 = s16[128,48,128]{2,1,0:T(8,128)(2,1)} all-gather(s16[16,48,128]{2,1,0:T(8,128)(2,1)S(1)} %slice.4), channel_id=2, replica_groups=mesh['z'=8,'g'=8,'ylo'=2,'core'=2] {'z'}, dimensions={0}, use_global_device_ids=true | all-gather | bytes 1769472 | tf_op jit(solution)/shard_map/all_gather | solution.py:482
  93.3 0.0 collective-permute-done.2.bias_other
  93.3 0.0 copy-start.3
  93.3 0.0 copy-done.2
  93.3 0.0 copy-done
  93.3 0.7 copy-done.3
  94.0 9.1 %token_attention.1 = (f32[16,24,512]{2,1,0:T(8,128)}, f32[16,24,384]{2,1,0:T(8,128)}) custom-call(s32[1]{0:T(128)} %bitcast.place, f32[1]{0:T(128)} %dynamic_slice.3.unit, s16[16,48,256]{2,1,0:T(8,128)(2,1)} %copy-done, s16[8,16,48,128]{3,2,1,0:T(8,128)(2,1)} %bitcast.6, s16[16,24,384]{2,1,0:T(8,128)(2,1)} %copy-done.2, s16[16,24,384]{2,1,0:T(8,128)(2,1)} %copy-done.3), custom_call_target="tpu_custom_call" | custom-call | flops 4000000000 | bytes 8000000 | tf_op jit(solution)/shard_map/token_attention/pallas_call | solution.py:517
  103.1 8.1 %collective-permute-start.3 = (f32[16,24,384]{2,1,0:T(8,128)}, f32[16,24,384]{2,1,0:T(8,128)S(1)}, u32[]{:S(2)}, u32[]{:S(2)}) collective-permute-start(f32[16,24,384]{2,1,0:T(8,128)} %get-tuple-element.18), channel_id=1, source_target_pairs={{0,1},{1,0},{2,3},{3,2},{4,5},{5,4},{6,7},{7,6},{8,9},{9,8},{10,11... | collective-permute-start | bytes 1769480 | tf_op jit(solution)/shard_map/ppermute | solution.py:537
  111.2 1.8 %collective-permute-done.3.other = f32[16,24,384]{2,1,0:T(8,128)S(1)} collective-permute-done((f32[16,24,384]{2,1,0:T(8,128)}, f32[16,24,384]{2,1,0:T(8,128)S(1)}, u32[]{:S(2)}, u32[]{:S(2)}) %collective-permute-start.3) | collective-permute-done | bytes 589856 | tf_op jit(solution)/shard_map/ppermute | solution.py:537
  113.1 0.0 copy-start.1
  113.1 0.8 copy-done.1
  113.9 2.4 %gradient_merge.1 = s16[16,48,256]{2,1,0:T(8,128)(2,1)} custom-call(f32[16,24,512]{2,1,0:T(8,128)} %get-tuple-element.17.mine, f32[16,24,384]{2,1,0:T(8,128)} %copy-done.1), custom_call_target="tpu_custom_call" | custom-call | flops 2000000 | bytes 2000000 | tf_op jit(solution)/shard_map/gradient_merge/pallas_call | solution.py:529
  116.3 13.8 %all_to_all.15.packed = s16[16,48,256]{2,1,0:T(8,128)(2,1)} all-to-all(s16[16,48,256]{2,1,0:T(8,128)(2,1)} %gradient_merge.1), channel_id=1, replica_groups=mesh['z'=8,'g'=8,'ylo'=2,'core'=2] {'g','ylo'}, dimensions={0} | all-to-all | bytes 786432 | tf_op jit(solution)/shard_map/all_to_all | solution.py:538
  130.1 12.0 %pair_gradient.1 = (bf16[24,384,128]{2,1,0:T(8,128)(2,1)}, bf16[2,24,768]{2,1,0:T(8,128)(2,1)}) custom-call(s16[16,48,256]{2,1,0:T(8,128)(2,1)} %all_to_all.15.packed, bf16[24,384,128]{2,1,0:T(8,128)(2,1)} %get-tuple-element.19.cond, bf16[16,128]{1,0:T(8,128)(2,1)} %bitcast.8), custom_call_target="tpu_custom_call" | custom-call | flops 400000000 | bytes 6000000 | tf_op jit(solution)/shard_map/pair_gradient/pallas_call | solution.py:539
  (2 shorter events, 0.0 us)
Async XLA Ops:
  4.0 33.7 %collective-permute-start = (bf16[2,64,128]{2,1,0:T(8,128)(2,1)}, bf16[2,64,128]{2,1,0:T(8,128)(2,1)S(1)}, u32[]{:S(2)}, u32[]{:S(2)}) collective-permute-start(bf16[2,64,128]{2,1,0:T(8,128)(2,1)} %get-tuple-element.12), channel_id=1, source_target_pairs={{0,4},{4,8},{8,12},{12,16},{16,20},{20,24},{24,28},{28,32},{32,36}... | collective-permute-start | bytes 98312 | tf_op jit(solution)/shard_map/ppermute | solution.py:467
  8.0 29.8 %collective-permute-start.1 = (bf16[2,64,128]{2,1,0:T(8,128)(2,1)}, bf16[2,64,128]{2,1,0:T(8,128)(2,1)S(1)}, u32[]{:S(2)}, u32[]{:S(2)}) collective-permute-start(bf16[2,64,128]{2,1,0:T(8,128)(2,1)} %get-tuple-element.13), channel_id=1, source_target_pairs={{4,0},{8,4},{12,8},{16,12},{20,16},{24,20},{28,24},{32,28},{36,32}... | collective-permute-start | bytes 98312 | tf_op jit(solution)/shard_map/ppermute | solution.py:468
  28.9 20.0 %all-to-all-start.1 = ((s16[16,24,384]{2,1,0:T(8,128)(2,1)}), s16[16,24,384]{2,1,0:T(8,128)(2,1)S(1)}, u32[]{:S(2)}, u32[]{:S(2)}) async-start(s16[16,24,384]{2,1,0:T(8,128)(2,1)} %get-tuple-element.16), calls=%async_computation.1 | async-start | bytes 589824 | tf_op jit(solution)/shard_map/all_to_all | solution.py:512
  37.7 0.6 copy-start.4
  37.7 0.6 copy-start.5
  48.9 44.4 %copy-start.2 = (s16[16,24,384]{2,1,0:T(8,128)(2,1)}, s16[16,24,384]{2,1,0:T(8,128)(2,1)S(1)}, u32[]{:S(2)}) copy-start(s16[16,24,384]{2,1,0:T(8,128)(2,1)S(1)} %all-to-all-done.1.bias_mine) | copy-start | bytes 884740
  48.9 14.9 %all-to-all-start = ((s16[16,48,256]{2,1,0:T(8,128)(2,1)}), s16[16,48,256]{2,1,0:T(8,128)(2,1)S(1)}, u32[]{:S(2)}, u32[]{:S(2)}) async-start(s16[16,48,256]{2,1,0:T(8,128)(2,1)} %atom_stage.1), calls=%async_computation | async-start | bytes 786432 | tf_op jit(solution)/shard_map/all_to_all | solution.py:481
  56.2 37.1 %collective-permute-start.2 = (s16[16,24,384]{2,1,0:T(8,128)(2,1)S(1)}, s16[16,24,384]{2,1,0:T(8,128)(2,1)S(1)}, u32[]{:S(2)}, u32[]{:S(2)}) collective-permute-start(s16[16,24,384]{2,1,0:T(8,128)(2,1)S(1)} %all-to-all-done.1.bias_mine), channel_id=1, source_target_pairs={{0,1},{1,0},{2,3},{3,2},{4,5},{5,4},{6,7},{7,6},{8,9},{9,8},{10,11... | collective-permute-start | bytes 884744 | tf_op jit(solution)/shard_map/ppermute | solution.py:514
  63.8 29.5 %copy-start = (s16[16,48,256]{2,1,0:T(8,128)(2,1)}, s16[16,48,256]{2,1,0:T(8,128)(2,1)S(1)}, u32[]{:S(2)}) copy-start(s16[16,48,256]{2,1,0:T(8,128)(2,1)S(1)} %all-to-all-done.queries) | copy-start | bytes 1179652
  93.3 0.7 copy-start.3
  103.1 10.0 %collective-permute-start.3 = (f32[16,24,384]{2,1,0:T(8,128)}, f32[16,24,384]{2,1,0:T(8,128)S(1)}, u32[]{:S(2)}, u32[]{:S(2)}) collective-permute-start(f32[16,24,384]{2,1,0:T(8,128)} %get-tuple-element.18), channel_id=1, source_target_pairs={{0,1},{1,0},{2,3},{3,2},{4,5},{5,4},{6,7},{7,6},{8,9},{9,8},{10,11... | collective-permute-start | bytes 1769480 | tf_op jit(solution)/shard_map/ppermute | solution.py:537
  113.1 0.8 copy-start.1

commit v3 on v2

--- a/solution.py
+++ b/solution.py
@@ -103,9 +103,11 @@
 
 def atom_kernel(
     place, offsets, levels, low, high, normed, atoms, atom_weight, agg_weight, atom_token,
-    single, single_weight, noise_weight, token_weight, cotangent, out
+    single, single_weight, noise_weight, token_weight, cotangent, out, weight_held, arrival
 ):
     tile = place[0]
+    fetch = pltpu.make_async_copy(token_weight, weight_held, arrival)
+    fetch.start()
     copies, rows, width = normed.shape
     blocks = rows // Q_BLOCK
     span = K_WIN + Q_BLOCK
@@ -113,6 +115,7 @@
     total = 64 * rows
     tok_rows = single.shape[0]
     head_of = lax.broadcasted_iota(jnp.int32, (Q_BLOCK, width), 1) // A_HEAD
+    twice_head = lax.broadcasted_iota(jnp.int32, (Q_BLOCK, 2 * width), 1) % width // A_HEAD
     reach = lax.broadcasted_iota(jnp.int32, (1, span), 1)
     local_token = atom_token[...].reshape(1, rows) - tile * tok_rows
     member = (lax.broadcasted_iota(jnp.int32, (tok_rows, rows), 0) == local_token).astype(F32)
@@ -120,32 +123,30 @@
     member = member.astype(BF)
     single_term = dot(single[...], single_weight[...])
     noise_row = noise_weight[...].reshape(1, noise_weight.shape[0])
-    token_in = []
+    scores = []
+    vals = []
     for n in range(copies):
         ext = jnp.concatenate([low[n], normed[n], high[n]], axis=0)
         proj = dot(ext, atom_weight[...])
         queries = proj[rim : rim + rows, :width] * (1.0 / math.sqrt(A_HEAD))
+        q_high, q_low = two_parts(queries)
         key_high, key_low = two_parts(proj[:, width : 2 * width])
-        val_high, val_low = two_parts(proj[:, 2 * width :])
         keys = jnp.concatenate([key_high, key_low], axis=1)
-        vals = jnp.concatenate([val_high, val_low], axis=1)
-        parts = []
+        vals.append(jnp.concatenate(two_parts(proj[:, 2 * width :]), axis=1))
+        twice = jnp.concatenate([q_high, q_high], axis=1)
+        once = jnp.concatenate([q_low, jnp.zeros_like(q_low)], axis=1)
+        blank = jnp.zeros((Q_BLOCK, 2 * width), BF)
         for b in range(blocks):
             first = b * Q_BLOCK
-            block = queries[first : first + Q_BLOCK]
-            spread = jnp.concatenate(
-                [jnp.where(head_of == h, block, 0.0) for h in range(A_HEADS)], axis=0
-            )
-            q_high, q_low = two_parts(spread)
             stacked = jnp.concatenate(
                 [
-                    jnp.concatenate([q_high, q_high], axis=1),
-                    jnp.concatenate([q_low, jnp.zeros_like(q_low)], axis=1),
+                    jnp.where(twice_head == h, part[first : first + Q_BLOCK], blank)
+                    for part in (twice, once)
+                    for h in range(A_HEADS)
                 ],
                 axis=0,
             )
-            scores = dot(stacked, keys[first : first + span], NT)
-            scores = scores[: A_HEADS * Q_BLOCK] + scores[A_HEADS * Q_BLOCK :]
+            both = dot(stacked, keys[first : first + span], NT)
             offset = offsets[b]
             position = tile * rows + first - rim + reach
             inside = (
@@ -154,11 +155,19 @@
                 & (position >= 0)
                 & (position < total)
             )
-            scores = jnp.where(inside, scores, excluded)
-            top = jnp.max(scores, axis=-1, keepdims=True)
-            weights = jnp.exp(scores - top)
-            weights = weights * (1.0 / jnp.sum(weights, axis=-1, keepdims=True))
-            mixed = dot(weights.astype(BF), vals[first : first + span])
+            half = A_HEADS * Q_BLOCK
+            scores.append(jnp.where(inside, both[:half] + both[half:], excluded))
+    scores = jnp.concatenate(scores, axis=0)
+    weights = jnp.exp(scores - jnp.max(scores, axis=-1, keepdims=True))
+    weights = weights * (1.0 / jnp.sum(weights, axis=-1, keepdims=True))
+    weights = weights.astype(BF)
+    token_in = []
+    for n in range(copies):
+        parts = []
+        for b in range(blocks):
+            first = b * Q_BLOCK
+            at = (n * blocks + b) * A_HEADS * Q_BLOCK
+            mixed = dot(weights[at : at + A_HEADS * Q_BLOCK], vals[n][first : first + span])
             mixed = mixed[:, :width] + mixed[:, width:]
             gathered = jnp.where(head_of == 0, mixed[:Q_BLOCK], 0.0)
             for h in range(1, A_HEADS):
@@ -177,83 +186,162 @@
     token_in = jnp.concatenate(token_in, axis=0)
     count = token_in.shape[0]
     stacked = jnp.concatenate(two_parts(token_in), axis=0)
-    proj = dot(stacked, token_weight[...])
+    fetch.wait()
+    proj = dot(stacked, weight_held[...])
     proj = proj[:count] + proj[count:]
     wide = H * HEAD
     cot = jnp.concatenate([cotangent[n].astype(F32) for n in range(copies)], axis=0)
-    lane = lax.broadcasted_iota(jnp.int32, (1, 128 - 2 * HEAD), 1)
+    head_at = lax.broadcasted_iota(jnp.int32, (H, wide), 1) // HEAD
+    mine = head_at == lax.broadcasted_iota(jnp.int32, (H, wide), 0)
+    lane = lax.broadcasted_iota(jnp.int32, (H, 128 - 2 * HEAD), 1)
+    codes = [jnp.zeros(lane.shape, F32)] * 2
+    coded = []
+    sources = [
+        proj[:, :wide] * (1.0 / math.sqrt(HEAD)), cot, proj[:, wide : 2 * wide], proj[:, 2 * wide :]
+    ]
+    for index, source in enumerate(sources):
+        top = jnp.max(jnp.abs(source), axis=0, keepdims=True)
+        steps, power = grid_scale(jnp.max(jnp.where(mine, top, 0.0), axis=1, keepdims=True))
+        inverse = 1.0 / scale_value(steps, power)
+        inverse = jnp.max(jnp.where(mine, inverse, 0.0), axis=0, keepdims=True)
+        coded.append(jnp.round(source * inverse))
+        half, at = index // 2, 2 * (index % 2)
+        codes[half] = jnp.where(
+            lane == at, steps, jnp.where(lane == at + 1, power, codes[half])
+        )
     for h in range(H):
         at = h * HEAD
-        pieces = [
-            proj[:, at : at + HEAD] * (1.0 / math.sqrt(HEAD)),
-            cot[:, at : at + HEAD],
-            proj[:, wide + at : wide + at + HEAD],
-            proj[:, 2 * wide + at : 2 * wide + at + HEAD],
-        ]
         for half in range(2):
-            row = []
-            codes = jnp.zeros((1, 128 - 2 * HEAD), F32)
-            for at_piece in range(2):
-                piece = pieces[2 * half + at_piece]
-                top = jnp.max(jnp.max(jnp.abs(piece), axis=0, keepdims=True), axis=1, keepdims=True)
-                steps, power = grid_scale(top)
-                codes = jnp.where(lane == 2 * at_piece, steps, codes)
-                codes = jnp.where(lane == 2 * at_piece + 1, power, codes)
-                row.append(piece * (1.0 / scale_value(steps, power)))
-            row.append(jnp.broadcast_to(codes, (count, 128 - 2 * HEAD)))
-            out[h, :, half * 128 : (half + 1) * 128] = whole(
-                jnp.concatenate(row, axis=1)
-            ).astype(jnp.int16)
-
-
-def pair_kernel(pair, trans_in, trans_out, bias_weight_t, unit, cond_out, bias_out, held):
-    inner = trans_out.shape[0]
-    cols = pair.shape[1]
-    step = pl.program_id(0)
-    lanes = 128
-    row_at = lax.broadcasted_iota(jnp.int32, (256, 256), 0)
-    col_at = lax.broadcasted_iota(jnp.int32, (256, 256), 1)
+            row = [coded[2 * half + k][:, at : at + HEAD] for k in range(2)]
+            row.append(jnp.broadcast_to(codes[half][h : h + 1], (count, 128 - 2 * HEAD)))
+            out[h, :, half * 128 : (half + 1) * 128] = (
+                jnp.concatenate(row, axis=1).astype(jnp.int32).astype(jnp.int16)
+            )
+
+
+def head_unit(weight):
+    weight = weight.astype(F32)
+    reach = jnp.sqrt(jnp.sum(weight * weight, axis=-1, keepdims=True))
+    return reach * (math.sqrt(128.0) * 1.01 / 32767.0) + 1e-30
+
+
+def lane_matrices(lanes):
+    row_at = lax.broadcasted_iota(jnp.int32, (2 * lanes, 2 * lanes), 0)
+    col_at = lax.broadcasted_iota(jnp.int32, (2 * lanes, 2 * lanes), 1)
     same = (row_at // lanes) == (col_at // lanes)
     ones = jnp.where(same, 1.0 / lanes, 0.0).astype(BF)
     centre = jnp.where(
         same, jnp.where(row_at == col_at, 1.0 - 1.0 / lanes, -1.0 / lanes), 0.0
     ).astype(BF)
+    return jnp.concatenate([ones, ones], axis=0), centre
+
+
+def lane_mean(value, ones):
+    return dot(jnp.concatenate(two_parts(value), axis=1), ones)
+
+
+def pair_block(pair, trans_in, trans_out, bias_weight_t, cond_out, store):
+    inner = trans_out.shape[0]
+    cols = pair.shape[1]
+    lanes = 128
+    ones, centre = lane_matrices(lanes)
+    unit = head_unit(bias_weight_t[...])
 
     def normalise(value):
         half = value.shape[0] // 2
         centred = dot(jnp.concatenate([value[:half], value[half:]], axis=1), centre)
-        high, low = two_parts(centred * centred)
-        spread = dot(high, ones) + dot(low, ones)
-        normal = (centred * lax.rsqrt(spread + epsilon)).astype(BF)
+        normal = (centred * lax.rsqrt(lane_mean(centred * centred, ones) + epsilon)).astype(BF)
         return jnp.concatenate([normal[:, :lanes], normal[:, lanes:]], axis=0)
 
     group = 4
-    chunk = 256
+    chunk = 128
+    weights = [
+        jnp.concatenate(
+            [
+                trans_in[:, f : f + chunk] * 0.5,
+                trans_in[:, inner + f : inner + f + chunk],
+            ],
+            axis=1,
+        )
+        for f in range(0, inner, chunk)
+    ]
     for part in range(pair.shape[0] // group):
         value = pair[part * group : (part + 1) * group].reshape(group * cols, lanes)
         normed = normalise(value)
         delta = value.astype(F32)
         hidden = []
-        for f in range(inner // chunk):
-            half = dot(normed, trans_in[:, f * chunk : (f + 1) * chunk] * 0.5)
-            up = dot(normed, trans_in[:, inner + f * chunk : inner + (f + 1) * chunk])
-            hidden.append(((half + half * jnp.tanh(half)) * up).astype(BF))
+        for weight in weights:
+            both = dot(normed, weight)
+            half = both[:, :chunk]
+            hidden.append(((half + half * jnp.tanh(half)) * both[:, chunk:]).astype(BF))
         delta = delta + dot(jnp.concatenate(hidden, axis=1), trans_out[...])
         cond = delta.astype(BF)
         cond_out[part * group : (part + 1) * group] = cond.reshape(group, cols, lanes)
-        bias = dot(bias_weight_t[...], normalise(cond), NT) * (1.0 / unit[...])
+        bias = dot(bias_weight_t[...], normalise(cond), NT) * (1.0 / unit)
         for i in range(group):
-            held[step, :, part * group + i, :] = bias[:, i * cols : (i + 1) * cols]
-
-    @pl.when(step == pl.num_programs(0) - 1)
-    def _():
-        for s in range(held.shape[0]):
-            rows = held.shape[2]
-            bias_out[:, s * rows : (s + 1) * rows, :] = whole(held[s]).astype(jnp.int16)
-
-
-def attend_kernel(place, unit, queries, kv, bias_mine, bias_other, update_mine, grad_other):
-    core = place[0]
+            store(part * group + i, bias[:, i * cols : (i + 1) * cols])
+
+
+def pair_first_kernel(pair, trans_in, trans_out, bias_weight_t, anchor, cond_out, bias_out):
+    def store(i, value):
+        bias_out[:, i, :] = value
+
+    pair_block(pair, trans_in, trans_out, bias_weight_t, cond_out, store)
+
+
+def pair_next_kernel(pair, trans_in, trans_out, bias_weight_t, anchor, cond, cond_out, bias_out):
+    pair_first_kernel(pair, trans_in, trans_out, bias_weight_t, anchor, cond_out, bias_out)
+
+
+def pair_last_kernel(
+    pair, trans_in, trans_out, bias_weight_t, anchor, cond, first, second, cond_out, bias_out, held
+):
+    def store(i, value):
+        held[:, i, :] = value
+
+    pair_block(pair, trans_in, trans_out, bias_weight_t, cond_out, store)
+    for h in range(bias_out.shape[0]):
+        parts = [first[h], second[h], held[h]]
+        bias_out[h] = whole(jnp.concatenate(parts, axis=0)).astype(jnp.int16)
+
+
+def pair_call(kernel, index, inputs, extra, anchor, cond, bias_shape, scratch=()):
+    pair_rep, trans_in, trans_out, bias_t = inputs
+    step, cols = 8, pair_rep.shape[1]
+    block = pl.BlockSpec((step, cols, 128), lambda i: (index, 0, 0))
+    operands = [pair_rep, trans_in, trans_out, bias_t, anchor]
+    if cond is not None:
+        operands.append(cond)
+    count = len(operands)
+    specs = [block] + [pl.BlockSpec(x.shape, lambda i: (0, 0)) for x in operands[1:4]]
+    specs += [ANY] * (count - 4)
+    specs += [pl.BlockSpec(x.shape, lambda i: (0, 0, 0)) for x in extra]
+    return pl.pallas_call(
+        kernel,
+        grid=(1,),
+        out_shape=(jax.ShapeDtypeStruct(pair_rep.shape, BF), bias_shape),
+        in_specs=specs,
+        out_specs=(block, pl.BlockSpec(bias_shape.shape, lambda i: (0, 0, 0))),
+        scratch_shapes=list(scratch),
+        input_output_aliases={} if cond is None else {5: 0},
+        compiler_params=params(),
+        cost_estimate=pl.CostEstimate(
+            flops=6_000_000_000, bytes_accessed=8_000_000, transcendentals=0
+        ),
+        name="pair_part",
+    )(*operands, *extra)
+
+
+def attend_kernel(
+    core_at, head_at, z_at, queries, kv0, kv1, kv2, kv3, kv4, kv5, kv6, kv7, bias_mine, bias_other, bias_weight_t,
+    update_mine, grad_other, kv
+):
+    core = core_at[0]
+    unit = head_unit(bias_weight_t[...])
+    this = lax.broadcasted_iota(jnp.int32, unit.shape, 0) == head_at[0]
+    unit = jnp.sum(jnp.where(this, unit, 0.0), axis=0, keepdims=True)
+    for back, block in enumerate((kv0, kv1, kv2, kv3, kv4, kv5, kv6, kv7)):
+        kv[lax.rem(z_at[0] + 8 - back, 8)] = block[...]
     blocks = [core, 2 + core, 1 - core, 3 - core]
     cols = 384
     tok = 24
@@ -282,7 +370,7 @@
             for g in range(8)
         ],
         axis=0,
-    ) * unit[0]
+    ) * unit
     grad = None
     for y in range(2):
         query_blocks = [decode(queries[2 * g + y, :, :128]) for g in range(8)]
@@ -378,13 +466,7 @@
         for p in range(2):
             update_out[p] = jnp.concatenate(pieces[p], axis=1).astype(BF)
 
-    row_at = lax.broadcasted_iota(jnp.int32, (256, 256), 0)
-    col_at = lax.broadcasted_iota(jnp.int32, (256, 256), 1)
-    same = (row_at // lanes) == (col_at // lanes)
-    ones = jnp.where(same, 1.0 / lanes, 0.0).astype(BF)
-    centre = jnp.where(
-        same, jnp.where(row_at == col_at, 1.0 - 1.0 / lanes, -1.0 / lanes), 0.0
-    ).astype(BF)
+    ones, centre = lane_matrices(lanes)
     weight = bias_weight[...].astype(F32)
     w_high, w_low = two_parts(weight - jnp.mean(weight, axis=-1, keepdims=True))
     parts = jnp.concatenate([w_high, w_high, w_high, w_low, w_low], axis=0)
@@ -395,22 +477,18 @@
     def paired(value):
         return jnp.concatenate([value[:half], value[half:]], axis=1)
 
-    def mean(value):
-        high, low = two_parts(value)
-        return dot(high, ones) + dot(low, ones)
-
     for part in range(rows // group):
-        normals = []
-        for i in range(group):
-            high, middle, low = three_parts(held[step, :, part * group + i, :])
-            stacked = jnp.concatenate([high, middle, low, high, middle], axis=0)
-            normals.append(dot(stacked, parts, TN))
-        grad_normal = paired(jnp.concatenate(normals, axis=0))
+        grad = jnp.concatenate(
+            [held[step, :, part * group + i, :] for i in range(group)], axis=1
+        )
+        high, middle, low = three_parts(grad)
+        stacked = jnp.concatenate([high, middle, low, high, middle], axis=0)
+        grad_normal = paired(dot(stacked, parts, TN))
         value = cond[part * group : (part + 1) * group].reshape(count, lanes)
         centred = dot(paired(value), centre)
-        scale = lax.rsqrt(mean(centred * centred) + epsilon)
+        scale = lax.rsqrt(lane_mean(centred * centred, ones) + epsilon)
         normal = centred * scale
-        result = ((grad_normal - normal * mean(grad_normal * normal)) * scale).astype(BF)
+        result = ((grad_normal - normal * lane_mean(grad_normal * normal, ones)) * scale).astype(BF)
         result = jnp.concatenate([result[:, :lanes], result[:, lanes:]], axis=0)
         out[part * group : (part + 1) * group] = result.reshape(group, cols, lanes)
 
@@ -421,6 +499,7 @@
 
 VMEM = pl.BlockSpec(memory_space=pltpu.VMEM)
 SMEM = pl.BlockSpec(memory_space=pltpu.SMEM)
+ANY = pl.BlockSpec(memory_space=pl.ANY)
 
 
 def on_device(
@@ -466,11 +545,18 @@
     backward = [(i + 1, i) for i in range(63)]
     low = lax.ppermute(last, TILE, forward)
     high = lax.ppermute(first, TILE, backward)
+    bias_t = bias_weight.T
+    inputs = (pair_rep, trans_in, trans_out, bias_t)
+    step = 8
+    part_bias = jax.ShapeDtypeStruct((H, step, cols), F32)
+    cond, bias_first = pair_call(pair_first_kernel, 0, inputs, [], last, None, part_bias)
+    low, high, bias_first = lax.optimization_barrier((low, high, bias_first))
     packed = pl.pallas_call(
         atom_kernel,
         out_shape=jax.ShapeDtypeStruct((H, copies * tok_rows, 256), jnp.int16),
-        in_specs=[SMEM] * 3 + [VMEM] * 12,
+        in_specs=[SMEM] * 3 + [VMEM] * 10 + [ANY, VMEM],
         out_specs=VMEM,
+        scratch_shapes=[pltpu.VMEM(token_weight.shape, BF), pltpu.SemaphoreType.DMA],
         compiler_params=params(),
         cost_estimate=pl.CostEstimate(flops=3_000_000_000, bytes_accessed=6_000_000, transcendentals=0),
         name="atom_stage",
@@ -478,54 +564,49 @@
         tile_index[None], window_offset, levels, low, high, normed, atoms, atom_weight, agg_weight,
         atom_token, single, single_weight, noise_weight, token_weight, cotangent,
     )
+    cond, bias_second = pair_call(
+        pair_next_kernel, 1, inputs, [], packed, cond, part_bias
+    )
     packed = lax.all_to_all(packed, PLANE, 0, 0, tiled=True)
-    kv = lax.all_gather(packed[:, :, 128:], "z", axis=0)
-
-    step = 8
+    packed, bias_second = lax.optimization_barrier((packed, bias_second))
+    own = packed[:, :, 128:]
+    ahead = [(i, (i + 1) % 8) for i in range(8)]
+    behind = [(i, (i + 7) % 8) for i in range(8)]
+    rising = [own, lax.ppermute(own, "z", ahead)]
+    falling = [own, lax.ppermute(own, "z", behind)]
+    cond, bias = pair_call(
+        pair_last_kernel, 2, inputs, [bias_first, bias_second], own, cond,
+        jax.ShapeDtypeStruct((H, tok_rows, cols), jnp.int16), [pltpu.VMEM((H, step, cols), F32)],
+    )
+    rising[1], falling[1], bias = lax.optimization_barrier((rising[1], falling[1], bias))
+    rising.append(lax.ppermute(rising[1], "z", ahead))
+    falling.append(lax.ppermute(falling[1], "z", behind))
+    rising.append(lax.ppermute(rising[2], "z", ahead))
+    falling.append(lax.ppermute(falling[2], "z", behind))
+    rising.append(lax.ppermute(rising[3], "z", ahead))
+    every = rising + [falling[3], falling[2], falling[1]]
     steps = tok_rows // step
-    bias_t = bias_weight.T
-    reach = jnp.sqrt(jnp.sum(jnp.square(bias_weight.astype(F32)), axis=0))
-    unit = (reach * (math.sqrt(128.0) * 1.01 / 32767.0) + 1e-30).astype(F32)
-    cond, bias = pl.pallas_call(
-        pair_kernel,
-        grid=(steps,),
-        out_shape=(
-            jax.ShapeDtypeStruct(pair_rep.shape, BF),
-            jax.ShapeDtypeStruct((H, tok_rows, cols), jnp.int16),
-        ),
-        in_specs=[
-            pl.BlockSpec((step, cols, 128), lambda i: (i, 0, 0)),
-            pl.BlockSpec(trans_in.shape, lambda i: (0, 0)),
-            pl.BlockSpec(trans_out.shape, lambda i: (0, 0)),
-            pl.BlockSpec(bias_t.shape, lambda i: (0, 0)),
-            pl.BlockSpec((H, 1), lambda i: (0, 0)),
-        ],
-        out_specs=(
-            pl.BlockSpec((step, cols, 128), lambda i: (i, 0, 0)),
-            pl.BlockSpec((H, tok_rows, cols), lambda i: (0, 0, 0)),
-        ),
-        scratch_shapes=[pltpu.VMEM((steps, H, step, cols), F32)],
-        compiler_params=params(),
-        cost_estimate=pl.CostEstimate(flops=4_000_000_000, bytes_accessed=6_000_000, transcendentals=5_000_000),
-        name="pair_transition",
-    )(pair_rep, trans_in, trans_out, bias_t, unit[:, None])
     bias_mine = lax.all_to_all(bias, PLANE, 0, 0, tiled=True)
     swap = [(0, 1), (1, 0)]
     bias_other = lax.ppermute(bias_mine, "core", swap)
 
-    head_index = lax.axis_index(PLANE)
+    head_index = lax.axis_index(PLANE).astype(jnp.int32)
+    z_index = lax.axis_index("z").astype(jnp.int32)
     grad_mine, grad_other = pl.pallas_call(
         attend_kernel,
         out_shape=(
             jax.ShapeDtypeStruct((H, tok_rows, cols + 128), F32),
             jax.ShapeDtypeStruct((H, tok_rows, cols), F32),
         ),
-        in_specs=[SMEM] * 2 + [VMEM] * 4,
+        in_specs=[SMEM] * 3 + [VMEM] * 12,
         out_specs=(VMEM, VMEM),
+        scratch_shapes=[pltpu.VMEM((8,) + own.shape, jnp.int16)],
         compiler_params=params(),
         cost_estimate=pl.CostEstimate(flops=4_000_000_000, bytes_accessed=8_000_000, transcendentals=1_200_000),
         name="token_attention",
-    )(core_index[None], lax.dynamic_slice(unit, (head_index,), (1,)), packed, kv, bias_mine, bias_other)
+    )(
+        core_index[None], head_index[None], z_index[None], packed, *every, bias_mine, bias_other, bias_t
+    )
     merged = pl.pallas_call(
         merge_kernel,
         out_shape=jax.ShapeDtypeStruct((H, 2 * tok_rows, 256), jnp.int16),

time: 143 us -> 120 us (0.84)
  blocking collectives: 43.3 us -> 13.8 us
  waiting for transfers between devices: 7.38 us -> 14.1 us
  starting transfers between devices: 30.9 us -> 37.6 us
  Pallas kernels: 54.3 us -> 50.1 us
    all_gather x1 -> x0, blocking collectives: 29.5 us -> none  [on_device(): kv = lax.all_gather(packed[:, :, 128:], 'z', axis=0)]
    ppermute x0 -> x7, starting transfers between devices: none -> 9.73 us  [the longest x1 3.27 us: on_device(): falling.append(lax.ppermute(falling[1], 'z', behind))]
    ppermute x0 -> x7, waiting for transfers between devices: none -> 7.09 us  [the longest x1 5.07 us: on_device(): falling.append(lax.ppermute(falling[2], 'z', behind))]
    ppermute x1, starting transfers between devices: 8.14 us -> 1.19 us  [on_device(): lax.ppermute(grad_other, 'core', swap)]
    pallas_call x1, Pallas kernels: 10.5 us -> 5.64 us  [on_device(): pl.pallas_call(atom_kernel, out_shape=jax.ShapeDtypeStruct((H, copies * t...]
    all_to_all x1, waiting for transfers between devices: 5.53 us -> 0.8 us  [on_device(): packed = lax.all_to_all(packed, PLANE, 0, 0, tiled=True)]
    all_to_all x1, starting transfers between devices: 6.65 us -> 11.3 us  [on_device(): packed = lax.all_to_all(packed, PLANE, 0, 0, tiled=True)]
    all_to_all x1, waiting for transfers between devices: 0.01 us -> 4.35 us  [on_device(): bias_mine = lax.all_to_all(bias, PLANE, 0, 0, tiled=True)]
  transfers between devices with their start and end apart: 6 -> 13, of which waited for: 2 -> 5; matrix products, arithmetic and copies ran while one was open for 1% -> 0% of each run, Pallas kernels for 20% -> 18%
where the time goes in v3:
time: 120 us
  Pallas kernels  50.1 us (42%)
  starting transfers between devices  37.6 us (31%)
  waiting for transfers between devices  14.1 us (12%)
  blocking collectives  13.8 us (12%)
  local copies, waits for them, and re-layouts  3.41 us (3%)
    pallas_call x3, Pallas kernels, pair_call(): pl.pallas_call(kernel, grid=(1,), out_shape=(jax.ShapeDtypeStruct(pair_re...  21.7 us
    all_to_all x1, blocking collectives, on_device(): merged = lax.all_to_all(merged, PLANE, 0, 0, tiled=True)  13.8 us
    all_to_all x1, starting transfers between devices, on_device(): packed = lax.all_to_all(packed, PLANE, 0, 0, tiled=True)  11.3 us
    pallas_call x1, Pallas kernels, on_device(): pl.pallas_call(grad_kernel, grid=(steps,), out_shape=(jax.ShapeDtypeStruc...  9.39 us
    pallas_call x1, Pallas kernels, on_device(): pl.pallas_call(attend_kernel, out_shape=(jax.ShapeDtypeStruct((H, tok_row...  8.82 us
    all_to_all x1, starting transfers between devices, on_device(): bias_mine = lax.all_to_all(bias, PLANE, 0, 0, tiled=True)  5.84 us
    pallas_call x1, Pallas kernels, on_device(): pl.pallas_call(atom_kernel, out_shape=jax.ShapeDtypeStruct((H, copies * t...  5.64 us
    ppermute x1, waiting for transfers between devices, on_device(): falling.append(lax.ppermute(falling[2], 'z', behind))  5.07 us
  transfers between devices with their start and end apart: 13, of which 5 were waited for; matrix products, arithmetic and copies ran while one was open for 0% of the time, Pallas kernels for 18%

profile of v3, /device:TPU:1, one launch (start us, length us, event | category | flops | bytes accessed | tf_op | source)
XLA Modules:
  0.0 119.8 jit_solution(2100095059457954703)
XLA Ops:
  0.6 1.3 %copy.21.coords = f32[2,3,192]{2,1,0:T(4,128)} copy(f32[2,3,192]{2,0,1:T(2,128)} %param.20) | data formatting | bytes 9216 | tf_op args[3]
  1.9 2.1 %atom_start.1 = (f32[2,192,128]{2,1,0:T(8,128)}, bf16[2,192,128]{2,1,0:T(8,128)(2,1)}, bf16[2,64,128]{2,1,0:T(8,128)(2,1)}, bf16[2,64,128]{2,1,0:T(8,128)(2,1)}) custom-call(s32[2]{0:T(128)} %levels.3, bf16[192,128]{1,0:T(8,128)(2,1)} %feat.1, f32[2,3,192]{2,1,0:T(4,128)} %copy.21.coords, f32[3,128]{1,0:T(4,128)} %coord_weight.1), custom_call_target="tpu_custom_call" | custom-call | flops 1000000 | bytes 500000 | tf_op jit(solution)/shard_map/atom_start/pallas_call | solution.py:530
  4.0 1.3 %collective-permute-start.1 = (bf16[2,64,128]{2,1,0:T(8,128)(2,1)}, bf16[2,64,128]{2,1,0:T(8,128)(2,1)S(1)}, u32[]{:S(2)}, u32[]{:S(2)}) collective-permute-start(bf16[2,64,128]{2,1,0:T(8,128)(2,1)} %get-tuple-element.25), channel_id=1, source_target_pairs={{4,0},{8,4},{12,8},{16,12},{20,16},{24,20},{28,24},{32,28},{36,32}... | collective-permute-start | bytes 98312 | tf_op jit(solution)/shard_map/ppermute | solution.py:547
  5.3 4.6 %collective-permute-start = (bf16[2,64,128]{2,1,0:T(8,128)(2,1)}, bf16[2,64,128]{2,1,0:T(8,128)(2,1)S(1)}, u32[]{:S(2)}, u32[]{:S(2)}) collective-permute-start(bf16[2,64,128]{2,1,0:T(8,128)(2,1)} %get-tuple-element.24.anchor), channel_id=1, source_target_pairs={{0,4},{4,8},{8,12},{12,16},{16,20},{20,24},{24,28},{28,32},{32,36}... | collective-permute-start | bytes 98312 | tf_op jit(solution)/shard_map/ppermute | solution.py:546
  9.9 7.2 %pair_part.3 = (bf16[24,384,128]{2,1,0:T(8,128)(2,1)}, f32[16,8,384]{2,1,0:T(8,128)}) custom-call(bf16[24,384,128]{2,1,0:T(8,128)(2,1)} %pair.5, bf16[128,1024]{1,0:T(8,128)(2,1)} %trans_in.5, bf16[512,128]{1,0:T(8,128)(2,1)} %trans_out.5, bf16[16,128]{1,0:T(8,128)(2,1)} %bitcast.5, bf16[2,64,128]{2,1,0:T(8,128)(2,1)} %get-tuple-element.24.anchor), custom_call_target="tpu_custom_call" | custom-call | flops 6000000000 | bytes 8000000 | tf_op jit(solution)/shard_map/pair_part/pallas_call | solution.py:319
  17.1 0.0 collective-permute-done.1.high
  17.1 0.0 collective-permute-done.low
  17.1 0.0 copy-start.13
  17.1 0.6 copy-done.12
  17.7 0.0 copy-done.13
  17.7 5.6 %atom_stage.1.anchor = s16[16,48,256]{2,1,0:T(8,128)(2,1)} custom-call(s32[1]{0:T(128)} %bitcast.3.place, s32[6]{0:T(128)} %offsets.1, s32[2]{0:T(128)} %levels.3, bf16[2,64,128]{2,1,0:T(8,128)(2,1)} %copy-done.13, bf16[2,64,128]{2,1,0:T(8,128)(2,1)} %copy-done.12, bf16[2,192,128]{2,1,0:T(8,128)(2,1)} %get-tuple-element.29.normed, ...), custom_call_target="tpu_custom_call" | custom-call | flops 3000000000 | bytes 6000000 | tf_op jit(solution)/shard_map/atom_stage/pallas_call | solution.py:554
  23.3 11.3 %all-to-all-start = ((s16[16,48,256]{2,1,0:T(8,128)(2,1)}), s16[16,48,256]{2,1,0:T(8,128)(2,1)S(1)}, u32[]{:S(2)}, u32[]{:S(2)}) async-start(s16[16,48,256]{2,1,0:T(8,128)(2,1)} %atom_stage.1.anchor), calls=%async_computation | async-start | bytes 786432 | tf_op jit(solution)/shard_map/all_to_all | solution.py:570
  34.6 7.2 %pair_part.4 = (bf16[24,384,128]{2,1,0:T(8,128)(2,1)}, f32[16,8,384]{2,1,0:T(8,128)}) custom-call(bf16[24,384,128]{2,1,0:T(8,128)(2,1)} %pair.5, bf16[128,1024]{1,0:T(8,128)(2,1)} %trans_in.5, bf16[512,128]{1,0:T(8,128)(2,1)} %trans_out.5, bf16[16,128]{1,0:T(8,128)(2,1)} %bitcast.6, ...), custom_call_target="tpu_custom_call", output_to_operand_aliasing={{0}: (5, {})} | custom-call | flops 6000000000 | bytes 8000000 | tf_op jit(solution)/shard_map/pair_part/pallas_call | solution.py:319
  41.8 0.8 all-to-all-done.queries
  42.6 0.0 copy-start.3
  42.7 3.1 %collective-permute-start.3 = (s16[16,48,128]{2,1,0:T(8,128)(2,1)S(1)}, s16[16,48,128]{2,1,0:T(8,128)(2,1)S(1)}, u32[]{:S(2)}, u32[]{:S(2)}) collective-permute-start(s16[16,48,128]{2,1,0:T(8,128)(2,1)S(1)} %slice.3.anchor.kv0), channel_id=1, source_target_pairs={{0,224},{32,0},{64,32},{96,64},{128,96},{160,128},{192,160},{224,1... | collective-permute-start | bytes 589832 | tf_op jit(solution)/shard_map/ppermute | solution.py:576
  45.8 0.0 collective-permute-start.2
  45.8 0.0 copy-done.3
  45.8 7.3 %pair_part.5 = (bf16[24,384,128]{2,1,0:T(8,128)(2,1)}, s16[16,24,384]{2,1,0:T(8,128)(2,1)}) custom-call(bf16[24,384,128]{2,1,0:T(8,128)(2,1)} %pair.5, bf16[128,1024]{1,0:T(8,128)(2,1)} %trans_in.5, bf16[512,128]{1,0:T(8,128)(2,1)} %trans_out.5, bf16[16,128]{1,0:T(8,128)(2,1)} %bitcast.7, ...), custom_call_target="tpu_custom_call", output_to_operand_aliasing={{0}: (5, {})} | custom-call | flops 6000000000 | bytes 8000000 | tf_op jit(solution)/shard_map/pair_part/pallas_call | solution.py:319
  53.1 0.0 copy-done
  53.1 0.0 collective-permute-done.3.kv7
  53.2 0.0 copy-start.5
  53.2 0.0 collective-permute-done.2.kv1
  53.2 0.0 copy-start.6
  53.2 0.4 collective-permute-start.4
  53.6 5.8 %all-to-all-start.1 = ((s16[16,24,384]{2,1,0:T(8,128)(2,1)}), s16[16,24,384]{2,1,0:T(8,128)(2,1)S(1)}, u32[]{:S(2)}, u32[]{:S(2)}) async-start(s16[16,24,384]{2,1,0:T(8,128)(2,1)} %get-tuple-element.40), calls=%async_computation.1 | async-start | bytes 589824 | tf_op jit(solution)/shard_map/all_to_all | solution.py:589
  59.4 3.3 %collective-permute-start.7 = (s16[16,48,128]{2,1,0:T(8,128)(2,1)S(1)}, s16[16,48,128]{2,1,0:T(8,128)(2,1)S(1)}, u32[]{:S(2)}, u32[]{:S(2)}) collective-permute-start(s16[16,48,128]{2,1,0:T(8,128)(2,1)S(1)} %collective-permute-done.3.kv7), channel_id=1, source_target_pairs={{0,224},{32,0},{64,32},{96,64},{128,96},{160,128},{192,160},{224,1... | collective-permute-start | bytes 589832 | tf_op jit(solution)/shard_map/ppermute | solution.py:583
  62.7 0.0 collective-permute-done.4.kv2
  62.7 0.0 collective-permute-start.5
  62.7 4.4 %all-to-all-done.1.bias_mine = s16[16,24,384]{2,1,0:T(8,128)(2,1)S(1)} async-done(((s16[16,24,384]{2,1,0:T(8,128)(2,1)}), s16[16,24,384]{2,1,0:T(8,128)(2,1)S(1)}, u32[]{:S(2)}, u32[]{:S(2)}) %all-to-all-start.1) | async-done | bytes 294944 | tf_op jit(solution)/shard_map/all_to_all | solution.py:589
  67.1 3.7 %collective-permute-start.9 = (s16[16,24,384]{2,1,0:T(8,128)(2,1)S(1)}, s16[16,24,384]{2,1,0:T(8,128)(2,1)S(1)}, u32[]{:S(2)}, u32[]{:S(2)}) collective-permute-start(s16[16,24,384]{2,1,0:T(8,128)(2,1)S(1)} %all-to-all-done.1.bias_mine), channel_id=1, source_target_pairs={{0,1},{1,0},{2,3},{3,2},{4,5},{5,4},{6,7},{7,6},{8,9},{9,8},{10,11... | collective-permute-start | bytes 884744 | tf_op jit(solution)/shard_map/ppermute | solution.py:591
  70.7 0.0 collective-permute-done.7.kv6
  70.8 2.7 %collective-permute-start.8 = (s16[16,48,128]{2,1,0:T(8,128)(2,1)S(1)}, s16[16,48,128]{2,1,0:T(8,128)(2,1)S(1)}, u32[]{:S(2)}, u32[]{:S(2)}) collective-permute-start(s16[16,48,128]{2,1,0:T(8,128)(2,1)S(1)} %collective-permute-done.7.kv6), channel_id=1, source_target_pairs={{0,224},{32,0},{64,32},{96,64},{128,96},{160,128},{192,160},{224,1... | collective-permute-start | bytes 589832 | tf_op jit(solution)/shard_map/ppermute | solution.py:585
  73.4 0.0 collective-permute-done.5.kv3
  73.4 0.3 collective-permute-start.6
  73.7 5.1 %collective-permute-done.8.kv5 = s16[16,48,128]{2,1,0:T(8,128)(2,1)S(1)} collective-permute-done((s16[16,48,128]{2,1,0:T(8,128)(2,1)S(1)}, s16[16,48,128]{2,1,0:T(8,128)(2,1)S(1)}, u32[]{:S(2)}, u32[]{:S(2)}) %collective-permute-start.8) | collective-permute-done | bytes 196640 | tf_op jit(solution)/shard_map/ppermute | solution.py:585
  78.8 0.0 collective-permute-done.9.bias_other
  78.8 2.0 %collective-permute-done.6.kv4 = s16[16,48,128]{2,1,0:T(8,128)(2,1)S(1)} collective-permute-done((s16[16,48,128]{2,1,0:T(8,128)(2,1)S(1)}, s16[16,48,128]{2,1,0:T(8,128)(2,1)S(1)}, u32[]{:S(2)}, u32[]{:S(2)}) %collective-permute-start.6) | collective-permute-done | bytes 196640 | tf_op jit(solution)/shard_map/ppermute | solution.py:586
  80.8 0.0 copy-done.5
  80.8 0.0 copy-done.6
  80.8 0.6 copy-done.11
  81.5 8.8 %token_attention.1 = (f32[16,24,512]{2,1,0:T(8,128)}, f32[16,24,384]{2,1,0:T(8,128)}) custom-call(s32[1]{0:T(128)} %bitcast.core_at, s32[1]{0:T(128)} %bitcast.1.head_at, s32[1]{0:T(128)} %bitcast.2.z_at, s16[16,48,256]{2,1,0:T(8,128)(2,1)} %copy-done, s16[16,48,128]{2,1,0:T(8,128)(2,1)} %copy-done.3, s16[16,48,128]{2,1,0:T(8,128)(2,1)} %copy-done.6, ...), custom_call_target="tpu_custom_call" | custom-call | flops 4000000000 | bytes 8000000 | tf_op jit(solution)/shard_map/token_attention/pallas_call | solution.py:595
  90.3 1.2 collective-permute-start.10
  91.5 1.8 %collective-permute-done.10.other = f32[16,24,384]{2,1,0:T(8,128)S(1)} collective-permute-done((f32[16,24,384]{2,1,0:T(8,128)}, f32[16,24,384]{2,1,0:T(8,128)S(1)}, u32[]{:S(2)}, u32[]{:S(2)}) %collective-permute-start.10) | collective-permute-done | bytes 589856 | tf_op jit(solution)/shard_map/ppermute | solution.py:618
  93.3 0.8 copy-done.1
  94.1 2.4 %gradient_merge.1 = s16[16,48,256]{2,1,0:T(8,128)(2,1)} custom-call(f32[16,24,512]{2,1,0:T(8,128)} %get-tuple-element.41.mine, f32[16,24,384]{2,1,0:T(8,128)} %copy-done.1), custom_call_target="tpu_custom_call" | custom-call | flops 2000000 | bytes 2000000 | tf_op jit(solution)/shard_map/gradient_merge/pallas_call | solution.py:610
  96.6 13.8 %all_to_all.15.packed = s16[16,48,256]{2,1,0:T(8,128)(2,1)} all-to-all(s16[16,48,256]{2,1,0:T(8,128)(2,1)} %gradient_merge.1), channel_id=1, replica_groups=mesh['z'=8,'g'=8,'ylo'=2,'core'=2] {'g','ylo'}, dimensions={0} | all-to-all | bytes 786432 | tf_op jit(solution)/shard_map/all_to_all | solution.py:619
  110.4 9.4 %pair_gradient.1 = (bf16[24,384,128]{2,1,0:T(8,128)(2,1)}, bf16[2,24,768]{2,1,0:T(8,128)(2,1)}) custom-call(s16[16,48,256]{2,1,0:T(8,128)(2,1)} %all_to_all.15.packed, bf16[24,384,128]{2,1,0:T(8,128)(2,1)} %get-tuple-element.43.cond, bf16[16,128]{1,0:T(8,128)(2,1)} %bitcast.9), custom_call_target="tpu_custom_call" | custom-call | flops 400000000 | bytes 6000000 | tf_op jit(solution)/shard_map/pair_gradient/pallas_call | solution.py:620
  (17 shorter events, 0.1 us)
Async XLA Ops:
  4.0 13.0 %collective-permute-start.1 = (bf16[2,64,128]{2,1,0:T(8,128)(2,1)}, bf16[2,64,128]{2,1,0:T(8,128)(2,1)S(1)}, u32[]{:S(2)}, u32[]{:S(2)}) collective-permute-start(bf16[2,64,128]{2,1,0:T(8,128)(2,1)} %get-tuple-element.25), channel_id=1, source_target_pairs={{4,0},{8,4},{12,8},{16,12},{20,16},{24,20},{28,24},{32,28},{36,32}... | collective-permute-start | bytes 98312 | tf_op jit(solution)/shard_map/ppermute | solution.py:547
  5.3 11.8 %collective-permute-start = (bf16[2,64,128]{2,1,0:T(8,128)(2,1)}, bf16[2,64,128]{2,1,0:T(8,128)(2,1)S(1)}, u32[]{:S(2)}, u32[]{:S(2)}) collective-permute-start(bf16[2,64,128]{2,1,0:T(8,128)(2,1)} %get-tuple-element.24.anchor), channel_id=1, source_target_pairs={{0,4},{4,8},{8,12},{12,16},{16,20},{20,24},{24,28},{28,32},{32,36}... | collective-permute-start | bytes 98312 | tf_op jit(solution)/shard_map/ppermute | solution.py:546
  17.1 0.6 copy-start.12
  17.1 0.6 copy-start.13
  23.3 19.3 %all-to-all-start = ((s16[16,48,256]{2,1,0:T(8,128)(2,1)}), s16[16,48,256]{2,1,0:T(8,128)(2,1)S(1)}, u32[]{:S(2)}, u32[]{:S(2)}) async-start(s16[16,48,256]{2,1,0:T(8,128)(2,1)} %atom_stage.1.anchor), calls=%async_computation | async-start | bytes 786432 | tf_op jit(solution)/shard_map/all_to_all | solution.py:570
  42.6 10.5 %copy-start = (s16[16,48,256]{2,1,0:T(8,128)(2,1)}, s16[16,48,256]{2,1,0:T(8,128)(2,1)S(1)}, u32[]{:S(2)}) copy-start(s16[16,48,256]{2,1,0:T(8,128)(2,1)S(1)} %all-to-all-done.queries) | copy-start | bytes 1179652
  42.6 3.2 %copy-start.3 = (s16[16,48,128]{2,1,0:T(8,128)(2,1)}, s16[16,48,128]{2,1,0:T(8,128)(2,1)S(1)}, u32[]{:S(2)}) copy-start(s16[16,48,128]{2,1,0:T(8,128)(2,1)S(1)} %slice.3.anchor.kv0) | copy-start | bytes 589828
  42.7 10.5 %collective-permute-start.3 = (s16[16,48,128]{2,1,0:T(8,128)(2,1)S(1)}, s16[16,48,128]{2,1,0:T(8,128)(2,1)S(1)}, u32[]{:S(2)}, u32[]{:S(2)}) collective-permute-start(s16[16,48,128]{2,1,0:T(8,128)(2,1)S(1)} %slice.3.anchor.kv0), channel_id=1, source_target_pairs={{0,224},{32,0},{64,32},{96,64},{128,96},{160,128},{192,160},{224,1... | collective-permute-start | bytes 589832 | tf_op jit(solution)/shard_map/ppermute | solution.py:576
  45.8 7.4 %collective-permute-start.2 = (s16[16,48,128]{2,1,0:T(8,128)(2,1)S(1)}, s16[16,48,128]{2,1,0:T(8,128)(2,1)S(1)}, u32[]{:S(2)}, u32[]{:S(2)}) collective-permute-start(s16[16,48,128]{2,1,0:T(8,128)(2,1)S(1)} %slice.3.anchor.kv0), channel_id=1, source_target_pairs={{0,32},{32,64},{64,96},{96,128},{128,160},{160,192},{192,224},{224... | collective-permute-start | bytes 589832 | tf_op jit(solution)/shard_map/ppermute | solution.py:575
  53.2 27.6 %copy-start.5 = (s16[16,48,128]{2,1,0:T(8,128)(2,1)}, s16[16,48,128]{2,1,0:T(8,128)(2,1)S(1)}, u32[]{:S(2)}) copy-start(s16[16,48,128]{2,1,0:T(8,128)(2,1)S(1)} %collective-permute-done.3.kv7) | copy-start | bytes 589828
  53.2 27.6 %copy-start.6 = (s16[16,48,128]{2,1,0:T(8,128)(2,1)}, s16[16,48,128]{2,1,0:T(8,128)(2,1)S(1)}, u32[]{:S(2)}) copy-start(s16[16,48,128]{2,1,0:T(8,128)(2,1)S(1)} %collective-permute-done.2.kv1) | copy-start | bytes 589828
  53.2 9.5 %collective-permute-start.4 = (s16[16,48,128]{2,1,0:T(8,128)(2,1)S(1)}, s16[16,48,128]{2,1,0:T(8,128)(2,1)S(1)}, u32[]{:S(2)}, u32[]{:S(2)}) collective-permute-start(s16[16,48,128]{2,1,0:T(8,128)(2,1)S(1)} %collective-permute-done.2.kv1), channel_id=1, source_target_pairs={{0,32},{32,64},{64,96},{96,128},{128,160},{160,192},{192,224},{224... | collective-permute-start | bytes 589832 | tf_op jit(solution)/shard_map/ppermute | solution.py:582
  53.6 13.5 %all-to-all-start.1 = ((s16[16,24,384]{2,1,0:T(8,128)(2,1)}), s16[16,24,384]{2,1,0:T(8,128)(2,1)S(1)}, u32[]{:S(2)}, u32[]{:S(2)}) async-start(s16[16,24,384]{2,1,0:T(8,128)(2,1)} %get-tuple-element.40), calls=%async_computation.1 | async-start | bytes 589824 | tf_op jit(solution)/shard_map/all_to_all | solution.py:589
  59.4 11.3 %collective-permute-start.7 = (s16[16,48,128]{2,1,0:T(8,128)(2,1)S(1)}, s16[16,48,128]{2,1,0:T(8,128)(2,1)S(1)}, u32[]{:S(2)}, u32[]{:S(2)}) collective-permute-start(s16[16,48,128]{2,1,0:T(8,128)(2,1)S(1)} %collective-permute-done.3.kv7), channel_id=1, source_target_pairs={{0,224},{32,0},{64,32},{96,64},{128,96},{160,128},{192,160},{224,1... | collective-permute-start | bytes 589832 | tf_op jit(solution)/shard_map/ppermute | solution.py:583
  62.7 18.1 %copy-start.7 = (s16[16,48,128]{2,1,0:T(8,128)(2,1)}, s16[16,48,128]{2,1,0:T(8,128)(2,1)S(1)}, u32[]{:S(2)}) copy-start(s16[16,48,128]{2,1,0:T(8,128)(2,1)S(1)} %collective-permute-done.4.kv2) | copy-start | bytes 589828
  62.7 10.7 %collective-permute-start.5 = (s16[16,48,128]{2,1,0:T(8,128)(2,1)S(1)}, s16[16,48,128]{2,1,0:T(8,128)(2,1)S(1)}, u32[]{:S(2)}, u32[]{:S(2)}) collective-permute-start(s16[16,48,128]{2,1,0:T(8,128)(2,1)S(1)} %collective-permute-done.4.kv2), channel_id=1, source_target_pairs={{0,32},{32,64},{64,96},{96,128},{128,160},{160,192},{192,224},{224... | collective-permute-start | bytes 589832 | tf_op jit(solution)/shard_map/ppermute | solution.py:584
  67.1 13.7 %copy-start.2 = (s16[16,24,384]{2,1,0:T(8,128)(2,1)}, s16[16,24,384]{2,1,0:T(8,128)(2,1)S(1)}, u32[]{:S(2)}) copy-start(s16[16,24,384]{2,1,0:T(8,128)(2,1)S(1)} %all-to-all-done.1.bias_mine) | copy-start | bytes 884740
  67.1 11.7 %collective-permute-start.9 = (s16[16,24,384]{2,1,0:T(8,128)(2,1)S(1)}, s16[16,24,384]{2,1,0:T(8,128)(2,1)S(1)}, u32[]{:S(2)}, u32[]{:S(2)}) collective-permute-start(s16[16,24,384]{2,1,0:T(8,128)(2,1)S(1)} %all-to-all-done.1.bias_mine), channel_id=1, source_target_pairs={{0,1},{1,0},{2,3},{3,2},{4,5},{5,4},{6,7},{7,6},{8,9},{9,8},{10,11... | collective-permute-start | bytes 884744 | tf_op jit(solution)/shard_map/ppermute | solution.py:591
  70.8 10.1 %copy-start.8 = (s16[16,48,128]{2,1,0:T(8,128)(2,1)}, s16[16,48,128]{2,1,0:T(8,128)(2,1)S(1)}, u32[]{:S(2)}) copy-start(s16[16,48,128]{2,1,0:T(8,128)(2,1)S(1)} %collective-permute-done.7.kv6) | copy-start | bytes 589828
  70.8 8.0 %collective-permute-start.8 = (s16[16,48,128]{2,1,0:T(8,128)(2,1)S(1)}, s16[16,48,128]{2,1,0:T(8,128)(2,1)S(1)}, u32[]{:S(2)}, u32[]{:S(2)}) collective-permute-start(s16[16,48,128]{2,1,0:T(8,128)(2,1)S(1)} %collective-permute-done.7.kv6), channel_id=1, source_target_pairs={{0,224},{32,0},{64,32},{96,64},{128,96},{160,128},{192,160},{224,1... | collective-permute-start | bytes 589832 | tf_op jit(solution)/shard_map/ppermute | solution.py:585
  73.4 7.4 %copy-start.9 = (s16[16,48,128]{2,1,0:T(8,128)(2,1)}, s16[16,48,128]{2,1,0:T(8,128)(2,1)S(1)}, u32[]{:S(2)}) copy-start(s16[16,48,128]{2,1,0:T(8,128)(2,1)S(1)} %collective-permute-done.5.kv3) | copy-start | bytes 589828
  73.4 7.3 %collective-permute-start.6 = (s16[16,48,128]{2,1,0:T(8,128)(2,1)S(1)}, s16[16,48,128]{2,1,0:T(8,128)(2,1)S(1)}, u32[]{:S(2)}, u32[]{:S(2)}) collective-permute-start(s16[16,48,128]{2,1,0:T(8,128)(2,1)S(1)} %collective-permute-done.5.kv3), channel_id=1, source_target_pairs={{0,32},{32,64},{64,96},{96,128},{128,160},{160,192},{192,224},{224... | collective-permute-start | bytes 589832 | tf_op jit(solution)/shard_map/ppermute | solution.py:586
  78.8 2.1 %copy-start.10 = (s16[16,48,128]{2,1,0:T(8,128)(2,1)}, s16[16,48,128]{2,1,0:T(8,128)(2,1)S(1)}, u32[]{:S(2)}) copy-start(s16[16,48,128]{2,1,0:T(8,128)(2,1)S(1)} %collective-permute-done.8.kv5) | copy-start | bytes 589828
  78.8 2.1 %copy-start.4 = (s16[16,24,384]{2,1,0:T(8,128)(2,1)}, s16[16,24,384]{2,1,0:T(8,128)(2,1)S(1)}, u32[]{:S(2)}) copy-start(s16[16,24,384]{2,1,0:T(8,128)(2,1)S(1)} %collective-permute-done.9.bias_other) | copy-start | bytes 884740
  80.8 0.7 copy-start.11
  90.3 3.0 %collective-permute-start.10 = (f32[16,24,384]{2,1,0:T(8,128)}, f32[16,24,384]{2,1,0:T(8,128)S(1)}, u32[]{:S(2)}, u32[]{:S(2)}) collective-permute-start(f32[16,24,384]{2,1,0:T(8,128)} %get-tuple-element.42), channel_id=1, source_target_pairs={{0,1},{1,0},{2,3},{3,2},{4,5},{5,4},{6,7},{7,6},{8,9},{9,8},{10,11... | collective-permute-start | bytes 1769480 | tf_op jit(solution)/shard_map/ppermute | solution.py:618
  93.3 0.8 copy-start.1

commit v4 on v3

--- a/solution.py
+++ b/solution.py
@@ -253,7 +253,7 @@
         normal = (centred * lax.rsqrt(lane_mean(centred * centred, ones) + epsilon)).astype(BF)
         return jnp.concatenate([normal[:, :lanes], normal[:, lanes:]], axis=0)
 
-    group = 4
+    group = 2
     chunk = 128
     weights = [
         jnp.concatenate(
@@ -265,21 +265,39 @@
         )
         for f in range(0, inner, chunk)
     ]
-    for part in range(pair.shape[0] // group):
-        value = pair[part * group : (part + 1) * group].reshape(group * cols, lanes)
-        normed = normalise(value)
-        delta = value.astype(F32)
-        hidden = []
-        for weight in weights:
-            both = dot(normed, weight)
+    count = pair.shape[0] // group
+    normed, hidden, cond = {}, {}, {}
+
+    def value_of(k):
+        return pair[k * group : (k + 1) * group].reshape(group * cols, lanes)
+
+    def gate(k, f):
+        if 0 <= k < count:
+            both = dot(normed[k], weights[f])
             half = both[:, :chunk]
-            hidden.append(((half + half * jnp.tanh(half)) * both[:, chunk:]).astype(BF))
-        delta = delta + dot(jnp.concatenate(hidden, axis=1), trans_out[...])
-        cond = delta.astype(BF)
-        cond_out[part * group : (part + 1) * group] = cond.reshape(group, cols, lanes)
-        bias = dot(bias_weight_t[...], normalise(cond), NT) * (1.0 / unit)
-        for i in range(group):
-            store(part * group + i, bias[:, i * cols : (i + 1) * cols])
+            hidden[k, f] = ((half + half * jnp.tanh(half)) * both[:, chunk:]).astype(BF)
+
+    def down(k):
+        if 0 <= k < count:
+            joined = jnp.concatenate([hidden[k, f] for f in range(len(weights))], axis=1)
+            cond[k] = (value_of(k).astype(F32) + dot(joined, trans_out[...])).astype(BF)
+            cond_out[k * group : (k + 1) * group] = cond[k].reshape(group, cols, lanes)
+
+    def project(k):
+        if 0 <= k < count:
+            bias = dot(bias_weight_t[...], normalise(cond[k]), NT) * (1.0 / unit)
+            for i in range(group):
+                store(k * group + i, bias[:, i * cols : (i + 1) * cols])
+
+    for t in range(count + 3):
+        gate(t - 1, 0)
+        project(t - 3)
+        gate(t - 1, 1)
+        down(t - 2)
+        gate(t - 1, 2)
+        if t < count:
+            normed[t] = normalise(value_of(t))
+        gate(t - 1, 3)
 
 
 def pair_first_kernel(pair, trans_in, trans_out, bias_weight_t, anchor, cond_out, bias_out):
@@ -294,20 +312,21 @@
 
 
 def pair_last_kernel(
-    pair, trans_in, trans_out, bias_weight_t, anchor, cond, first, second, cond_out, bias_out, held
+    pair, trans_in, trans_out, bias_weight_t, anchor, cond, first, second, third, cond_out, bias_out,
+    held
 ):
     def store(i, value):
         held[:, i, :] = value
 
     pair_block(pair, trans_in, trans_out, bias_weight_t, cond_out, store)
     for h in range(bias_out.shape[0]):
-        parts = [first[h], second[h], held[h]]
+        parts = [first[h], second[h], third[h], held[h]]
         bias_out[h] = whole(jnp.concatenate(parts, axis=0)).astype(jnp.int16)
 
 
-def pair_call(kernel, index, inputs, extra, anchor, cond, bias_shape, scratch=()):
+def pair_call(kernel, step, index, inputs, extra, anchor, cond, bias_shape, scratch=()):
     pair_rep, trans_in, trans_out, bias_t = inputs
-    step, cols = 8, pair_rep.shape[1]
+    cols = pair_rep.shape[1]
     block = pl.BlockSpec((step, cols, 128), lambda i: (index, 0, 0))
     operands = [pair_rep, trans_in, trans_out, bias_t, anchor]
     if cond is not None:
@@ -326,7 +345,7 @@
         input_output_aliases={} if cond is None else {5: 0},
         compiler_params=params(),
         cost_estimate=pl.CostEstimate(
-            flops=6_000_000_000, bytes_accessed=8_000_000, transcendentals=0
+            flops=step * 750_000_000, bytes_accessed=step * 1_000_000, transcendentals=0
         ),
         name="pair_part",
     )(*operands, *extra)
@@ -371,45 +390,57 @@
         ],
         axis=0,
     ) * unit
+    def products_of(y, p, query_blocks, token_blocks):
+        query = jnp.concatenate([b[p * tok : (p + 1) * tok] for b in query_blocks], axis=0)
+        q_high, q_low = two_parts(jnp.where(is_key, query, 0.0))
+        c_high, c_low = two_parts(jnp.where(is_value, query, 0.0))
+        high, low = two_parts(
+            jnp.concatenate([b[p * tok : (p + 1) * tok] for b in token_blocks], axis=0)
+        )
+        both = jnp.concatenate([high, low], axis=1)
+        none = jnp.zeros_like(q_low)
+        stacked = jnp.concatenate(
+            [
+                jnp.concatenate([q_high, q_high], axis=1),
+                jnp.concatenate([q_low, none], axis=1),
+                jnp.concatenate([c_high, c_high], axis=1),
+                jnp.concatenate([c_low, none], axis=1),
+            ],
+            axis=0,
+        )
+        return both, dot(stacked, both, NT)
+
+    def products_at(index):
+        y, p = index // 2, index % 2
+        if p == 0:
+            blocks_of[y] = (
+                [decode(queries[2 * g + y, :, :128]) for g in range(8)],
+                [decode(kv[2 * c + z, 2 * g + y]) for c in blocks for z in range(2) for g in range(8)],
+            )
+        return products_of(y, p, *blocks_of[y])
+
+    blocks_of = {}
     grad = None
-    for y in range(2):
-        query_blocks = [decode(queries[2 * g + y, :, :128]) for g in range(8)]
-        token_blocks = [
-            decode(kv[2 * c + z, 2 * g + y]) for c in blocks for z in range(2) for g in range(8)
-        ]
-        for p in range(2):
-            query = jnp.concatenate([b[p * tok : (p + 1) * tok] for b in query_blocks], axis=0)
-            q_high, q_low = two_parts(jnp.where(is_key, query, 0.0))
-            c_high, c_low = two_parts(jnp.where(is_value, query, 0.0))
-            high, low = two_parts(
-                jnp.concatenate([b[p * tok : (p + 1) * tok] for b in token_blocks], axis=0)
-            )
-            both = jnp.concatenate([high, low], axis=1)
-            none = jnp.zeros_like(q_low)
-            stacked = jnp.concatenate(
-                [
-                    jnp.concatenate([q_high, q_high], axis=1),
-                    jnp.concatenate([q_low, none], axis=1),
-                    jnp.concatenate([c_high, c_high], axis=1),
-                    jnp.concatenate([c_low, none], axis=1),
-                ],
-                axis=0,
-            )
-            products = dot(stacked, both, NT)
-            scores = products[:rows] + products[rows : 2 * rows] + bias
-            prob_grad = products[2 * rows : 3 * rows] + products[3 * rows :]
-            top = jnp.max(scores, axis=-1, keepdims=True)
-            weights = jnp.exp(scores - top)
-            weights = weights * (1.0 / jnp.sum(weights, axis=-1, keepdims=True))
-            mixed = dot(weights.astype(BF), both)
-            mixed = mixed[:, :128] + mixed[:, 128:]
-            for g in range(8):
-                update_mine[2 * g + y, :, cols + p * HEAD : cols + (p + 1) * HEAD] = mixed[
-                    g * tok : (g + 1) * tok, HEAD : 2 * HEAD
-                ]
-            term = weights * prob_grad
-            term = term - weights * jnp.sum(term, axis=-1, keepdims=True)
-            grad = term if grad is None else grad + term
+    coming = products_at(0)
+    for index in range(4):
+        y, p = index // 2, index % 2
+        both, products = coming
+        if index < 3:
+            coming = products_at(index + 1)
+        scores = products[:rows] + products[rows : 2 * rows] + bias
+        prob_grad = products[2 * rows : 3 * rows] + products[3 * rows :]
+        top = jnp.max(scores, axis=-1, keepdims=True)
+        weights = jnp.exp(scores - top)
+        weights = weights * (1.0 / jnp.sum(weights, axis=-1, keepdims=True))
+        mixed = dot(weights.astype(BF), both)
+        mixed = mixed[:, :128] + mixed[:, 128:]
+        for g in range(8):
+            update_mine[2 * g + y, :, cols + p * HEAD : cols + (p + 1) * HEAD] = mixed[
+                g * tok : (g + 1) * tok, HEAD : 2 * HEAD
+            ]
+        term = weights * prob_grad
+        term = term - weights * jnp.sum(term, axis=-1, keepdims=True)
+        grad = term if grad is None else grad + term
     for g in range(8):
         for c in range(4):
             (update_mine if c < 2 else grad_other)[2 * g + c % 2, :, :cols] = grad[
@@ -549,7 +580,7 @@
     inputs = (pair_rep, trans_in, trans_out, bias_t)
     step = 8
     part_bias = jax.ShapeDtypeStruct((H, step, cols), F32)
-    cond, bias_first = pair_call(pair_first_kernel, 0, inputs, [], last, None, part_bias)
+    cond, bias_first = pair_call(pair_first_kernel, step, 0, inputs, [], last, None, part_bias)
     low, high, bias_first = lax.optimization_barrier((low, high, bias_first))
     packed = pl.pallas_call(
         atom_kernel,
@@ -565,7 +596,7 @@
         atom_token, single, single_weight, noise_weight, token_weight, cotangent,
     )
     cond, bias_second = pair_call(
-        pair_next_kernel, 1, inputs, [], packed, cond, part_bias
+        pair_next_kernel, step, 1, inputs, [], packed, cond, part_bias
     )
     packed = lax.all_to_all(packed, PLANE, 0, 0, tiled=True)
     packed, bias_second = lax.optimization_barrier((packed, bias_second))
@@ -574,13 +605,21 @@
     behind = [(i, (i + 7) % 8) for i in range(8)]
     rising = [own, lax.ppermute(own, "z", ahead)]
     falling = [own, lax.ppermute(own, "z", behind)]
-    cond, bias = pair_call(
-        pair_last_kernel, 2, inputs, [bias_first, bias_second], own, cond,
-        jax.ShapeDtypeStruct((H, tok_rows, cols), jnp.int16), [pltpu.VMEM((H, step, cols), F32)],
+    small = step // 2
+    small_bias = jax.ShapeDtypeStruct((H, small, cols), F32)
+    cond, bias_third = pair_call(
+        pair_next_kernel, small, 4, inputs, [], own, cond, small_bias
     )
-    rising[1], falling[1], bias = lax.optimization_barrier((rising[1], falling[1], bias))
+    rising[1], falling[1], bias_third = lax.optimization_barrier(
+        (rising[1], falling[1], bias_third)
+    )
     rising.append(lax.ppermute(rising[1], "z", ahead))
     falling.append(lax.ppermute(falling[1], "z", behind))
+    cond, bias = pair_call(
+        pair_last_kernel, small, 5, inputs, [bias_first, bias_second, bias_third], rising[1], cond,
+        jax.ShapeDtypeStruct((H, tok_rows, cols), jnp.int16), [pltpu.VMEM((H, small, cols), F32)],
+    )
+    rising[2], falling[2], bias = lax.optimization_barrier((rising[2], falling[2], bias))
     rising.append(lax.ppermute(rising[2], "z", ahead))
     falling.append(lax.ppermute(falling[2], "z", behind))
     rising.append(lax.ppermute(rising[3], "z", ahead))

time: 120 us -> 126 us (1.050)
  waiting for transfers between devices: 14.1 us -> 19.4 us
  Pallas kernels: 50.1 us -> 51.9 us
  starting transfers between devices: 37.6 us -> 36.3 us
    all_to_all x1, waiting for transfers between devices: 4.35 us -> 7.43 us  [on_device(): bias_mine = lax.all_to_all(bias, PLANE, 0, 0, tiled=True)]
    pallas_call x3 -> x4, Pallas kernels: 21.7 us -> 24.2 us  [pair_call(): pl.pallas_call(kernel, grid=(1,), out_shape=(jax.ShapeDtypeStruct(pair_re...]
    ppermute x1, starting transfers between devices: 3.7 us -> 5.71 us  [on_device(): bias_other = lax.ppermute(bias_mine, 'core', swap)]
    ppermute x1, waiting for transfers between devices: 0.01 us -> 1.5 us  [on_device(): rising = [own, lax.ppermute(own, 'z', ahead)]]
    ppermute x1, starting transfers between devices: 2.68 us -> 1.21 us  [on_device(): falling.append(lax.ppermute(falling[2], 'z', behind))]
    ppermute x1, starting transfers between devices: 3.27 us -> 1.84 us  [on_device(): falling.append(lax.ppermute(falling[1], 'z', behind))]
  transfers between devices with their start and end apart: 13 -> 13, of which waited for: 5 -> 7; matrix products, arithmetic and copies ran while one was open for 0% -> 0% of each run, Pallas kernels for 18% -> 19%
where the time goes in v4:
time: 126 us
  Pallas kernels  51.9 us (41%)
  starting transfers between devices  36.3 us (29%)
  waiting for transfers between devices  19.4 us (15%)
  blocking collectives  13.8 us (11%)
  local copies, waits for them, and re-layouts  3.53 us (3%)
    pallas_call x4, Pallas kernels, pair_call(): pl.pallas_call(kernel, grid=(1,), out_shape=(jax.ShapeDtypeStruct(pair_re...  24.2 us
    all_to_all x1, blocking collectives, on_device(): merged = lax.all_to_all(merged, PLANE, 0, 0, tiled=True)  13.8 us
    all_to_all x1, starting transfers between devices, on_device(): packed = lax.all_to_all(packed, PLANE, 0, 0, tiled=True)  11.3 us
    pallas_call x1, Pallas kernels, on_device(): pl.pallas_call(grad_kernel, grid=(steps,), out_shape=(jax.ShapeDtypeStruc...  9.39 us
    pallas_call x1, Pallas kernels, on_device(): pl.pallas_call(attend_kernel, out_shape=(jax.ShapeDtypeStruct((H, tok_row...  8.16 us
    all_to_all x1, waiting for transfers between devices, on_device(): bias_mine = lax.all_to_all(bias, PLANE, 0, 0, tiled=True)  7.43 us
    all_to_all x1, starting transfers between devices, on_device(): bias_mine = lax.all_to_all(bias, PLANE, 0, 0, tiled=True)  5.82 us
    ppermute x1, starting transfers between devices, on_device(): bias_other = lax.ppermute(bias_mine, 'core', swap)  5.71 us
  transfers between devices with their start and end apart: 13, of which 7 were waited for; matrix products, arithmetic and copies ran while one was open for 0% of the time, Pallas kernels for 19%

profile of v4, /device:TPU:1, one launch (start us, length us, event | category | flops | bytes accessed | tf_op | source)
XLA Modules:
  0.0 125.7 jit_solution(1437712853370238090)
XLA Ops:
  0.6 1.3 %copy.22.coords = f32[2,3,192]{2,1,0:T(4,128)} copy(f32[2,3,192]{2,0,1:T(2,128)} %param.20) | data formatting | bytes 9216 | tf_op args[3]
  1.9 2.1 %atom_start.1 = (f32[2,192,128]{2,1,0:T(8,128)}, bf16[2,192,128]{2,1,0:T(8,128)(2,1)}, bf16[2,64,128]{2,1,0:T(8,128)(2,1)}, bf16[2,64,128]{2,1,0:T(8,128)(2,1)}) custom-call(s32[2]{0:T(128)} %levels.3, bf16[192,128]{1,0:T(8,128)(2,1)} %feat.1, f32[2,3,192]{2,1,0:T(4,128)} %copy.22.coords, f32[3,128]{1,0:T(4,128)} %coord_weight.1), custom_call_target="tpu_custom_call" | custom-call | flops 1000000 | bytes 500000 | tf_op jit(solution)/shard_map/atom_start/pallas_call | solution.py:561
  4.0 1.3 %collective-permute-start.1 = (bf16[2,64,128]{2,1,0:T(8,128)(2,1)}, bf16[2,64,128]{2,1,0:T(8,128)(2,1)S(1)}, u32[]{:S(2)}, u32[]{:S(2)}) collective-permute-start(bf16[2,64,128]{2,1,0:T(8,128)(2,1)} %get-tuple-element.30), channel_id=1, source_target_pairs={{4,0},{8,4},{12,8},{16,12},{20,16},{24,20},{28,24},{32,28},{36,32}... | collective-permute-start | bytes 98312 | tf_op jit(solution)/shard_map/ppermute | solution.py:578
  5.3 4.6 %collective-permute-start = (bf16[2,64,128]{2,1,0:T(8,128)(2,1)}, bf16[2,64,128]{2,1,0:T(8,128)(2,1)S(1)}, u32[]{:S(2)}, u32[]{:S(2)}) collective-permute-start(bf16[2,64,128]{2,1,0:T(8,128)(2,1)} %get-tuple-element.29.anchor), channel_id=1, source_target_pairs={{0,4},{4,8},{8,12},{12,16},{16,20},{20,24},{24,28},{28,32},{32,36}... | collective-permute-start | bytes 98312 | tf_op jit(solution)/shard_map/ppermute | solution.py:577
  9.9 7.2 %pair_part.4 = (bf16[24,384,128]{2,1,0:T(8,128)(2,1)}, f32[16,8,384]{2,1,0:T(8,128)}) custom-call(bf16[24,384,128]{2,1,0:T(8,128)(2,1)} %pair.7, bf16[128,1024]{1,0:T(8,128)(2,1)} %trans_in.7, bf16[512,128]{1,0:T(8,128)(2,1)} %trans_out.7, bf16[16,128]{1,0:T(8,128)(2,1)} %bitcast.5, bf16[2,64,128]{2,1,0:T(8,128)(2,1)} %get-tuple-element.29.anchor), custom_call_target="tpu_custom_call" | custom-call | flops 6000000000 | bytes 8000000 | tf_op jit(solution)/shard_map/pair_part/pallas_call | solution.py:338
  17.0 0.0 collective-permute-done.1.high
  17.1 0.0 collective-permute-done.low
  17.1 0.0 copy-start.13
  17.1 0.6 copy-done.12
  17.7 0.0 copy-done.13
  17.7 5.6 %atom_stage.1.anchor = s16[16,48,256]{2,1,0:T(8,128)(2,1)} custom-call(s32[1]{0:T(128)} %bitcast.3.place, s32[6]{0:T(128)} %offsets.1, s32[2]{0:T(128)} %levels.3, bf16[2,64,128]{2,1,0:T(8,128)(2,1)} %copy-done.13, bf16[2,64,128]{2,1,0:T(8,128)(2,1)} %copy-done.12, bf16[2,192,128]{2,1,0:T(8,128)(2,1)} %get-tuple-element.34.normed, ...), custom_call_target="tpu_custom_call" | custom-call | flops 3000000000 | bytes 6000000 | tf_op jit(solution)/shard_map/atom_stage/pallas_call | solution.py:585
  23.3 11.3 %all-to-all-start = ((s16[16,48,256]{2,1,0:T(8,128)(2,1)}), s16[16,48,256]{2,1,0:T(8,128)(2,1)S(1)}, u32[]{:S(2)}, u32[]{:S(2)}) async-start(s16[16,48,256]{2,1,0:T(8,128)(2,1)} %atom_stage.1.anchor), calls=%async_computation | async-start | bytes 786432 | tf_op jit(solution)/shard_map/all_to_all | solution.py:601
  34.6 7.1 %pair_part.5 = (bf16[24,384,128]{2,1,0:T(8,128)(2,1)}, f32[16,8,384]{2,1,0:T(8,128)}) custom-call(bf16[24,384,128]{2,1,0:T(8,128)(2,1)} %pair.7, bf16[128,1024]{1,0:T(8,128)(2,1)} %trans_in.7, bf16[512,128]{1,0:T(8,128)(2,1)} %trans_out.7, bf16[16,128]{1,0:T(8,128)(2,1)} %bitcast.6, ...), custom_call_target="tpu_custom_call", output_to_operand_aliasing={{0}: (5, {})} | custom-call | flops 6000000000 | bytes 8000000 | tf_op jit(solution)/shard_map/pair_part/pallas_call | solution.py:338
  41.8 0.8 all-to-all-done.queries
  42.6 0.0 copy-start.3
  42.6 3.1 %collective-permute-start.3 = (s16[16,48,128]{2,1,0:T(8,128)(2,1)S(1)}, s16[16,48,128]{2,1,0:T(8,128)(2,1)S(1)}, u32[]{:S(2)}, u32[]{:S(2)}) collective-permute-start(s16[16,48,128]{2,1,0:T(8,128)(2,1)S(1)} %slice.3.anchor.kv0), channel_id=1, source_target_pairs={{0,224},{32,0},{64,32},{96,64},{128,96},{160,128},{192,160},{224,1... | collective-permute-start | bytes 589832 | tf_op jit(solution)/shard_map/ppermute | solution.py:607
  45.8 0.0 collective-permute-start.2
  45.8 0.0 copy-done.3
  45.8 4.8 %pair_part.6 = (bf16[24,384,128]{2,1,0:T(8,128)(2,1)}, f32[16,4,384]{2,1,0:T(4,128)}) custom-call(bf16[24,384,128]{2,1,0:T(8,128)(2,1)} %pair.7, bf16[128,1024]{1,0:T(8,128)(2,1)} %trans_in.7, bf16[512,128]{1,0:T(8,128)(2,1)} %trans_out.7, bf16[16,128]{1,0:T(8,128)(2,1)} %bitcast.7, s16[16,48,128]{2,1,0:T(8,128)(2,1)} %copy-done.3, ...), custom_call_target="tpu_custom_call", output_to_operand_aliasing={{0}: (5, {})} | custom-call | flops 3000000000 | bytes 4000000 | tf_op jit(solution)/shard_map/pair_part/pallas_call | solution.py:338
  50.6 0.0 copy-done
  50.6 0.0 collective-permute-done.3.kv7
  50.6 1.5 %collective-permute-done.2.anchor.kv1 = s16[16,48,128]{2,1,0:T(8,128)(2,1)S(1)} collective-permute-done((s16[16,48,128]{2,1,0:T(8,128)(2,1)S(1)}, s16[16,48,128]{2,1,0:T(8,128)(2,1)S(1)}, u32[]{:S(2)}, u32[]{:S(2)}) %collective-permute-start.2) | collective-permute-done | bytes 196640 | tf_op jit(solution)/shard_map/ppermute | solution.py:606
  52.1 1.8 %collective-permute-start.5 = (s16[16,48,128]{2,1,0:T(8,128)(2,1)S(1)}, s16[16,48,128]{2,1,0:T(8,128)(2,1)S(1)}, u32[]{:S(2)}, u32[]{:S(2)}) collective-permute-start(s16[16,48,128]{2,1,0:T(8,128)(2,1)S(1)} %collective-permute-done.3.kv7), channel_id=1, source_target_pairs={{0,224},{32,0},{64,32},{96,64},{128,96},{160,128},{192,160},{224,1... | collective-permute-start | bytes 589832 | tf_op jit(solution)/shard_map/ppermute | solution.py:617
  53.9 0.0 collective-permute-start.4
  53.9 0.0 copy-done.6
  53.9 5.1 %pair_part.7 = (bf16[24,384,128]{2,1,0:T(8,128)(2,1)}, s16[16,24,384]{2,1,0:T(8,128)(2,1)}) custom-call(bf16[24,384,128]{2,1,0:T(8,128)(2,1)} %pair.7, bf16[128,1024]{1,0:T(8,128)(2,1)} %trans_in.7, bf16[512,128]{1,0:T(8,128)(2,1)} %trans_out.7, bf16[16,128]{1,0:T(8,128)(2,1)} %bitcast.8, ...), custom_call_target="tpu_custom_call", output_to_operand_aliasing={{0}: (5, {})} | custom-call | flops 3000000000 | bytes 4000000 | tf_op jit(solution)/shard_map/pair_part/pallas_call | solution.py:338
  59.0 0.0 collective-permute-done.5.kv6
  59.0 0.6 collective-permute-done.4.kv2
  59.6 5.8 %all-to-all-start.1 = ((s16[16,24,384]{2,1,0:T(8,128)(2,1)}), s16[16,24,384]{2,1,0:T(8,128)(2,1)S(1)}, u32[]{:S(2)}, u32[]{:S(2)}) async-start(s16[16,24,384]{2,1,0:T(8,128)(2,1)} %get-tuple-element.50), calls=%async_computation.1 | async-start | bytes 589824 | tf_op jit(solution)/shard_map/all_to_all | solution.py:628
  65.5 0.1 collective-permute-start.6
  65.6 7.4 %all-to-all-done.1.bias_mine = s16[16,24,384]{2,1,0:T(8,128)(2,1)S(1)} async-done(((s16[16,24,384]{2,1,0:T(8,128)(2,1)}), s16[16,24,384]{2,1,0:T(8,128)(2,1)S(1)}, u32[]{:S(2)}, u32[]{:S(2)}) %all-to-all-start.1) | async-done | bytes 294944 | tf_op jit(solution)/shard_map/all_to_all | solution.py:628
  73.0 5.7 %collective-permute-start.9 = (s16[16,24,384]{2,1,0:T(8,128)(2,1)S(1)}, s16[16,24,384]{2,1,0:T(8,128)(2,1)S(1)}, u32[]{:S(2)}, u32[]{:S(2)}) collective-permute-start(s16[16,24,384]{2,1,0:T(8,128)(2,1)S(1)} %all-to-all-done.1.bias_mine), channel_id=1, source_target_pairs={{0,1},{1,0},{2,3},{3,2},{4,5},{5,4},{6,7},{7,6},{8,9},{9,8},{10,11... | collective-permute-start | bytes 884744 | tf_op jit(solution)/shard_map/ppermute | solution.py:630
  78.7 1.2 collective-permute-start.8
  79.9 0.0 collective-permute-done.6.kv3
  79.9 0.3 collective-permute-start.7
  80.2 5.1 %collective-permute-done.8.kv5 = s16[16,48,128]{2,1,0:T(8,128)(2,1)S(1)} collective-permute-done((s16[16,48,128]{2,1,0:T(8,128)(2,1)S(1)}, s16[16,48,128]{2,1,0:T(8,128)(2,1)S(1)}, u32[]{:S(2)}, u32[]{:S(2)}) %collective-permute-start.8) | collective-permute-done | bytes 196640 | tf_op jit(solution)/shard_map/ppermute | solution.py:624
  85.2 2.1 %collective-permute-done.7.kv4 = s16[16,48,128]{2,1,0:T(8,128)(2,1)S(1)} collective-permute-done((s16[16,48,128]{2,1,0:T(8,128)(2,1)S(1)}, s16[16,48,128]{2,1,0:T(8,128)(2,1)S(1)}, u32[]{:S(2)}, u32[]{:S(2)}) %collective-permute-start.7) | collective-permute-done | bytes 196640 | tf_op jit(solution)/shard_map/ppermute | solution.py:625
  87.4 0.0 collective-permute-done.9.bias_other
  87.4 0.0 copy-done.7
  87.4 0.6 copy-done.11
  88.0 0.1 copy-done.4
  88.2 8.2 %token_attention.1 = (f32[16,24,512]{2,1,0:T(8,128)}, f32[16,24,384]{2,1,0:T(8,128)}) custom-call(s32[1]{0:T(128)} %bitcast.core_at, s32[1]{0:T(128)} %bitcast.1.head_at, s32[1]{0:T(128)} %bitcast.2.z_at, s16[16,48,256]{2,1,0:T(8,128)(2,1)} %copy-done, s16[16,48,128]{2,1,0:T(8,128)(2,1)} %copy-done.3, s16[16,48,128]{2,1,0:T(8,128)(2,1)} %copy-done.6, ...), custom_call_target="tpu_custom_call" | custom-call | flops 4000000000 | bytes 8000000 | tf_op jit(solution)/shard_map/token_attention/pallas_call | solution.py:634
  96.3 1.1 collective-permute-start.10
  97.4 1.8 %collective-permute-done.10.other = f32[16,24,384]{2,1,0:T(8,128)S(1)} collective-permute-done((f32[16,24,384]{2,1,0:T(8,128)}, f32[16,24,384]{2,1,0:T(8,128)S(1)}, u32[]{:S(2)}, u32[]{:S(2)}) %collective-permute-start.10) | collective-permute-done | bytes 589856 | tf_op jit(solution)/shard_map/ppermute | solution.py:657
  99.3 0.8 copy-done.1
  100.1 2.4 %gradient_merge.1 = s16[16,48,256]{2,1,0:T(8,128)(2,1)} custom-call(f32[16,24,512]{2,1,0:T(8,128)} %get-tuple-element.51.mine, f32[16,24,384]{2,1,0:T(8,128)} %copy-done.1), custom_call_target="tpu_custom_call" | custom-call | flops 2000000 | bytes 2000000 | tf_op jit(solution)/shard_map/gradient_merge/pallas_call | solution.py:649
  102.5 13.8 %all_to_all.15.packed = s16[16,48,256]{2,1,0:T(8,128)(2,1)} all-to-all(s16[16,48,256]{2,1,0:T(8,128)(2,1)} %gradient_merge.1), channel_id=1, replica_groups=mesh['z'=8,'g'=8,'ylo'=2,'core'=2] {'g','ylo'}, dimensions={0} | all-to-all | bytes 786432 | tf_op jit(solution)/shard_map/all_to_all | solution.py:658
  116.3 9.4 %pair_gradient.1 = (bf16[24,384,128]{2,1,0:T(8,128)(2,1)}, bf16[2,24,768]{2,1,0:T(8,128)(2,1)}) custom-call(s16[16,48,256]{2,1,0:T(8,128)(2,1)} %all_to_all.15.packed, bf16[24,384,128]{2,1,0:T(8,128)(2,1)} %get-tuple-element.53.cond, bf16[16,128]{1,0:T(8,128)(2,1)} %bitcast.10), custom_call_target="tpu_custom_call" | custom-call | flops 400000000 | bytes 6000000 | tf_op jit(solution)/shard_map/pair_gradient/pallas_call | solution.py:659
  (18 shorter events, 0.1 us)
Async XLA Ops:
  4.0 13.0 %collective-permute-start.1 = (bf16[2,64,128]{2,1,0:T(8,128)(2,1)}, bf16[2,64,128]{2,1,0:T(8,128)(2,1)S(1)}, u32[]{:S(2)}, u32[]{:S(2)}) collective-permute-start(bf16[2,64,128]{2,1,0:T(8,128)(2,1)} %get-tuple-element.30), channel_id=1, source_target_pairs={{4,0},{8,4},{12,8},{16,12},{20,16},{24,20},{28,24},{32,28},{36,32}... | collective-permute-start | bytes 98312 | tf_op jit(solution)/shard_map/ppermute | solution.py:578
  5.3 11.7 %collective-permute-start = (bf16[2,64,128]{2,1,0:T(8,128)(2,1)}, bf16[2,64,128]{2,1,0:T(8,128)(2,1)S(1)}, u32[]{:S(2)}, u32[]{:S(2)}) collective-permute-start(bf16[2,64,128]{2,1,0:T(8,128)(2,1)} %get-tuple-element.29.anchor), channel_id=1, source_target_pairs={{0,4},{4,8},{8,12},{12,16},{16,20},{20,24},{24,28},{28,32},{32,36}... | collective-permute-start | bytes 98312 | tf_op jit(solution)/shard_map/ppermute | solution.py:577
  17.0 0.6 copy-start.12
  17.1 0.6 copy-start.13
  23.3 19.3 %all-to-all-start = ((s16[16,48,256]{2,1,0:T(8,128)(2,1)}), s16[16,48,256]{2,1,0:T(8,128)(2,1)S(1)}, u32[]{:S(2)}, u32[]{:S(2)}) async-start(s16[16,48,256]{2,1,0:T(8,128)(2,1)} %atom_stage.1.anchor), calls=%async_computation | async-start | bytes 786432 | tf_op jit(solution)/shard_map/all_to_all | solution.py:601
  42.6 8.0 %copy-start = (s16[16,48,256]{2,1,0:T(8,128)(2,1)}, s16[16,48,256]{2,1,0:T(8,128)(2,1)S(1)}, u32[]{:S(2)}) copy-start(s16[16,48,256]{2,1,0:T(8,128)(2,1)S(1)} %all-to-all-done.queries) | copy-start | bytes 1179652
  42.6 3.1 %copy-start.3 = (s16[16,48,128]{2,1,0:T(8,128)(2,1)}, s16[16,48,128]{2,1,0:T(8,128)(2,1)S(1)}, u32[]{:S(2)}) copy-start(s16[16,48,128]{2,1,0:T(8,128)(2,1)S(1)} %slice.3.anchor.kv0) | copy-start | bytes 589828
  42.6 7.9 %collective-permute-start.3 = (s16[16,48,128]{2,1,0:T(8,128)(2,1)S(1)}, s16[16,48,128]{2,1,0:T(8,128)(2,1)S(1)}, u32[]{:S(2)}, u32[]{:S(2)}) collective-permute-start(s16[16,48,128]{2,1,0:T(8,128)(2,1)S(1)} %slice.3.anchor.kv0), channel_id=1, source_target_pairs={{0,224},{32,0},{64,32},{96,64},{128,96},{160,128},{192,160},{224,1... | collective-permute-start | bytes 589832 | tf_op jit(solution)/shard_map/ppermute | solution.py:607
  45.8 6.3 %collective-permute-start.2 = (s16[16,48,128]{2,1,0:T(8,128)(2,1)S(1)}, s16[16,48,128]{2,1,0:T(8,128)(2,1)S(1)}, u32[]{:S(2)}, u32[]{:S(2)}) collective-permute-start(s16[16,48,128]{2,1,0:T(8,128)(2,1)S(1)} %slice.3.anchor.kv0), channel_id=1, source_target_pairs={{0,32},{32,64},{64,96},{96,128},{128,160},{160,192},{192,224},{224... | collective-permute-start | bytes 589832 | tf_op jit(solution)/shard_map/ppermute | solution.py:606
  50.6 8.4 %copy-start.5 = (s16[16,48,128]{2,1,0:T(8,128)(2,1)}, s16[16,48,128]{2,1,0:T(8,128)(2,1)S(1)}, u32[]{:S(2)}) copy-start(s16[16,48,128]{2,1,0:T(8,128)(2,1)S(1)} %collective-permute-done.3.kv7) | copy-start | bytes 589828
  52.1 1.8 %copy-start.6 = (s16[16,48,128]{2,1,0:T(8,128)(2,1)}, s16[16,48,128]{2,1,0:T(8,128)(2,1)S(1)}, u32[]{:S(2)}) copy-start(s16[16,48,128]{2,1,0:T(8,128)(2,1)S(1)} %collective-permute-done.2.anchor.kv1) | copy-start | bytes 589828
  52.1 6.9 %collective-permute-start.5 = (s16[16,48,128]{2,1,0:T(8,128)(2,1)S(1)}, s16[16,48,128]{2,1,0:T(8,128)(2,1)S(1)}, u32[]{:S(2)}, u32[]{:S(2)}) collective-permute-start(s16[16,48,128]{2,1,0:T(8,128)(2,1)S(1)} %collective-permute-done.3.kv7), channel_id=1, source_target_pairs={{0,224},{32,0},{64,32},{96,64},{128,96},{160,128},{192,160},{224,1... | collective-permute-start | bytes 589832 | tf_op jit(solution)/shard_map/ppermute | solution.py:617
  53.9 5.7 %collective-permute-start.4 = (s16[16,48,128]{2,1,0:T(8,128)(2,1)S(1)}, s16[16,48,128]{2,1,0:T(8,128)(2,1)S(1)}, u32[]{:S(2)}, u32[]{:S(2)}) collective-permute-start(s16[16,48,128]{2,1,0:T(8,128)(2,1)S(1)} %collective-permute-done.2.anchor.kv1), channel_id=1, source_target_pairs={{0,32},{32,64},{64,96},{96,128},{128,160},{160,192},{192,224},{224... | collective-permute-start | bytes 589832 | tf_op jit(solution)/shard_map/ppermute | solution.py:616
  59.0 28.4 %copy-start.7 = (s16[16,48,128]{2,1,0:T(8,128)(2,1)}, s16[16,48,128]{2,1,0:T(8,128)(2,1)S(1)}, u32[]{:S(2)}) copy-start(s16[16,48,128]{2,1,0:T(8,128)(2,1)S(1)} %collective-permute-done.5.kv6) | copy-start | bytes 589828
  59.6 27.7 %copy-start.8 = (s16[16,48,128]{2,1,0:T(8,128)(2,1)}, s16[16,48,128]{2,1,0:T(8,128)(2,1)S(1)}, u32[]{:S(2)}) copy-start(s16[16,48,128]{2,1,0:T(8,128)(2,1)S(1)} %collective-permute-done.4.kv2) | copy-start | bytes 589828
  59.6 13.4 %all-to-all-start.1 = ((s16[16,24,384]{2,1,0:T(8,128)(2,1)}), s16[16,24,384]{2,1,0:T(8,128)(2,1)S(1)}, u32[]{:S(2)}, u32[]{:S(2)}) async-start(s16[16,24,384]{2,1,0:T(8,128)(2,1)} %get-tuple-element.50), calls=%async_computation.1 | async-start | bytes 589824 | tf_op jit(solution)/shard_map/all_to_all | solution.py:628
  65.5 14.5 %collective-permute-start.6 = (s16[16,48,128]{2,1,0:T(8,128)(2,1)S(1)}, s16[16,48,128]{2,1,0:T(8,128)(2,1)S(1)}, u32[]{:S(2)}, u32[]{:S(2)}) collective-permute-start(s16[16,48,128]{2,1,0:T(8,128)(2,1)S(1)} %collective-permute-done.4.kv2), channel_id=1, source_target_pairs={{0,32},{32,64},{64,96},{96,128},{128,160},{160,192},{192,224},{224... | collective-permute-start | bytes 589832 | tf_op jit(solution)/shard_map/ppermute | solution.py:623
  73.0 14.4 %copy-start.2 = (s16[16,24,384]{2,1,0:T(8,128)(2,1)}, s16[16,24,384]{2,1,0:T(8,128)(2,1)S(1)}, u32[]{:S(2)}) copy-start(s16[16,24,384]{2,1,0:T(8,128)(2,1)S(1)} %all-to-all-done.1.bias_mine) | copy-start | bytes 884740
  73.0 14.4 %collective-permute-start.9 = (s16[16,24,384]{2,1,0:T(8,128)(2,1)S(1)}, s16[16,24,384]{2,1,0:T(8,128)(2,1)S(1)}, u32[]{:S(2)}, u32[]{:S(2)}) collective-permute-start(s16[16,24,384]{2,1,0:T(8,128)(2,1)S(1)} %all-to-all-done.1.bias_mine), channel_id=1, source_target_pairs={{0,1},{1,0},{2,3},{3,2},{4,5},{5,4},{6,7},{7,6},{8,9},{9,8},{10,11... | collective-permute-start | bytes 884744 | tf_op jit(solution)/shard_map/ppermute | solution.py:630
  78.7 6.5 %collective-permute-start.8 = (s16[16,48,128]{2,1,0:T(8,128)(2,1)S(1)}, s16[16,48,128]{2,1,0:T(8,128)(2,1)S(1)}, u32[]{:S(2)}, u32[]{:S(2)}) collective-permute-start(s16[16,48,128]{2,1,0:T(8,128)(2,1)S(1)} %collective-permute-done.5.kv6), channel_id=1, source_target_pairs={{0,224},{32,0},{64,32},{96,64},{128,96},{160,128},{192,160},{224,1... | collective-permute-start | bytes 589832 | tf_op jit(solution)/shard_map/ppermute | solution.py:624
  79.9 7.5 %copy-start.9 = (s16[16,48,128]{2,1,0:T(8,128)(2,1)}, s16[16,48,128]{2,1,0:T(8,128)(2,1)S(1)}, u32[]{:S(2)}) copy-start(s16[16,48,128]{2,1,0:T(8,128)(2,1)S(1)} %collective-permute-done.6.kv3) | copy-start | bytes 589828
  79.9 7.4 %collective-permute-start.7 = (s16[16,48,128]{2,1,0:T(8,128)(2,1)S(1)}, s16[16,48,128]{2,1,0:T(8,128)(2,1)S(1)}, u32[]{:S(2)}, u32[]{:S(2)}) collective-permute-start(s16[16,48,128]{2,1,0:T(8,128)(2,1)S(1)} %collective-permute-done.6.kv3), channel_id=1, source_target_pairs={{0,32},{32,64},{64,96},{96,128},{128,160},{160,192},{192,224},{224... | collective-permute-start | bytes 589832 | tf_op jit(solution)/shard_map/ppermute | solution.py:625
  85.2 2.2 %copy-start.10 = (s16[16,48,128]{2,1,0:T(8,128)(2,1)}, s16[16,48,128]{2,1,0:T(8,128)(2,1)S(1)}, u32[]{:S(2)}) copy-start(s16[16,48,128]{2,1,0:T(8,128)(2,1)S(1)} %collective-permute-done.8.kv5) | copy-start | bytes 589828
  87.4 0.7 copy-start.11
  87.4 0.8 copy-start.4
  96.3 2.9 %collective-permute-start.10 = (f32[16,24,384]{2,1,0:T(8,128)}, f32[16,24,384]{2,1,0:T(8,128)S(1)}, u32[]{:S(2)}, u32[]{:S(2)}) collective-permute-start(f32[16,24,384]{2,1,0:T(8,128)} %get-tuple-element.52), channel_id=1, source_target_pairs={{0,1},{1,0},{2,3},{3,2},{4,5},{5,4},{6,7},{7,6},{8,9},{9,8},{10,11... | collective-permute-start | bytes 1769480 | tf_op jit(solution)/shard_map/ppermute | solution.py:657
  99.3 0.8 copy-start.1

commit v5 on v4

--- a/solution.py
+++ b/solution.py
@@ -312,19 +312,18 @@
 
 
 def pair_last_kernel(
-    pair, trans_in, trans_out, bias_weight_t, anchor, cond, first, second, third, cond_out, bias_out,
-    held
+    pair, trans_in, trans_out, bias_weight_t, anchor, cond, first, second, cond_out, bias_out, held
 ):
     def store(i, value):
         held[:, i, :] = value
 
     pair_block(pair, trans_in, trans_out, bias_weight_t, cond_out, store)
     for h in range(bias_out.shape[0]):
-        parts = [first[h], second[h], third[h], held[h]]
+        parts = [first[h], second[h], held[h]]
         bias_out[h] = whole(jnp.concatenate(parts, axis=0)).astype(jnp.int16)
 
 
-def pair_call(kernel, step, index, inputs, extra, anchor, cond, bias_shape, scratch=()):
+def pair_call(kernel, step, index, inputs, extra, anchor, cond, bias_shape, scratch=(), room=56):
     pair_rep, trans_in, trans_out, bias_t = inputs
     cols = pair_rep.shape[1]
     block = pl.BlockSpec((step, cols, 128), lambda i: (index, 0, 0))
@@ -343,7 +342,7 @@
         out_specs=(block, pl.BlockSpec(bias_shape.shape, lambda i: (0, 0, 0))),
         scratch_shapes=list(scratch),
         input_output_aliases={} if cond is None else {5: 0},
-        compiler_params=params(),
+        compiler_params=params(room),
         cost_estimate=pl.CostEstimate(
             flops=step * 750_000_000, bytes_accessed=step * 1_000_000, transcendentals=0
         ),
@@ -472,7 +471,20 @@
         ).astype(jnp.int16)
 
 
-def grad_kernel(packed, cond, bias_weight, out, update_out, held):
+def normal_kernel(cond, anchor, normal_out, scale_out):
+    rows, cols, lanes = cond.shape
+    ones, centre = lane_matrices(lanes)
+    group = 4
+    for part in range(rows // group):
+        value = cond[part * group : (part + 1) * group].reshape(group * cols, lanes)
+        half = group * cols // 2
+        centred = dot(jnp.concatenate([value[:half], value[half:]], axis=1), centre)
+        scale = lax.rsqrt(lane_mean(centred * centred, ones) + epsilon)
+        normal_out[part] = centred * scale
+        scale_out[part] = scale
+
+
+def grad_kernel(packed, normals, scales, bias_weight, out, update_out, held):
     step = pl.program_id(0)
     lanes = 128
     heads, _, rows, cols = held.shape[1], 0, held.shape[2], held.shape[3]
@@ -497,7 +509,7 @@
         for p in range(2):
             update_out[p] = jnp.concatenate(pieces[p], axis=1).astype(BF)
 
-    ones, centre = lane_matrices(lanes)
+    ones, _ = lane_matrices(lanes)
     weight = bias_weight[...].astype(F32)
     w_high, w_low = two_parts(weight - jnp.mean(weight, axis=-1, keepdims=True))
     parts = jnp.concatenate([w_high, w_high, w_high, w_low, w_low], axis=0)
@@ -515,17 +527,15 @@
         high, middle, low = three_parts(grad)
         stacked = jnp.concatenate([high, middle, low, high, middle], axis=0)
         grad_normal = paired(dot(stacked, parts, TN))
-        value = cond[part * group : (part + 1) * group].reshape(count, lanes)
-        centred = dot(paired(value), centre)
-        scale = lax.rsqrt(lane_mean(centred * centred, ones) + epsilon)
-        normal = centred * scale
+        normal = normals[step * (rows // group) + part]
+        scale = scales[step * (rows // group) + part]
         result = ((grad_normal - normal * lane_mean(grad_normal * normal, ones)) * scale).astype(BF)
         result = jnp.concatenate([result[:, :lanes], result[:, lanes:]], axis=0)
         out[part * group : (part + 1) * group] = result.reshape(group, cols, lanes)
 
 
-def params(**more):
-    return pltpu.CompilerParams(vmem_limit_bytes=56 * 1024 * 1024, **more)
+def params(mebibytes):
+    return pltpu.CompilerParams(vmem_limit_bytes=mebibytes * 1024 * 1024)
 
 
 VMEM = pl.BlockSpec(memory_space=pltpu.VMEM)
@@ -568,7 +578,7 @@
         ),
         in_specs=[SMEM] + [VMEM] * 3,
         out_specs=(VMEM,) * 4,
-        compiler_params=params(),
+        compiler_params=params(56),
         cost_estimate=pl.CostEstimate(flops=1_000_000, bytes_accessed=500_000, transcendentals=0),
         name="atom_start",
     )(levels, atom_feat, coords, coord_weight)
@@ -580,7 +590,9 @@
     inputs = (pair_rep, trans_in, trans_out, bias_t)
     step = 8
     part_bias = jax.ShapeDtypeStruct((H, step, cols), F32)
-    cond, bias_first = pair_call(pair_first_kernel, step, 0, inputs, [], last, None, part_bias)
+    cond, bias_first = pair_call(
+        pair_first_kernel, step, 0, inputs, [], last, None, part_bias
+    )
     low, high, bias_first = lax.optimization_barrier((low, high, bias_first))
     packed = pl.pallas_call(
         atom_kernel,
@@ -588,7 +600,7 @@
         in_specs=[SMEM] * 3 + [VMEM] * 10 + [ANY, VMEM],
         out_specs=VMEM,
         scratch_shapes=[pltpu.VMEM(token_weight.shape, BF), pltpu.SemaphoreType.DMA],
-        compiler_params=params(),
+        compiler_params=params(56),
         cost_estimate=pl.CostEstimate(flops=3_000_000_000, bytes_accessed=6_000_000, transcendentals=0),
         name="atom_stage",
     )(
@@ -605,30 +617,33 @@
     behind = [(i, (i + 7) % 8) for i in range(8)]
     rising = [own, lax.ppermute(own, "z", ahead)]
     falling = [own, lax.ppermute(own, "z", behind)]
-    small = step // 2
-    small_bias = jax.ShapeDtypeStruct((H, small, cols), F32)
-    cond, bias_third = pair_call(
-        pair_next_kernel, small, 4, inputs, [], own, cond, small_bias
+    cond, bias = pair_call(
+        pair_last_kernel, step, 2, inputs, [bias_first, bias_second], own, cond,
+        jax.ShapeDtypeStruct((H, tok_rows, cols), jnp.int16), [pltpu.VMEM((H, step, cols), F32)],
     )
-    rising[1], falling[1], bias_third = lax.optimization_barrier(
-        (rising[1], falling[1], bias_third)
-    )
+    rising[1], falling[1], bias = lax.optimization_barrier((rising[1], falling[1], bias))
     rising.append(lax.ppermute(rising[1], "z", ahead))
     falling.append(lax.ppermute(falling[1], "z", behind))
-    cond, bias = pair_call(
-        pair_last_kernel, small, 5, inputs, [bias_first, bias_second, bias_third], rising[1], cond,
-        jax.ShapeDtypeStruct((H, tok_rows, cols), jnp.int16), [pltpu.VMEM((H, small, cols), F32)],
-    )
-    rising[2], falling[2], bias = lax.optimization_barrier((rising[2], falling[2], bias))
     rising.append(lax.ppermute(rising[2], "z", ahead))
     falling.append(lax.ppermute(falling[2], "z", behind))
     rising.append(lax.ppermute(rising[3], "z", ahead))
-    every = rising + [falling[3], falling[2], falling[1]]
     steps = tok_rows // step
     bias_mine = lax.all_to_all(bias, PLANE, 0, 0, tiled=True)
     swap = [(0, 1), (1, 0)]
     bias_other = lax.ppermute(bias_mine, "core", swap)
 
+    pieces = (tok_rows // 4, 2 * cols, 256)
+    normals, scales = pl.pallas_call(
+        normal_kernel,
+        out_shape=(jax.ShapeDtypeStruct(pieces, F32),) * 2,
+        in_specs=[VMEM, ANY],
+        out_specs=(VMEM, VMEM),
+        compiler_params=params(20),
+        cost_estimate=pl.CostEstimate(flops=1_500_000_000, bytes_accessed=12_000_000, transcendentals=0),
+        name="pair_normal",
+    )(cond, rising[3])
+    rising[4], normals, scales = lax.optimization_barrier((rising[4], normals, scales))
+    every = rising + [falling[3], falling[2], falling[1]]
     head_index = lax.axis_index(PLANE).astype(jnp.int32)
     z_index = lax.axis_index("z").astype(jnp.int32)
     grad_mine, grad_other = pl.pallas_call(
@@ -640,7 +655,7 @@
         in_specs=[SMEM] * 3 + [VMEM] * 12,
         out_specs=(VMEM, VMEM),
         scratch_shapes=[pltpu.VMEM((8,) + own.shape, jnp.int16)],
-        compiler_params=params(),
+        compiler_params=params(24),
         cost_estimate=pl.CostEstimate(flops=4_000_000_000, bytes_accessed=8_000_000, transcendentals=1_200_000),
         name="token_attention",
     )(
@@ -651,7 +666,7 @@
         out_shape=jax.ShapeDtypeStruct((H, 2 * tok_rows, 256), jnp.int16),
         in_specs=[VMEM] * 2,
         out_specs=VMEM,
-        compiler_params=params(),
+        compiler_params=params(6),
         cost_estimate=pl.CostEstimate(flops=2_000_000, bytes_accessed=2_000_000, transcendentals=0),
         name="gradient_merge",
     )(grad_mine, lax.ppermute(grad_other, "core", swap))
@@ -665,7 +680,8 @@
         ),
         in_specs=[
             pl.BlockSpec(merged.shape, lambda i: (0, 0, 0)),
-            pl.BlockSpec((step, cols, 128), lambda i: (i, 0, 0)),
+            VMEM,
+            VMEM,
             pl.BlockSpec(bias_t.shape, lambda i: (0, 0)),
         ],
         out_specs=(
@@ -673,10 +689,10 @@
             pl.BlockSpec(cotangent.shape, lambda i: (0, 0, 0)),
         ),
         scratch_shapes=[pltpu.VMEM((steps, H, step, cols), F32)],
-        compiler_params=params(),
+        compiler_params=params(24),
         cost_estimate=pl.CostEstimate(flops=400_000_000, bytes_accessed=6_000_000, transcendentals=0),
         name="pair_gradient",
-    )(merged, cond, bias_t)
+    )(merged, normals, scales, bias_t)
     return (update, gradient)
 
 

time: 126 us -> 106 us (0.84); the launches traced: 126 us -> 104 us
  waiting for transfers between devices: 19.4 us -> 9.46 us
  Pallas kernels: 51.9 us -> 42.2 us
  blocking collectives: 13.8 us -> 12.5 us
    pallas_call x1, Pallas kernels: 9.39 us -> 4.75 us  [on_device(): pl.pallas_call(grad_kernel, grid=(steps,), out_shape=(jax.ShapeDtypeStruc...]
    ppermute x1, waiting for transfers between devices: 5.06 us -> 0.97 us  [on_device(): falling.append(lax.ppermute(falling[2], 'z', behind))]
    all_to_all x1, waiting for transfers between devices: 7.43 us -> 4.69 us  [on_device(): bias_mine = lax.all_to_all(bias, PLANE, 0, 0, tiled=True)]
    pallas_call x1, Pallas kernels: 8.16 us -> 5.53 us  [on_device(): pl.pallas_call(attend_kernel, out_shape=(jax.ShapeDtypeStruct((H, tok_row...]
    pallas_call x4 -> x3, Pallas kernels: 24.2 us -> 21.6 us  [pair_call(): pl.pallas_call(kernel, grid=(1,), out_shape=(jax.ShapeDtypeStruct(pair_re...]
    all_to_all x1, starting transfers between devices: 11.3 us -> 8.79 us  [on_device(): packed = lax.all_to_all(packed, PLANE, 0, 0, tiled=True)]
    ppermute x1, starting transfers between devices: 5.71 us -> 3.39 us  [on_device(): bias_other = lax.ppermute(bias_mine, 'core', swap)]
    pallas_call x0 -> x1, Pallas kernels: none -> 2.17 us  [on_device(): pl.pallas_call(normal_kernel, out_shape=(jax.ShapeDtypeStruct(pieces, F32...]
  transfers between devices with their start and end apart: 13 -> 13, of which waited for: 7 -> 5; matrix products, arithmetic and copies ran while one was open for 0% -> 0% of each run, Pallas kernels for 19% -> 23%
where the time goes in v5:
time: 106 us; the launch traced here: 104 us
  Pallas kernels  42.2 us (40%)
  starting transfers between devices  35.8 us (34%)
  blocking collectives  12.5 us (12%)
  waiting for transfers between devices  9.46 us (9%)
  local copies, waits for them, and re-layouts  3.61 us (3%)
    pallas_call x3, Pallas kernels, pair_call(): pl.pallas_call(kernel, grid=(1,), out_shape=(jax.ShapeDtypeStruct(pair_re...  21.6 us
    all_to_all x1, blocking collectives, on_device(): merged = lax.all_to_all(merged, PLANE, 0, 0, tiled=True)  12.5 us
    all_to_all x1, starting transfers between devices, on_device(): packed = lax.all_to_all(packed, PLANE, 0, 0, tiled=True)  8.79 us
    all_to_all x1, starting transfers between devices, on_device(): bias_mine = lax.all_to_all(bias, PLANE, 0, 0, tiled=True)  5.81 us
    pallas_call x1, Pallas kernels, on_device(): pl.pallas_call(atom_kernel, out_shape=jax.ShapeDtypeStruct((H, copies * t...  5.64 us
    pallas_call x1, Pallas kernels, on_device(): pl.pallas_call(attend_kernel, out_shape=(jax.ShapeDtypeStruct((H, tok_row...  5.53 us
    pallas_call x1, Pallas kernels, on_device(): pl.pallas_call(grad_kernel, grid=(steps,), out_shape=(jax.ShapeDtypeStruc...  4.75 us
    all_to_all x1, waiting for transfers between devices, on_device(): bias_mine = lax.all_to_all(bias, PLANE, 0, 0, tiled=True)  4.69 us
  transfers between devices with their start and end apart: 13, of which 5 were waited for; matrix products, arithmetic and copies ran while one was open for 0% of the time, Pallas kernels for 23%

profile of v5, /device:TPU:1, one launch (start us, length us, event | category | flops | bytes accessed | tf_op | source)
XLA Modules:
  0.0 104.3 jit_solution(5763118311731994851)
XLA Ops:
  0.6 1.3 %copy.21.coords = f32[2,3,192]{2,1,0:T(4,128)} copy(f32[2,3,192]{2,0,1:T(2,128)} %param.20) | data formatting | bytes 9216 | tf_op args[3]
  1.9 2.1 %atom_start.1 = (f32[2,192,128]{2,1,0:T(8,128)}, bf16[2,192,128]{2,1,0:T(8,128)(2,1)}, bf16[2,64,128]{2,1,0:T(8,128)(2,1)}, bf16[2,64,128]{2,1,0:T(8,128)(2,1)}) custom-call(s32[2]{0:T(128)} %levels.3, bf16[192,128]{1,0:T(8,128)(2,1)} %feat.1, f32[2,3,192]{2,1,0:T(4,128)} %copy.21.coords, f32[3,128]{1,0:T(4,128)} %coord_weight.1), custom_call_target="tpu_custom_call" | custom-call | flops 1000000 | bytes 500000 | tf_op jit(solution)/shard_map/atom_start/pallas_call | solution.py:571
  4.0 3.9 %collective-permute-start = (bf16[2,64,128]{2,1,0:T(8,128)(2,1)}, bf16[2,64,128]{2,1,0:T(8,128)(2,1)S(1)}, u32[]{:S(2)}, u32[]{:S(2)}) collective-permute-start(bf16[2,64,128]{2,1,0:T(8,128)(2,1)} %get-tuple-element.29.anchor), channel_id=1, source_target_pairs={{0,4},{4,8},{8,12},{12,16},{16,20},{20,24},{24,28},{28,32},{32,36}... | collective-permute-start | bytes 98312 | tf_op jit(solution)/shard_map/ppermute | solution.py:587
  8.0 1.3 %collective-permute-start.1 = (bf16[2,64,128]{2,1,0:T(8,128)(2,1)}, bf16[2,64,128]{2,1,0:T(8,128)(2,1)S(1)}, u32[]{:S(2)}, u32[]{:S(2)}) collective-permute-start(bf16[2,64,128]{2,1,0:T(8,128)(2,1)} %get-tuple-element.30), channel_id=1, source_target_pairs={{4,0},{8,4},{12,8},{16,12},{20,16},{24,20},{28,24},{32,28},{36,32}... | collective-permute-start | bytes 98312 | tf_op jit(solution)/shard_map/ppermute | solution.py:588
  9.3 7.2 %pair_part.3 = (bf16[24,384,128]{2,1,0:T(8,128)(2,1)}, f32[16,8,384]{2,1,0:T(8,128)}) custom-call(bf16[24,384,128]{2,1,0:T(8,128)(2,1)} %pair.5, bf16[128,1024]{1,0:T(8,128)(2,1)} %trans_in.5, bf16[512,128]{1,0:T(8,128)(2,1)} %trans_out.5, bf16[16,128]{1,0:T(8,128)(2,1)} %bitcast.5, bf16[2,64,128]{2,1,0:T(8,128)(2,1)} %get-tuple-element.29.anchor), custom_call_target="tpu_custom_call" | custom-call | flops 6000000000 | bytes 8000000 | tf_op jit(solution)/shard_map/pair_part/pallas_call | solution.py:337
  16.4 0.0 collective-permute-done.low
  16.4 0.0 copy-start.4
  16.4 0.0 collective-permute-done.1.high
  16.4 0.0 copy-start.5
  16.4 0.6 copy-done.4
  17.0 0.0 copy-done.5
  17.0 5.6 %atom_stage.1.anchor = s16[16,48,256]{2,1,0:T(8,128)(2,1)} custom-call(s32[1]{0:T(128)} %bitcast.3.place, s32[6]{0:T(128)} %offsets.1, s32[2]{0:T(128)} %levels.3, bf16[2,64,128]{2,1,0:T(8,128)(2,1)} %copy-done.4, bf16[2,64,128]{2,1,0:T(8,128)(2,1)} %copy-done.5, bf16[2,192,128]{2,1,0:T(8,128)(2,1)} %get-tuple-element.34.normed, ...), custom_call_target="tpu_custom_call" | custom-call | flops 3000000000 | bytes 6000000 | tf_op jit(solution)/shard_map/atom_stage/pallas_call | solution.py:597
  22.7 8.8 %all-to-all-start = ((s16[16,48,256]{2,1,0:T(8,128)(2,1)}), s16[16,48,256]{2,1,0:T(8,128)(2,1)S(1)}, u32[]{:S(2)}, u32[]{:S(2)}) async-start(s16[16,48,256]{2,1,0:T(8,128)(2,1)} %atom_stage.1.anchor), calls=%async_computation | async-start | bytes 786432 | tf_op jit(solution)/shard_map/all_to_all | solution.py:613
  31.5 7.1 %pair_part.4 = (bf16[24,384,128]{2,1,0:T(8,128)(2,1)}, f32[16,8,384]{2,1,0:T(8,128)}) custom-call(bf16[24,384,128]{2,1,0:T(8,128)(2,1)} %pair.5, bf16[128,1024]{1,0:T(8,128)(2,1)} %trans_in.5, bf16[512,128]{1,0:T(8,128)(2,1)} %trans_out.5, bf16[16,128]{1,0:T(8,128)(2,1)} %bitcast.6, ...), custom_call_target="tpu_custom_call", output_to_operand_aliasing={{0}: (5, {})} | custom-call | flops 6000000000 | bytes 8000000 | tf_op jit(solution)/shard_map/pair_part/pallas_call | solution.py:337
  38.6 0.9 all-to-all-done.queries
  39.6 0.0 copy-start
  39.6 1.8 %collective-permute-start.2 = (s16[16,48,128]{2,1,0:T(8,128)(2,1)S(1)}, s16[16,48,128]{2,1,0:T(8,128)(2,1)S(1)}, u32[]{:S(2)}, u32[]{:S(2)}) collective-permute-start(s16[16,48,128]{2,1,0:T(8,128)(2,1)S(1)} %slice.3.anchor.kv0), channel_id=1, source_target_pairs={{0,32},{32,64},{64,96},{96,128},{128,160},{160,192},{192,224},{224... | collective-permute-start | bytes 589832 | tf_op jit(solution)/shard_map/ppermute | solution.py:618
  41.4 4.0 %collective-permute-start.3 = (s16[16,48,128]{2,1,0:T(8,128)(2,1)S(1)}, s16[16,48,128]{2,1,0:T(8,128)(2,1)S(1)}, u32[]{:S(2)}, u32[]{:S(2)}) collective-permute-start(s16[16,48,128]{2,1,0:T(8,128)(2,1)S(1)} %slice.3.anchor.kv0), channel_id=1, source_target_pairs={{0,224},{32,0},{64,32},{96,64},{128,96},{160,128},{192,160},{224,1... | collective-permute-start | bytes 589832 | tf_op jit(solution)/shard_map/ppermute | solution.py:619
  45.4 0.0 copy-done
  45.4 7.3 %pair_part.5 = (bf16[24,384,128]{2,1,0:T(8,128)(2,1)}, s16[16,24,384]{2,1,0:T(8,128)(2,1)}) custom-call(bf16[24,384,128]{2,1,0:T(8,128)(2,1)} %pair.5, bf16[128,1024]{1,0:T(8,128)(2,1)} %trans_in.5, bf16[512,128]{1,0:T(8,128)(2,1)} %trans_out.5, bf16[16,128]{1,0:T(8,128)(2,1)} %bitcast.7, ...), custom_call_target="tpu_custom_call", output_to_operand_aliasing={{0}: (5, {})} | custom-call | flops 6000000000 | bytes 8000000 | tf_op jit(solution)/shard_map/pair_part/pallas_call | solution.py:337
  52.7 0.0 collective-permute-done.2.kv1
  52.7 0.0 collective-permute-done.3.kv7
  52.7 0.1 collective-permute-start.4
  52.8 5.8 %all-to-all-start.1 = ((s16[16,24,384]{2,1,0:T(8,128)(2,1)}), s16[16,24,384]{2,1,0:T(8,128)(2,1)S(1)}, u32[]{:S(2)}, u32[]{:S(2)}) async-start(s16[16,24,384]{2,1,0:T(8,128)(2,1)} %get-tuple-element.49), calls=%async_computation.1 | async-start | bytes 589824 | tf_op jit(solution)/shard_map/all_to_all | solution.py:631
  58.6 0.0 collective-permute-done.4.kv2
  58.6 1.1 %collective-permute-start.5 = (s16[16,48,128]{2,1,0:T(8,128)(2,1)S(1)}, s16[16,48,128]{2,1,0:T(8,128)(2,1)S(1)}, u32[]{:S(2)}, u32[]{:S(2)}) collective-permute-start(s16[16,48,128]{2,1,0:T(8,128)(2,1)S(1)} %collective-permute-done.4.kv2), channel_id=1, source_target_pairs={{0,32},{32,64},{64,96},{96,128},{128,160},{160,192},{192,224},{224... | collective-permute-start | bytes 589832 | tf_op jit(solution)/shard_map/ppermute | solution.py:627
  59.7 1.7 %collective-permute-start.7 = (s16[16,48,128]{2,1,0:T(8,128)(2,1)S(1)}, s16[16,48,128]{2,1,0:T(8,128)(2,1)S(1)}, u32[]{:S(2)}, u32[]{:S(2)}) collective-permute-start(s16[16,48,128]{2,1,0:T(8,128)(2,1)S(1)} %collective-permute-done.3.kv7), channel_id=1, source_target_pairs={{0,224},{32,0},{64,32},{96,64},{128,96},{160,128},{192,160},{224,1... | collective-permute-start | bytes 589832 | tf_op jit(solution)/shard_map/ppermute | solution.py:626
  61.5 4.7 %all-to-all-done.1.bias_mine = s16[16,24,384]{2,1,0:T(8,128)(2,1)S(1)} async-done(((s16[16,24,384]{2,1,0:T(8,128)(2,1)}), s16[16,24,384]{2,1,0:T(8,128)(2,1)S(1)}, u32[]{:S(2)}, u32[]{:S(2)}) %all-to-all-start.1) | async-done | bytes 294944 | tf_op jit(solution)/shard_map/all_to_all | solution.py:631
  66.2 3.4 %collective-permute-start.9 = (s16[16,24,384]{2,1,0:T(8,128)(2,1)S(1)}, s16[16,24,384]{2,1,0:T(8,128)(2,1)S(1)}, u32[]{:S(2)}, u32[]{:S(2)}) collective-permute-start(s16[16,24,384]{2,1,0:T(8,128)(2,1)S(1)} %all-to-all-done.1.bias_mine), channel_id=1, source_target_pairs={{0,1},{1,0},{2,3},{3,2},{4,5},{5,4},{6,7},{7,6},{8,9},{9,8},{10,11... | collective-permute-start | bytes 884744 | tf_op jit(solution)/shard_map/ppermute | solution.py:633
  69.5 0.0 collective-permute-done.5.anchor.kv3
  69.5 2.3 %collective-permute-start.6 = (s16[16,48,128]{2,1,0:T(8,128)(2,1)S(1)}, s16[16,48,128]{2,1,0:T(8,128)(2,1)S(1)}, u32[]{:S(2)}, u32[]{:S(2)}) collective-permute-start(s16[16,48,128]{2,1,0:T(8,128)(2,1)S(1)} %collective-permute-done.5.anchor.kv3), channel_id=1, source_target_pairs={{0,32},{32,64},{64,96},{96,128},{128,160},{160,192},{192,224},{224... | collective-permute-start | bytes 589832 | tf_op jit(solution)/shard_map/ppermute | solution.py:629
  71.8 0.0 collective-permute-done.7.kv6
  71.8 0.8 collective-permute-start.8
  72.6 0.0 copy-start.3
  72.6 1.7 %copy-done.3 = bf16[24,384,128]{2,1,0:T(8,128)(2,1)S(1)} copy-done((bf16[24,384,128]{2,1,0:T(8,128)(2,1)S(1)}, bf16[24,384,128]{2,1,0:T(8,128)(2,1)}, u32[]{:S(2)}) %copy-start.3) | copy-done | bytes 2359320
  74.2 0.0 copy-start.1
  74.2 2.2 %pair_normal.1 = (f32[6,768,256]{2,1,0:T(8,128)S(1)}, f32[6,768,256]{2,1,0:T(8,128)S(1)}) custom-call(bf16[24,384,128]{2,1,0:T(8,128)(2,1)S(1)} %copy-done.3, s16[16,48,128]{2,1,0:T(8,128)(2,1)S(1)} %collective-permute-done.5.anchor.kv3), custom_call_target="tpu_custom_call" | custom-call | flops 1500000000 | bytes 12000000 | tf_op jit(solution)/shard_map/pair_normal/pallas_call | solution.py:636
  76.4 1.2 %collective-permute-done.6.kv4 = s16[16,48,128]{2,1,0:T(8,128)(2,1)S(1)} collective-permute-done((s16[16,48,128]{2,1,0:T(8,128)(2,1)S(1)}, s16[16,48,128]{2,1,0:T(8,128)(2,1)S(1)}, u32[]{:S(2)}, u32[]{:S(2)}) %collective-permute-start.6) | collective-permute-done | bytes 196640 | tf_op jit(solution)/shard_map/ppermute | solution.py:629
  77.6 1.0 collective-permute-done.8.kv5
  78.6 0.0 collective-permute-done.9.bias_other
  78.6 0.0 copy-done.1
  78.6 0.0 copy-done.2
  78.6 5.5 %token_attention.1 = (f32[16,24,512]{2,1,0:T(8,128)S(1)}, f32[16,24,384]{2,1,0:T(8,128)S(1)}) custom-call(s32[1]{0:T(128)} %bitcast.core_at, s32[1]{0:T(128)} %bitcast.1.head_at, s32[1]{0:T(128)} %bitcast.2.z_at, s16[16,48,256]{2,1,0:T(8,128)(2,1)S(1)} %all-to-all-done.queries, s16[16,48,128]{2,1,0:T(8,128)(2,1)S(1)} %copy-done.1, ...), custom_call_target="tpu_custom_call" | custom-call | flops 4000000000 | bytes 8000000 | tf_op jit(solution)/shard_map/token_attention/pallas_call | solution.py:649
  84.2 0.9 collective-permute-start.10
  85.0 1.6 %collective-permute-done.10.other = f32[16,24,384]{2,1,0:T(8,128)S(1)} collective-permute-done((f32[16,24,384]{2,1,0:T(8,128)S(1)}, f32[16,24,384]{2,1,0:T(8,128)S(1)}, u32[]{:S(2)}, u32[]{:S(2)}) %collective-permute-start.10) | collective-permute-done | bytes 589856 | tf_op jit(solution)/shard_map/ppermute | solution.py:672
  86.7 0.4 gradient_merge.1
  87.1 12.5 %all_to_all.15.packed = s16[16,48,256]{2,1,0:T(8,128)(2,1)S(1)} all-to-all(s16[16,48,256]{2,1,0:T(8,128)(2,1)S(1)} %gradient_merge.1), channel_id=1, replica_groups=mesh['z'=8,'g'=8,'ylo'=2,'core'=2] {'g','ylo'}, dimensions={0} | all-to-all | bytes 786432 | tf_op jit(solution)/shard_map/all_to_all | solution.py:673
  99.5 4.8 %pair_gradient.1 = (bf16[24,384,128]{2,1,0:T(8,128)(2,1)}, bf16[2,24,768]{2,1,0:T(8,128)(2,1)}) custom-call(s16[16,48,256]{2,1,0:T(8,128)(2,1)S(1)} %all_to_all.15.packed, f32[6,768,256]{2,1,0:T(8,128)S(1)} %get-tuple-element.52.normals, f32[6,768,256]{2,1,0:T(8,128)S(1)} %get-tuple-element.53.scales, bf16[16,128]{1,0:T(8,128)(2,1)S(1)} %bitcast.9), custom_call_target="tpu_custom_call" | custom-call | flops 400000000 | bytes 6000000 | tf_op jit(solution)/shard_map/pair_gradient/pallas_call | solution.py:674
  (2 shorter events, 0.0 us)
Async XLA Ops:
  4.0 12.4 %collective-permute-start = (bf16[2,64,128]{2,1,0:T(8,128)(2,1)}, bf16[2,64,128]{2,1,0:T(8,128)(2,1)S(1)}, u32[]{:S(2)}, u32[]{:S(2)}) collective-permute-start(bf16[2,64,128]{2,1,0:T(8,128)(2,1)} %get-tuple-element.29.anchor), channel_id=1, source_target_pairs={{0,4},{4,8},{8,12},{12,16},{16,20},{20,24},{24,28},{28,32},{32,36}... | collective-permute-start | bytes 98312 | tf_op jit(solution)/shard_map/ppermute | solution.py:587
  8.0 8.5 %collective-permute-start.1 = (bf16[2,64,128]{2,1,0:T(8,128)(2,1)}, bf16[2,64,128]{2,1,0:T(8,128)(2,1)S(1)}, u32[]{:S(2)}, u32[]{:S(2)}) collective-permute-start(bf16[2,64,128]{2,1,0:T(8,128)(2,1)} %get-tuple-element.30), channel_id=1, source_target_pairs={{4,0},{8,4},{12,8},{16,12},{20,16},{24,20},{28,24},{32,28},{36,32}... | collective-permute-start | bytes 98312 | tf_op jit(solution)/shard_map/ppermute | solution.py:588
  16.4 0.6 copy-start.4
  16.4 0.6 copy-start.5
  22.7 16.8 %all-to-all-start = ((s16[16,48,256]{2,1,0:T(8,128)(2,1)}), s16[16,48,256]{2,1,0:T(8,128)(2,1)S(1)}, u32[]{:S(2)}, u32[]{:S(2)}) async-start(s16[16,48,256]{2,1,0:T(8,128)(2,1)} %atom_stage.1.anchor), calls=%async_computation | async-start | bytes 786432 | tf_op jit(solution)/shard_map/all_to_all | solution.py:613
  39.6 5.8 %copy-start = (s16[16,48,128]{2,1,0:T(8,128)(2,1)}, s16[16,48,128]{2,1,0:T(8,128)(2,1)S(1)}, u32[]{:S(2)}) copy-start(s16[16,48,128]{2,1,0:T(8,128)(2,1)S(1)} %slice.3.anchor.kv0) | copy-start | bytes 589828
  39.6 13.1 %collective-permute-start.2 = (s16[16,48,128]{2,1,0:T(8,128)(2,1)S(1)}, s16[16,48,128]{2,1,0:T(8,128)(2,1)S(1)}, u32[]{:S(2)}, u32[]{:S(2)}) collective-permute-start(s16[16,48,128]{2,1,0:T(8,128)(2,1)S(1)} %slice.3.anchor.kv0), channel_id=1, source_target_pairs={{0,32},{32,64},{64,96},{96,128},{128,160},{160,192},{192,224},{224... | collective-permute-start | bytes 589832 | tf_op jit(solution)/shard_map/ppermute | solution.py:618
  41.4 11.3 %collective-permute-start.3 = (s16[16,48,128]{2,1,0:T(8,128)(2,1)S(1)}, s16[16,48,128]{2,1,0:T(8,128)(2,1)S(1)}, u32[]{:S(2)}, u32[]{:S(2)}) collective-permute-start(s16[16,48,128]{2,1,0:T(8,128)(2,1)S(1)} %slice.3.anchor.kv0), channel_id=1, source_target_pairs={{0,224},{32,0},{64,32},{96,64},{128,96},{160,128},{192,160},{224,1... | collective-permute-start | bytes 589832 | tf_op jit(solution)/shard_map/ppermute | solution.py:619
  52.7 5.9 %collective-permute-start.4 = (s16[16,48,128]{2,1,0:T(8,128)(2,1)S(1)}, s16[16,48,128]{2,1,0:T(8,128)(2,1)S(1)}, u32[]{:S(2)}, u32[]{:S(2)}) collective-permute-start(s16[16,48,128]{2,1,0:T(8,128)(2,1)S(1)} %collective-permute-done.2.kv1), channel_id=1, source_target_pairs={{0,32},{32,64},{64,96},{96,128},{128,160},{160,192},{192,224},{224... | collective-permute-start | bytes 589832 | tf_op jit(solution)/shard_map/ppermute | solution.py:625
  52.8 13.3 %all-to-all-start.1 = ((s16[16,24,384]{2,1,0:T(8,128)(2,1)}), s16[16,24,384]{2,1,0:T(8,128)(2,1)S(1)}, u32[]{:S(2)}, u32[]{:S(2)}) async-start(s16[16,24,384]{2,1,0:T(8,128)(2,1)} %get-tuple-element.49), calls=%async_computation.1 | async-start | bytes 589824 | tf_op jit(solution)/shard_map/all_to_all | solution.py:631
  58.6 10.9 %collective-permute-start.5 = (s16[16,48,128]{2,1,0:T(8,128)(2,1)S(1)}, s16[16,48,128]{2,1,0:T(8,128)(2,1)S(1)}, u32[]{:S(2)}, u32[]{:S(2)}) collective-permute-start(s16[16,48,128]{2,1,0:T(8,128)(2,1)S(1)} %collective-permute-done.4.kv2), channel_id=1, source_target_pairs={{0,32},{32,64},{64,96},{96,128},{128,160},{160,192},{192,224},{224... | collective-permute-start | bytes 589832 | tf_op jit(solution)/shard_map/ppermute | solution.py:627
  59.7 12.1 %collective-permute-start.7 = (s16[16,48,128]{2,1,0:T(8,128)(2,1)S(1)}, s16[16,48,128]{2,1,0:T(8,128)(2,1)S(1)}, u32[]{:S(2)}, u32[]{:S(2)}) collective-permute-start(s16[16,48,128]{2,1,0:T(8,128)(2,1)S(1)} %collective-permute-done.3.kv7), channel_id=1, source_target_pairs={{0,224},{32,0},{64,32},{96,64},{128,96},{160,128},{192,160},{224,1... | collective-permute-start | bytes 589832 | tf_op jit(solution)/shard_map/ppermute | solution.py:626
  66.2 12.5 %collective-permute-start.9 = (s16[16,24,384]{2,1,0:T(8,128)(2,1)S(1)}, s16[16,24,384]{2,1,0:T(8,128)(2,1)S(1)}, u32[]{:S(2)}, u32[]{:S(2)}) collective-permute-start(s16[16,24,384]{2,1,0:T(8,128)(2,1)S(1)} %all-to-all-done.1.bias_mine), channel_id=1, source_target_pairs={{0,1},{1,0},{2,3},{3,2},{4,5},{5,4},{6,7},{7,6},{8,9},{9,8},{10,11... | collective-permute-start | bytes 884744 | tf_op jit(solution)/shard_map/ppermute | solution.py:633
  69.5 8.1 %collective-permute-start.6 = (s16[16,48,128]{2,1,0:T(8,128)(2,1)S(1)}, s16[16,48,128]{2,1,0:T(8,128)(2,1)S(1)}, u32[]{:S(2)}, u32[]{:S(2)}) collective-permute-start(s16[16,48,128]{2,1,0:T(8,128)(2,1)S(1)} %collective-permute-done.5.anchor.kv3), channel_id=1, source_target_pairs={{0,32},{32,64},{64,96},{96,128},{128,160},{160,192},{192,224},{224... | collective-permute-start | bytes 589832 | tf_op jit(solution)/shard_map/ppermute | solution.py:629
  71.8 6.8 %collective-permute-start.8 = (s16[16,48,128]{2,1,0:T(8,128)(2,1)S(1)}, s16[16,48,128]{2,1,0:T(8,128)(2,1)S(1)}, u32[]{:S(2)}, u32[]{:S(2)}) collective-permute-start(s16[16,48,128]{2,1,0:T(8,128)(2,1)S(1)} %collective-permute-done.7.kv6), channel_id=1, source_target_pairs={{0,224},{32,0},{64,32},{96,64},{128,96},{160,128},{192,160},{224,1... | collective-permute-start | bytes 589832 | tf_op jit(solution)/shard_map/ppermute | solution.py:628
  72.6 1.7 %copy-start.3 = (bf16[24,384,128]{2,1,0:T(8,128)(2,1)S(1)}, bf16[24,384,128]{2,1,0:T(8,128)(2,1)}, u32[]{:S(2)}) copy-start(bf16[24,384,128]{2,1,0:T(8,128)(2,1)} %get-tuple-element.44.cond) | copy-start | bytes 7077892
  74.2 4.4 %copy-start.1 = (s16[16,48,128]{2,1,0:T(8,128)(2,1)S(1)}, s16[16,48,128]{2,1,0:T(8,128)(2,1)}, u32[]{:S(2)}) copy-start(s16[16,48,128]{2,1,0:T(8,128)(2,1)} %copy-done) | copy-start | bytes 589828
  74.2 4.4 %copy-start.2 = (bf16[128,16]{0,1:T(8,128)(2,1)S(1)}, bf16[128,16]{0,1:T(8,128)(2,1)}, u32[]{:S(2)}) copy-start(bf16[128,16]{0,1:T(8,128)(2,1)} %param.26) | copy-start | bytes 12292
  84.2 2.5 %collective-permute-start.10 = (f32[16,24,384]{2,1,0:T(8,128)S(1)}, f32[16,24,384]{2,1,0:T(8,128)S(1)}, u32[]{:S(2)}, u32[]{:S(2)}) collective-permute-start(f32[16,24,384]{2,1,0:T(8,128)S(1)} %get-tuple-element.51), channel_id=1, source_target_pairs={{0,1},{1,0},{2,3},{3,2},{4,5},{5,4},{6,7},{7,6},{8,9},{9,8},{10,11... | collective-permute-start | bytes 1769480 | tf_op jit(solution)/shard_map/ppermute | solution.py:672

commit v6 on v5

--- a/solution.py
+++ b/solution.py
@@ -247,10 +247,24 @@
     ones, centre = lane_matrices(lanes)
     unit = head_unit(bias_weight_t[...])
 
-    def normalise(value):
+    def half_mean(value):
+        return jnp.concatenate(
+            [
+                jnp.broadcast_to(
+                    jnp.mean(value[:, at : at + lanes], axis=-1, keepdims=True),
+                    (value.shape[0], lanes),
+                )
+                for at in (0, lanes)
+            ],
+            axis=1,
+        )
+
+    def normalise(value, by_product):
         half = value.shape[0] // 2
         centred = dot(jnp.concatenate([value[:half], value[half:]], axis=1), centre)
-        normal = (centred * lax.rsqrt(lane_mean(centred * centred, ones) + epsilon)).astype(BF)
+        square = centred * centred
+        spread = lane_mean(square, ones) if by_product else half_mean(square)
+        normal = (centred * lax.rsqrt(spread + epsilon)).astype(BF)
         return jnp.concatenate([normal[:, :lanes], normal[:, lanes:]], axis=0)
 
     group = 2
@@ -285,7 +299,7 @@
 
     def project(k):
         if 0 <= k < count:
-            bias = dot(bias_weight_t[...], normalise(cond[k]), NT) * (1.0 / unit)
+            bias = dot(bias_weight_t[...], normalise(cond[k], True), NT) * (1.0 / unit)
             for i in range(group):
                 store(k * group + i, bias[:, i * cols : (i + 1) * cols])
 
@@ -296,13 +310,13 @@
         down(t - 2)
         gate(t - 1, 2)
         if t < count:
-            normed[t] = normalise(value_of(t))
+            normed[t] = normalise(value_of(t), False)
         gate(t - 1, 3)
 
 
 def pair_first_kernel(pair, trans_in, trans_out, bias_weight_t, anchor, cond_out, bias_out):
     def store(i, value):
-        bias_out[:, i, :] = value
+        bias_out[0, :, i, :] = value
 
     pair_block(pair, trans_in, trans_out, bias_weight_t, cond_out, store)
 
@@ -314,37 +328,43 @@
 def pair_last_kernel(
     pair, trans_in, trans_out, bias_weight_t, anchor, cond, first, second, cond_out, bias_out, held
 ):
+    step = pl.program_id(0)
+
     def store(i, value):
-        held[:, i, :] = value
+        held[step, :, i, :] = value
 
     pair_block(pair, trans_in, trans_out, bias_weight_t, cond_out, store)
-    for h in range(bias_out.shape[0]):
-        parts = [first[h], second[h], held[h]]
-        bias_out[h] = whole(jnp.concatenate(parts, axis=0)).astype(jnp.int16)
-
-
-def pair_call(kernel, step, index, inputs, extra, anchor, cond, bias_shape, scratch=(), room=56):
+
+    @pl.when(step == pl.num_programs(0) - 1)
+    def _():
+        for h in range(bias_out.shape[0]):
+            parts = [ref[s, h] for ref in (first, second, held) for s in range(held.shape[0])]
+            bias_out[h] = whole(jnp.concatenate(parts, axis=0)).astype(jnp.int16)
+
+
+def pair_call(kernel, index, inputs, extra, anchor, cond, bias_shape, bias_block, scratch=()):
     pair_rep, trans_in, trans_out, bias_t = inputs
     cols = pair_rep.shape[1]
-    block = pl.BlockSpec((step, cols, 128), lambda i: (index, 0, 0))
+    rows, steps = 4, 2
+    block = pl.BlockSpec((rows, cols, 128), lambda i: (steps * index + i, 0, 0))
     operands = [pair_rep, trans_in, trans_out, bias_t, anchor]
     if cond is not None:
         operands.append(cond)
     count = len(operands)
     specs = [block] + [pl.BlockSpec(x.shape, lambda i: (0, 0)) for x in operands[1:4]]
     specs += [ANY] * (count - 4)
-    specs += [pl.BlockSpec(x.shape, lambda i: (0, 0, 0)) for x in extra]
+    specs += [pl.BlockSpec(x.shape, lambda i: (0, 0, 0, 0)) for x in extra]
     return pl.pallas_call(
         kernel,
-        grid=(1,),
+        grid=(steps,),
         out_shape=(jax.ShapeDtypeStruct(pair_rep.shape, BF), bias_shape),
         in_specs=specs,
-        out_specs=(block, pl.BlockSpec(bias_shape.shape, lambda i: (0, 0, 0))),
+        out_specs=(block, bias_block),
         scratch_shapes=list(scratch),
         input_output_aliases={} if cond is None else {5: 0},
-        compiler_params=params(room),
+        compiler_params=params(56),
         cost_estimate=pl.CostEstimate(
-            flops=step * 750_000_000, bytes_accessed=step * 1_000_000, transcendentals=0
+            flops=6_000_000_000, bytes_accessed=8_000_000, transcendentals=0
         ),
         name="pair_part",
     )(*operands, *extra)
@@ -589,10 +609,9 @@
     bias_t = bias_weight.T
     inputs = (pair_rep, trans_in, trans_out, bias_t)
     step = 8
-    part_bias = jax.ShapeDtypeStruct((H, step, cols), F32)
-    cond, bias_first = pair_call(
-        pair_first_kernel, step, 0, inputs, [], last, None, part_bias
-    )
+    part_bias = jax.ShapeDtypeStruct((2, H, step // 2, cols), F32)
+    part_block = pl.BlockSpec((1, H, step // 2, cols), lambda i: (i, 0, 0, 0))
+    cond, bias_first = pair_call(pair_first_kernel, 0, inputs, [], last, None, part_bias, part_block)
     low, high, bias_first = lax.optimization_barrier((low, high, bias_first))
     packed = pl.pallas_call(
         atom_kernel,
@@ -608,7 +627,7 @@
         atom_token, single, single_weight, noise_weight, token_weight, cotangent,
     )
     cond, bias_second = pair_call(
-        pair_next_kernel, step, 1, inputs, [], packed, cond, part_bias
+        pair_next_kernel, 1, inputs, [], packed, cond, part_bias, part_block
     )
     packed = lax.all_to_all(packed, PLANE, 0, 0, tiled=True)
     packed, bias_second = lax.optimization_barrier((packed, bias_second))
@@ -618,8 +637,10 @@
     rising = [own, lax.ppermute(own, "z", ahead)]
     falling = [own, lax.ppermute(own, "z", behind)]
     cond, bias = pair_call(
-        pair_last_kernel, step, 2, inputs, [bias_first, bias_second], own, cond,
-        jax.ShapeDtypeStruct((H, tok_rows, cols), jnp.int16), [pltpu.VMEM((H, step, cols), F32)],
+        pair_last_kernel, 2, inputs, [bias_first, bias_second], own, cond,
+        jax.ShapeDtypeStruct((H, tok_rows, cols), jnp.int16),
+        pl.BlockSpec((H, tok_rows, cols), lambda i: (0, 0, 0)),
+        [pltpu.VMEM(part_bias.shape, F32)],
     )
     rising[1], falling[1], bias = lax.optimization_barrier((rising[1], falling[1], bias))
     rising.append(lax.ppermute(rising[1], "z", ahead))

time: 106 us -> 106 us (level)
  no operation moved by 1% of the time
where the time goes in v6:
time: 106 us; the launch traced here: 105 us
  Pallas kernels  42.7 us (40%)
  starting transfers between devices  36.3 us (34%)
  blocking collectives  12.4 us (12%)
  waiting for transfers between devices  8.89 us (8%)
  local copies, waits for them, and re-layouts  3.61 us (3%)
    pallas_call x3, Pallas kernels, pair_call(): pl.pallas_call(kernel, grid=(steps,), out_shape=(jax.ShapeDtypeStruct(pai...  22.1 us
    all_to_all x1, blocking collectives, on_device(): merged = lax.all_to_all(merged, PLANE, 0, 0, tiled=True)  12.4 us
    all_to_all x1, starting transfers between devices, on_device(): packed = lax.all_to_all(packed, PLANE, 0, 0, tiled=True)  8.78 us
    all_to_all x1, starting transfers between devices, on_device(): bias_mine = lax.all_to_all(bias, PLANE, 0, 0, tiled=True)  5.87 us
    pallas_call x1, Pallas kernels, on_device(): pl.pallas_call(atom_kernel, out_shape=jax.ShapeDtypeStruct((H, copies * t...  5.65 us
    pallas_call x1, Pallas kernels, on_device(): pl.pallas_call(attend_kernel, out_shape=(jax.ShapeDtypeStruct((H, tok_row...  5.53 us
    pallas_call x1, Pallas kernels, on_device(): pl.pallas_call(grad_kernel, grid=(steps,), out_shape=(jax.ShapeDtypeStruc...  4.75 us
    all_to_all x1, waiting for transfers between devices, on_device(): bias_mine = lax.all_to_all(bias, PLANE, 0, 0, tiled=True)  4.69 us
  transfers between devices with their start and end apart: 13, of which 5 were waited for; matrix products, arithmetic and copies ran while one was open for 0% of the time, Pallas kernels for 23%

profile of v6, /device:TPU:1, one launch (start us, length us, event | category | flops | bytes accessed | tf_op | source)
XLA Modules:
  0.0 104.6 jit_solution(11334517726739614838)
XLA Ops:
  0.6 1.3 %copy.21.coords = f32[2,3,192]{2,1,0:T(4,128)} copy(f32[2,3,192]{2,0,1:T(2,128)} %param.20) | data formatting | bytes 9216 | tf_op args[3]
  1.9 2.1 %atom_start.1 = (f32[2,192,128]{2,1,0:T(8,128)}, bf16[2,192,128]{2,1,0:T(8,128)(2,1)}, bf16[2,64,128]{2,1,0:T(8,128)(2,1)}, bf16[2,64,128]{2,1,0:T(8,128)(2,1)}) custom-call(s32[2]{0:T(128)} %levels.3, bf16[192,128]{1,0:T(8,128)(2,1)} %feat.1, f32[2,3,192]{2,1,0:T(4,128)} %copy.21.coords, f32[3,128]{1,0:T(4,128)} %coord_weight.1), custom_call_target="tpu_custom_call" | custom-call | flops 1000000 | bytes 500000 | tf_op jit(solution)/shard_map/atom_start/pallas_call | solution.py:591
  4.0 3.9 %collective-permute-start = (bf16[2,64,128]{2,1,0:T(8,128)(2,1)}, bf16[2,64,128]{2,1,0:T(8,128)(2,1)S(1)}, u32[]{:S(2)}, u32[]{:S(2)}) collective-permute-start(bf16[2,64,128]{2,1,0:T(8,128)(2,1)} %get-tuple-element.29.anchor), channel_id=1, source_target_pairs={{0,4},{4,8},{8,12},{12,16},{16,20},{20,24},{24,28},{28,32},{32,36}... | collective-permute-start | bytes 98312 | tf_op jit(solution)/shard_map/ppermute | solution.py:607
  8.0 1.3 %collective-permute-start.1 = (bf16[2,64,128]{2,1,0:T(8,128)(2,1)}, bf16[2,64,128]{2,1,0:T(8,128)(2,1)S(1)}, u32[]{:S(2)}, u32[]{:S(2)}) collective-permute-start(bf16[2,64,128]{2,1,0:T(8,128)(2,1)} %get-tuple-element.30), channel_id=1, source_target_pairs={{4,0},{8,4},{12,8},{16,12},{20,16},{24,20},{28,24},{32,28},{36,32}... | collective-permute-start | bytes 98312 | tf_op jit(solution)/shard_map/ppermute | solution.py:608
  9.3 7.2 %pair_part.3 = (bf16[24,384,128]{2,1,0:T(8,128)(2,1)}, f32[2,16,4,384]{3,2,1,0:T(4,128)}) custom-call(bf16[24,384,128]{2,1,0:T(8,128)(2,1)} %pair.5, bf16[128,1024]{1,0:T(8,128)(2,1)} %trans_in.5, bf16[512,128]{1,0:T(8,128)(2,1)} %trans_out.5, bf16[16,128]{1,0:T(8,128)(2,1)} %bitcast.5, bf16[2,64,128]{2,1,0:T(8,128)(2,1)} %get-tuple-element.29.anchor), custom_call_target="tpu_custom_call" | custom-call | flops 6000000000 | bytes 8000000 | tf_op jit(solution)/shard_map/pair_part/pallas_call | solution.py:357
  16.5 0.0 collective-permute-done.low
  16.5 0.0 copy-start.4
  16.5 0.0 collective-permute-done.1.high
  16.5 0.0 copy-start.5
  16.5 0.6 copy-done.4
  17.1 0.0 copy-done.5
  17.1 5.6 %atom_stage.1.anchor = s16[16,48,256]{2,1,0:T(8,128)(2,1)} custom-call(s32[1]{0:T(128)} %bitcast.3.place, s32[6]{0:T(128)} %offsets.1, s32[2]{0:T(128)} %levels.3, bf16[2,64,128]{2,1,0:T(8,128)(2,1)} %copy-done.4, bf16[2,64,128]{2,1,0:T(8,128)(2,1)} %copy-done.5, bf16[2,192,128]{2,1,0:T(8,128)(2,1)} %get-tuple-element.34.normed, ...), custom_call_target="tpu_custom_call" | custom-call | flops 3000000000 | bytes 6000000 | tf_op jit(solution)/shard_map/atom_stage/pallas_call | solution.py:616
  22.8 8.8 %all-to-all-start = ((s16[16,48,256]{2,1,0:T(8,128)(2,1)}), s16[16,48,256]{2,1,0:T(8,128)(2,1)S(1)}, u32[]{:S(2)}, u32[]{:S(2)}) async-start(s16[16,48,256]{2,1,0:T(8,128)(2,1)} %atom_stage.1.anchor), calls=%async_computation | async-start | bytes 786432 | tf_op jit(solution)/shard_map/all_to_all | solution.py:632
  31.6 7.2 %pair_part.4 = (bf16[24,384,128]{2,1,0:T(8,128)(2,1)}, f32[2,16,4,384]{3,2,1,0:T(4,128)}) custom-call(bf16[24,384,128]{2,1,0:T(8,128)(2,1)} %pair.5, bf16[128,1024]{1,0:T(8,128)(2,1)} %trans_in.5, bf16[512,128]{1,0:T(8,128)(2,1)} %trans_out.5, bf16[16,128]{1,0:T(8,128)(2,1)} %bitcast.6, ...), custom_call_target="tpu_custom_call", output_to_operand_aliasing={{0}: (5, {})} | custom-call | flops 6000000000 | bytes 8000000 | tf_op jit(solution)/shard_map/pair_part/pallas_call | solution.py:357
  38.8 0.8 all-to-all-done.queries
  39.7 0.0 copy-start
  39.7 1.8 %collective-permute-start.2 = (s16[16,48,128]{2,1,0:T(8,128)(2,1)S(1)}, s16[16,48,128]{2,1,0:T(8,128)(2,1)S(1)}, u32[]{:S(2)}, u32[]{:S(2)}) collective-permute-start(s16[16,48,128]{2,1,0:T(8,128)(2,1)S(1)} %slice.3.anchor.kv0), channel_id=1, source_target_pairs={{0,32},{32,64},{64,96},{96,128},{128,160},{160,192},{192,224},{224... | collective-permute-start | bytes 589832 | tf_op jit(solution)/shard_map/ppermute | solution.py:637
  41.4 4.2 %collective-permute-start.3 = (s16[16,48,128]{2,1,0:T(8,128)(2,1)S(1)}, s16[16,48,128]{2,1,0:T(8,128)(2,1)S(1)}, u32[]{:S(2)}, u32[]{:S(2)}) collective-permute-start(s16[16,48,128]{2,1,0:T(8,128)(2,1)S(1)} %slice.3.anchor.kv0), channel_id=1, source_target_pairs={{0,224},{32,0},{64,32},{96,64},{128,96},{160,128},{192,160},{224,1... | collective-permute-start | bytes 589832 | tf_op jit(solution)/shard_map/ppermute | solution.py:638
  45.6 0.0 copy-done
  45.7 7.6 %pair_part.5 = (bf16[24,384,128]{2,1,0:T(8,128)(2,1)}, s16[16,24,384]{2,1,0:T(8,128)(2,1)}) custom-call(bf16[24,384,128]{2,1,0:T(8,128)(2,1)} %pair.5, bf16[128,1024]{1,0:T(8,128)(2,1)} %trans_in.5, bf16[512,128]{1,0:T(8,128)(2,1)} %trans_out.5, bf16[16,128]{1,0:T(8,128)(2,1)} %bitcast.7, ...), custom_call_target="tpu_custom_call", output_to_operand_aliasing={{0}: (5, {})} | custom-call | flops 6000000000 | bytes 8000000 | tf_op jit(solution)/shard_map/pair_part/pallas_call | solution.py:357
  53.3 0.0 collective-permute-done.2.kv1
  53.3 0.0 collective-permute-done.3.kv7
  53.3 0.1 collective-permute-start.4
  53.4 5.9 %all-to-all-start.1 = ((s16[16,24,384]{2,1,0:T(8,128)(2,1)}), s16[16,24,384]{2,1,0:T(8,128)(2,1)S(1)}, u32[]{:S(2)}, u32[]{:S(2)}) async-start(s16[16,24,384]{2,1,0:T(8,128)(2,1)} %get-tuple-element.49), calls=%async_computation.1 | async-start | bytes 589824 | tf_op jit(solution)/shard_map/all_to_all | solution.py:652
  59.3 0.0 collective-permute-done.4.kv2
  59.3 0.8 collective-permute-start.5
  60.1 2.0 %collective-permute-start.7 = (s16[16,48,128]{2,1,0:T(8,128)(2,1)S(1)}, s16[16,48,128]{2,1,0:T(8,128)(2,1)S(1)}, u32[]{:S(2)}, u32[]{:S(2)}) collective-permute-start(s16[16,48,128]{2,1,0:T(8,128)(2,1)S(1)} %collective-permute-done.3.kv7), channel_id=1, source_target_pairs={{0,224},{32,0},{64,32},{96,64},{128,96},{160,128},{192,160},{224,1... | collective-permute-start | bytes 589832 | tf_op jit(solution)/shard_map/ppermute | solution.py:647
  62.1 4.7 %all-to-all-done.1.bias_mine = s16[16,24,384]{2,1,0:T(8,128)(2,1)S(1)} async-done(((s16[16,24,384]{2,1,0:T(8,128)(2,1)}), s16[16,24,384]{2,1,0:T(8,128)(2,1)S(1)}, u32[]{:S(2)}, u32[]{:S(2)}) %all-to-all-start.1) | async-done | bytes 294944 | tf_op jit(solution)/shard_map/all_to_all | solution.py:652
  66.8 3.4 %collective-permute-start.9 = (s16[16,24,384]{2,1,0:T(8,128)(2,1)S(1)}, s16[16,24,384]{2,1,0:T(8,128)(2,1)S(1)}, u32[]{:S(2)}, u32[]{:S(2)}) collective-permute-start(s16[16,24,384]{2,1,0:T(8,128)(2,1)S(1)} %all-to-all-done.1.bias_mine), channel_id=1, source_target_pairs={{0,1},{1,0},{2,3},{3,2},{4,5},{5,4},{6,7},{7,6},{8,9},{9,8},{10,11... | collective-permute-start | bytes 884744 | tf_op jit(solution)/shard_map/ppermute | solution.py:654
  70.2 0.0 collective-permute-done.5.anchor.kv3
  70.2 2.0 %collective-permute-start.6 = (s16[16,48,128]{2,1,0:T(8,128)(2,1)S(1)}, s16[16,48,128]{2,1,0:T(8,128)(2,1)S(1)}, u32[]{:S(2)}, u32[]{:S(2)}) collective-permute-start(s16[16,48,128]{2,1,0:T(8,128)(2,1)S(1)} %collective-permute-done.5.anchor.kv3), channel_id=1, source_target_pairs={{0,32},{32,64},{64,96},{96,128},{128,160},{160,192},{192,224},{224... | collective-permute-start | bytes 589832 | tf_op jit(solution)/shard_map/ppermute | solution.py:650
  72.2 0.0 collective-permute-done.7.kv6
  72.2 1.2 %collective-permute-start.8 = (s16[16,48,128]{2,1,0:T(8,128)(2,1)S(1)}, s16[16,48,128]{2,1,0:T(8,128)(2,1)S(1)}, u32[]{:S(2)}, u32[]{:S(2)}) collective-permute-start(s16[16,48,128]{2,1,0:T(8,128)(2,1)S(1)} %collective-permute-done.7.kv6), channel_id=1, source_target_pairs={{0,224},{32,0},{64,32},{96,64},{128,96},{160,128},{192,160},{224,1... | collective-permute-start | bytes 589832 | tf_op jit(solution)/shard_map/ppermute | solution.py:649
  73.4 0.0 copy-start.3
  73.4 1.7 %copy-done.3 = bf16[24,384,128]{2,1,0:T(8,128)(2,1)S(1)} copy-done((bf16[24,384,128]{2,1,0:T(8,128)(2,1)S(1)}, bf16[24,384,128]{2,1,0:T(8,128)(2,1)}, u32[]{:S(2)}) %copy-start.3) | copy-done | bytes 2359320
  75.1 0.0 copy-start.1
  75.1 2.2 %pair_normal.1 = (f32[6,768,256]{2,1,0:T(8,128)S(1)}, f32[6,768,256]{2,1,0:T(8,128)S(1)}) custom-call(bf16[24,384,128]{2,1,0:T(8,128)(2,1)S(1)} %copy-done.3, s16[16,48,128]{2,1,0:T(8,128)(2,1)S(1)} %collective-permute-done.5.anchor.kv3), custom_call_target="tpu_custom_call" | custom-call | flops 1500000000 | bytes 12000000 | tf_op jit(solution)/shard_map/pair_normal/pallas_call | solution.py:657
  77.3 1.1 %collective-permute-done.6.kv4 = s16[16,48,128]{2,1,0:T(8,128)(2,1)S(1)} collective-permute-done((s16[16,48,128]{2,1,0:T(8,128)(2,1)S(1)}, s16[16,48,128]{2,1,0:T(8,128)(2,1)S(1)}, u32[]{:S(2)}, u32[]{:S(2)}) %collective-permute-start.6) | collective-permute-done | bytes 196640 | tf_op jit(solution)/shard_map/ppermute | solution.py:650
  78.4 0.6 collective-permute-done.8.kv5
  79.0 0.0 collective-permute-done.9.bias_other
  79.0 0.0 copy-done.1
  79.0 0.0 copy-done.2
  79.0 5.5 %token_attention.1 = (f32[16,24,512]{2,1,0:T(8,128)S(1)}, f32[16,24,384]{2,1,0:T(8,128)S(1)}) custom-call(s32[1]{0:T(128)} %bitcast.core_at, s32[1]{0:T(128)} %bitcast.1.head_at, s32[1]{0:T(128)} %bitcast.2.z_at, s16[16,48,256]{2,1,0:T(8,128)(2,1)S(1)} %all-to-all-done.queries, s16[16,48,128]{2,1,0:T(8,128)(2,1)S(1)} %copy-done.1, ...), custom_call_target="tpu_custom_call" | custom-call | flops 4000000000 | bytes 8000000 | tf_op jit(solution)/shard_map/token_attention/pallas_call | solution.py:670
  84.5 0.9 collective-permute-start.10
  85.4 1.6 %collective-permute-done.10.other = f32[16,24,384]{2,1,0:T(8,128)S(1)} collective-permute-done((f32[16,24,384]{2,1,0:T(8,128)S(1)}, f32[16,24,384]{2,1,0:T(8,128)S(1)}, u32[]{:S(2)}, u32[]{:S(2)}) %collective-permute-start.10) | collective-permute-done | bytes 589856 | tf_op jit(solution)/shard_map/ppermute | solution.py:693
  87.0 0.4 gradient_merge.1
  87.5 12.4 %all_to_all.15.packed = s16[16,48,256]{2,1,0:T(8,128)(2,1)S(1)} all-to-all(s16[16,48,256]{2,1,0:T(8,128)(2,1)S(1)} %gradient_merge.1), channel_id=1, replica_groups=mesh['z'=8,'g'=8,'ylo'=2,'core'=2] {'g','ylo'}, dimensions={0} | all-to-all | bytes 786432 | tf_op jit(solution)/shard_map/all_to_all | solution.py:694
  99.9 4.8 %pair_gradient.1 = (bf16[24,384,128]{2,1,0:T(8,128)(2,1)}, bf16[2,24,768]{2,1,0:T(8,128)(2,1)}) custom-call(s16[16,48,256]{2,1,0:T(8,128)(2,1)S(1)} %all_to_all.15.packed, f32[6,768,256]{2,1,0:T(8,128)S(1)} %get-tuple-element.52.normals, f32[6,768,256]{2,1,0:T(8,128)S(1)} %get-tuple-element.53.scales, bf16[16,128]{1,0:T(8,128)(2,1)S(1)} %bitcast.9), custom_call_target="tpu_custom_call" | custom-call | flops 400000000 | bytes 6000000 | tf_op jit(solution)/shard_map/pair_gradient/pallas_call | solution.py:695
  (2 shorter events, 0.0 us)
Async XLA Ops:
  4.0 12.5 %collective-permute-start = (bf16[2,64,128]{2,1,0:T(8,128)(2,1)}, bf16[2,64,128]{2,1,0:T(8,128)(2,1)S(1)}, u32[]{:S(2)}, u32[]{:S(2)}) collective-permute-start(bf16[2,64,128]{2,1,0:T(8,128)(2,1)} %get-tuple-element.29.anchor), channel_id=1, source_target_pairs={{0,4},{4,8},{8,12},{12,16},{16,20},{20,24},{24,28},{28,32},{32,36}... | collective-permute-start | bytes 98312 | tf_op jit(solution)/shard_map/ppermute | solution.py:607
  8.0 8.5 %collective-permute-start.1 = (bf16[2,64,128]{2,1,0:T(8,128)(2,1)}, bf16[2,64,128]{2,1,0:T(8,128)(2,1)S(1)}, u32[]{:S(2)}, u32[]{:S(2)}) collective-permute-start(bf16[2,64,128]{2,1,0:T(8,128)(2,1)} %get-tuple-element.30), channel_id=1, source_target_pairs={{4,0},{8,4},{12,8},{16,12},{20,16},{24,20},{28,24},{32,28},{36,32}... | collective-permute-start | bytes 98312 | tf_op jit(solution)/shard_map/ppermute | solution.py:608
  16.5 0.6 copy-start.4
  16.5 0.6 copy-start.5
  22.8 16.8 %all-to-all-start = ((s16[16,48,256]{2,1,0:T(8,128)(2,1)}), s16[16,48,256]{2,1,0:T(8,128)(2,1)S(1)}, u32[]{:S(2)}, u32[]{:S(2)}) async-start(s16[16,48,256]{2,1,0:T(8,128)(2,1)} %atom_stage.1.anchor), calls=%async_computation | async-start | bytes 786432 | tf_op jit(solution)/shard_map/all_to_all | solution.py:632
  39.7 6.0 %copy-start = (s16[16,48,128]{2,1,0:T(8,128)(2,1)}, s16[16,48,128]{2,1,0:T(8,128)(2,1)S(1)}, u32[]{:S(2)}) copy-start(s16[16,48,128]{2,1,0:T(8,128)(2,1)S(1)} %slice.3.anchor.kv0) | copy-start | bytes 589828
  39.7 13.6 %collective-permute-start.2 = (s16[16,48,128]{2,1,0:T(8,128)(2,1)S(1)}, s16[16,48,128]{2,1,0:T(8,128)(2,1)S(1)}, u32[]{:S(2)}, u32[]{:S(2)}) collective-permute-start(s16[16,48,128]{2,1,0:T(8,128)(2,1)S(1)} %slice.3.anchor.kv0), channel_id=1, source_target_pairs={{0,32},{32,64},{64,96},{96,128},{128,160},{160,192},{192,224},{224... | collective-permute-start | bytes 589832 | tf_op jit(solution)/shard_map/ppermute | solution.py:637
  41.4 11.9 %collective-permute-start.3 = (s16[16,48,128]{2,1,0:T(8,128)(2,1)S(1)}, s16[16,48,128]{2,1,0:T(8,128)(2,1)S(1)}, u32[]{:S(2)}, u32[]{:S(2)}) collective-permute-start(s16[16,48,128]{2,1,0:T(8,128)(2,1)S(1)} %slice.3.anchor.kv0), channel_id=1, source_target_pairs={{0,224},{32,0},{64,32},{96,64},{128,96},{160,128},{192,160},{224,1... | collective-permute-start | bytes 589832 | tf_op jit(solution)/shard_map/ppermute | solution.py:638
  53.3 6.0 %collective-permute-start.4 = (s16[16,48,128]{2,1,0:T(8,128)(2,1)S(1)}, s16[16,48,128]{2,1,0:T(8,128)(2,1)S(1)}, u32[]{:S(2)}, u32[]{:S(2)}) collective-permute-start(s16[16,48,128]{2,1,0:T(8,128)(2,1)S(1)} %collective-permute-done.2.kv1), channel_id=1, source_target_pairs={{0,32},{32,64},{64,96},{96,128},{128,160},{160,192},{192,224},{224... | collective-permute-start | bytes 589832 | tf_op jit(solution)/shard_map/ppermute | solution.py:646
  53.4 13.4 %all-to-all-start.1 = ((s16[16,24,384]{2,1,0:T(8,128)(2,1)}), s16[16,24,384]{2,1,0:T(8,128)(2,1)S(1)}, u32[]{:S(2)}, u32[]{:S(2)}) async-start(s16[16,24,384]{2,1,0:T(8,128)(2,1)} %get-tuple-element.49), calls=%async_computation.1 | async-start | bytes 589824 | tf_op jit(solution)/shard_map/all_to_all | solution.py:652
  59.3 10.9 %collective-permute-start.5 = (s16[16,48,128]{2,1,0:T(8,128)(2,1)S(1)}, s16[16,48,128]{2,1,0:T(8,128)(2,1)S(1)}, u32[]{:S(2)}, u32[]{:S(2)}) collective-permute-start(s16[16,48,128]{2,1,0:T(8,128)(2,1)S(1)} %collective-permute-done.4.kv2), channel_id=1, source_target_pairs={{0,32},{32,64},{64,96},{96,128},{128,160},{160,192},{192,224},{224... | collective-permute-start | bytes 589832 | tf_op jit(solution)/shard_map/ppermute | solution.py:648
  60.1 12.1 %collective-permute-start.7 = (s16[16,48,128]{2,1,0:T(8,128)(2,1)S(1)}, s16[16,48,128]{2,1,0:T(8,128)(2,1)S(1)}, u32[]{:S(2)}, u32[]{:S(2)}) collective-permute-start(s16[16,48,128]{2,1,0:T(8,128)(2,1)S(1)} %collective-permute-done.3.kv7), channel_id=1, source_target_pairs={{0,224},{32,0},{64,32},{96,64},{128,96},{160,128},{192,160},{224,1... | collective-permute-start | bytes 589832 | tf_op jit(solution)/shard_map/ppermute | solution.py:647
  66.8 12.2 %collective-permute-start.9 = (s16[16,24,384]{2,1,0:T(8,128)(2,1)S(1)}, s16[16,24,384]{2,1,0:T(8,128)(2,1)S(1)}, u32[]{:S(2)}, u32[]{:S(2)}) collective-permute-start(s16[16,24,384]{2,1,0:T(8,128)(2,1)S(1)} %all-to-all-done.1.bias_mine), channel_id=1, source_target_pairs={{0,1},{1,0},{2,3},{3,2},{4,5},{5,4},{6,7},{7,6},{8,9},{9,8},{10,11... | collective-permute-start | bytes 884744 | tf_op jit(solution)/shard_map/ppermute | solution.py:654
  70.2 8.2 %collective-permute-start.6 = (s16[16,48,128]{2,1,0:T(8,128)(2,1)S(1)}, s16[16,48,128]{2,1,0:T(8,128)(2,1)S(1)}, u32[]{:S(2)}, u32[]{:S(2)}) collective-permute-start(s16[16,48,128]{2,1,0:T(8,128)(2,1)S(1)} %collective-permute-done.5.anchor.kv3), channel_id=1, source_target_pairs={{0,32},{32,64},{64,96},{96,128},{128,160},{160,192},{192,224},{224... | collective-permute-start | bytes 589832 | tf_op jit(solution)/shard_map/ppermute | solution.py:650
  72.2 6.8 %collective-permute-start.8 = (s16[16,48,128]{2,1,0:T(8,128)(2,1)S(1)}, s16[16,48,128]{2,1,0:T(8,128)(2,1)S(1)}, u32[]{:S(2)}, u32[]{:S(2)}) collective-permute-start(s16[16,48,128]{2,1,0:T(8,128)(2,1)S(1)} %collective-permute-done.7.kv6), channel_id=1, source_target_pairs={{0,224},{32,0},{64,32},{96,64},{128,96},{160,128},{192,160},{224,1... | collective-permute-start | bytes 589832 | tf_op jit(solution)/shard_map/ppermute | solution.py:649
  73.4 1.7 %copy-start.3 = (bf16[24,384,128]{2,1,0:T(8,128)(2,1)S(1)}, bf16[24,384,128]{2,1,0:T(8,128)(2,1)}, u32[]{:S(2)}) copy-start(bf16[24,384,128]{2,1,0:T(8,128)(2,1)} %get-tuple-element.44.cond) | copy-start | bytes 7077892
  75.1 3.9 %copy-start.1 = (s16[16,48,128]{2,1,0:T(8,128)(2,1)S(1)}, s16[16,48,128]{2,1,0:T(8,128)(2,1)}, u32[]{:S(2)}) copy-start(s16[16,48,128]{2,1,0:T(8,128)(2,1)} %copy-done) | copy-start | bytes 589828
  75.1 3.9 %copy-start.2 = (bf16[128,16]{0,1:T(8,128)(2,1)S(1)}, bf16[128,16]{0,1:T(8,128)(2,1)}, u32[]{:S(2)}) copy-start(bf16[128,16]{0,1:T(8,128)(2,1)} %param.26) | copy-start | bytes 12292
  84.5 2.5 %collective-permute-start.10 = (f32[16,24,384]{2,1,0:T(8,128)S(1)}, f32[16,24,384]{2,1,0:T(8,128)S(1)}, u32[]{:S(2)}, u32[]{:S(2)}) collective-permute-start(f32[16,24,384]{2,1,0:T(8,128)S(1)} %get-tuple-element.51), channel_id=1, source_target_pairs={{0,1},{1,0},{2,3},{3,2},{4,5},{5,4},{6,7},{7,6},{8,9},{9,8},{10,11... | collective-permute-start | bytes 1769480 | tf_op jit(solution)/shard_map/ppermute | solution.py:693

commit v7 on v5

--- a/solution.py
+++ b/solution.py
@@ -87,9 +87,11 @@
 def start_kernel(levels, feat, coords, coord_weight, atoms_out, normed_out, first_out, last_out):
     rows = feat.shape[0]
     rim = K_WIN // 2
-    for n in range(coords.shape[0]):
+    for n in range(coords.shape[1]):
         input_scale, _ = noise_parts(levels[n])
-        scaled = coords[n] * input_scale[:, :1]
+        scaled = jnp.concatenate(
+            [coords[x, n : n + 1] for x in range(coords.shape[0])], axis=0
+        ) * input_scale[:, :1]
         atoms = feat[...].astype(F32) + lax.dot_general(
             scaled, coord_weight[...], TN, precision=lax.Precision.HIGHEST, preferred_element_type=F32
         )
@@ -581,7 +583,7 @@
         compiler_params=params(56),
         cost_estimate=pl.CostEstimate(flops=1_000_000, bytes_accessed=500_000, transcendentals=0),
         name="atom_start",
-    )(levels, atom_feat, coords, coord_weight)
+    )(levels, atom_feat, coords.transpose(1, 0, 2), coord_weight)
     forward = [(i, i + 1) for i in range(63)]
     backward = [(i + 1, i) for i in range(63)]
     low = lax.ppermute(last, TILE, forward)

time: 106 us -> 104 us (0.981)
  local copies, waits for them, and re-layouts: 3.61 us -> 2.32 us
    unnamed x13 -> x12, local copies, waits for them, and re-layouts: 3.58 us -> 2.29 us
where the time goes in v7:
time: 104 us; the launch traced here: 103 us
  Pallas kernels  42.2 us (41%)
  starting transfers between devices  35.8 us (34%)
  blocking collectives  12.5 us (12%)
  waiting for transfers between devices  9.47 us (9%)
  local copies, waits for them, and re-layouts  2.32 us (2%)
    pallas_call x3, Pallas kernels, pair_call(): pl.pallas_call(kernel, grid=(1,), out_shape=(jax.ShapeDtypeStruct(pair_re...  21.6 us
    all_to_all x1, blocking collectives, on_device(): merged = lax.all_to_all(merged, PLANE, 0, 0, tiled=True)  12.5 us
    all_to_all x1, starting transfers between devices, on_device(): packed = lax.all_to_all(packed, PLANE, 0, 0, tiled=True)  8.8 us
    all_to_all x1, starting transfers between devices, on_device(): bias_mine = lax.all_to_all(bias, PLANE, 0, 0, tiled=True)  5.82 us
    pallas_call x1, Pallas kernels, on_device(): pl.pallas_call(atom_kernel, out_shape=jax.ShapeDtypeStruct((H, copies * t...  5.64 us
    pallas_call x1, Pallas kernels, on_device(): pl.pallas_call(attend_kernel, out_shape=(jax.ShapeDtypeStruct((H, tok_row...  5.53 us
    pallas_call x1, Pallas kernels, on_device(): pl.pallas_call(grad_kernel, grid=(steps,), out_shape=(jax.ShapeDtypeStruc...  4.75 us
    all_to_all x1, waiting for transfers between devices, on_device(): bias_mine = lax.all_to_all(bias, PLANE, 0, 0, tiled=True)  4.69 us
  transfers between devices with their start and end apart: 13, of which 5 were waited for; matrix products, arithmetic and copies ran while one was open for 0% of the time, Pallas kernels for 23%

profile of v7, /device:TPU:1, one launch (start us, length us, event | category | flops | bytes accessed | tf_op | source)
XLA Modules:
  0.0 103.0 jit_solution(1068307492338969616)
XLA Ops:
  0.6 2.1 %atom_start.1 = (f32[2,192,128]{2,1,0:T(8,128)}, bf16[2,192,128]{2,1,0:T(8,128)(2,1)}, bf16[2,64,128]{2,1,0:T(8,128)(2,1)}, bf16[2,64,128]{2,1,0:T(8,128)(2,1)}) custom-call(s32[2]{0:T(128)} %levels.3, bf16[192,128]{1,0:T(8,128)(2,1)} %feat.1, f32[3,2,192]{2,1,0:T(2,128)} %bitcast.11, f32[3,128]{1,0:T(4,128)} %coord_weight.1), custom_call_target="tpu_custom_call" | custom-call | flops 1000000 | bytes 500000 | tf_op jit(solution)/shard_map/atom_start/pallas_call | solution.py:573
  2.7 3.9 %collective-permute-start = (bf16[2,64,128]{2,1,0:T(8,128)(2,1)}, bf16[2,64,128]{2,1,0:T(8,128)(2,1)S(1)}, u32[]{:S(2)}, u32[]{:S(2)}) collective-permute-start(bf16[2,64,128]{2,1,0:T(8,128)(2,1)} %get-tuple-element.29.anchor), channel_id=1, source_target_pairs={{0,4},{4,8},{8,12},{12,16},{16,20},{20,24},{24,28},{28,32},{32,36}... | collective-permute-start | bytes 98312 | tf_op jit(solution)/shard_map/ppermute | solution.py:589
  6.7 1.3 %collective-permute-start.1 = (bf16[2,64,128]{2,1,0:T(8,128)(2,1)}, bf16[2,64,128]{2,1,0:T(8,128)(2,1)S(1)}, u32[]{:S(2)}, u32[]{:S(2)}) collective-permute-start(bf16[2,64,128]{2,1,0:T(8,128)(2,1)} %get-tuple-element.30), channel_id=1, source_target_pairs={{4,0},{8,4},{12,8},{16,12},{20,16},{24,20},{28,24},{32,28},{36,32}... | collective-permute-start | bytes 98312 | tf_op jit(solution)/shard_map/ppermute | solution.py:590
  8.0 7.2 %pair_part.3 = (bf16[24,384,128]{2,1,0:T(8,128)(2,1)}, f32[16,8,384]{2,1,0:T(8,128)}) custom-call(bf16[24,384,128]{2,1,0:T(8,128)(2,1)} %pair.5, bf16[128,1024]{1,0:T(8,128)(2,1)} %trans_in.5, bf16[512,128]{1,0:T(8,128)(2,1)} %trans_out.5, bf16[16,128]{1,0:T(8,128)(2,1)} %bitcast.6, bf16[2,64,128]{2,1,0:T(8,128)(2,1)} %get-tuple-element.29.anchor), custom_call_target="tpu_custom_call" | custom-call | flops 6000000000 | bytes 8000000 | tf_op jit(solution)/shard_map/pair_part/pallas_call | solution.py:339
  15.1 0.0 collective-permute-done.low
  15.1 0.0 copy-start.4
  15.1 0.0 collective-permute-done.1.high
  15.1 0.0 copy-start.5
  15.1 0.6 copy-done.4
  15.7 0.0 copy-done.5
  15.7 5.6 %atom_stage.1.anchor = s16[16,48,256]{2,1,0:T(8,128)(2,1)} custom-call(s32[1]{0:T(128)} %bitcast.3.place, s32[6]{0:T(128)} %offsets.1, s32[2]{0:T(128)} %levels.3, bf16[2,64,128]{2,1,0:T(8,128)(2,1)} %copy-done.4, bf16[2,64,128]{2,1,0:T(8,128)(2,1)} %copy-done.5, bf16[2,192,128]{2,1,0:T(8,128)(2,1)} %get-tuple-element.34.normed, ...), custom_call_target="tpu_custom_call" | custom-call | flops 3000000000 | bytes 6000000 | tf_op jit(solution)/shard_map/atom_stage/pallas_call | solution.py:599
  21.4 8.8 %all-to-all-start = ((s16[16,48,256]{2,1,0:T(8,128)(2,1)}), s16[16,48,256]{2,1,0:T(8,128)(2,1)S(1)}, u32[]{:S(2)}, u32[]{:S(2)}) async-start(s16[16,48,256]{2,1,0:T(8,128)(2,1)} %atom_stage.1.anchor), calls=%async_computation | async-start | bytes 786432 | tf_op jit(solution)/shard_map/all_to_all | solution.py:615
  30.2 7.1 %pair_part.4 = (bf16[24,384,128]{2,1,0:T(8,128)(2,1)}, f32[16,8,384]{2,1,0:T(8,128)}) custom-call(bf16[24,384,128]{2,1,0:T(8,128)(2,1)} %pair.5, bf16[128,1024]{1,0:T(8,128)(2,1)} %trans_in.5, bf16[512,128]{1,0:T(8,128)(2,1)} %trans_out.5, bf16[16,128]{1,0:T(8,128)(2,1)} %bitcast.7, ...), custom_call_target="tpu_custom_call", output_to_operand_aliasing={{0}: (5, {})} | custom-call | flops 6000000000 | bytes 8000000 | tf_op jit(solution)/shard_map/pair_part/pallas_call | solution.py:339
  37.3 0.9 all-to-all-done.queries
  38.3 0.0 copy-start
  38.3 1.8 %collective-permute-start.2 = (s16[16,48,128]{2,1,0:T(8,128)(2,1)S(1)}, s16[16,48,128]{2,1,0:T(8,128)(2,1)S(1)}, u32[]{:S(2)}, u32[]{:S(2)}) collective-permute-start(s16[16,48,128]{2,1,0:T(8,128)(2,1)S(1)} %slice.3.anchor.kv0), channel_id=1, source_target_pairs={{0,32},{32,64},{64,96},{96,128},{128,160},{160,192},{192,224},{224... | collective-permute-start | bytes 589832 | tf_op jit(solution)/shard_map/ppermute | solution.py:620
  40.1 4.0 %collective-permute-start.3 = (s16[16,48,128]{2,1,0:T(8,128)(2,1)S(1)}, s16[16,48,128]{2,1,0:T(8,128)(2,1)S(1)}, u32[]{:S(2)}, u32[]{:S(2)}) collective-permute-start(s16[16,48,128]{2,1,0:T(8,128)(2,1)S(1)} %slice.3.anchor.kv0), channel_id=1, source_target_pairs={{0,224},{32,0},{64,32},{96,64},{128,96},{160,128},{192,160},{224,1... | collective-permute-start | bytes 589832 | tf_op jit(solution)/shard_map/ppermute | solution.py:621
  44.1 0.0 copy-done
  44.1 7.3 %pair_part.5 = (bf16[24,384,128]{2,1,0:T(8,128)(2,1)}, s16[16,24,384]{2,1,0:T(8,128)(2,1)}) custom-call(bf16[24,384,128]{2,1,0:T(8,128)(2,1)} %pair.5, bf16[128,1024]{1,0:T(8,128)(2,1)} %trans_in.5, bf16[512,128]{1,0:T(8,128)(2,1)} %trans_out.5, bf16[16,128]{1,0:T(8,128)(2,1)} %bitcast.8, ...), custom_call_target="tpu_custom_call", output_to_operand_aliasing={{0}: (5, {})} | custom-call | flops 6000000000 | bytes 8000000 | tf_op jit(solution)/shard_map/pair_part/pallas_call | solution.py:339
  51.4 0.0 collective-permute-done.2.kv1
  51.4 0.0 collective-permute-done.3.kv7
  51.4 0.1 collective-permute-start.4
  51.5 5.8 %all-to-all-start.1 = ((s16[16,24,384]{2,1,0:T(8,128)(2,1)}), s16[16,24,384]{2,1,0:T(8,128)(2,1)S(1)}, u32[]{:S(2)}, u32[]{:S(2)}) async-start(s16[16,24,384]{2,1,0:T(8,128)(2,1)} %get-tuple-element.49), calls=%async_computation.1 | async-start | bytes 589824 | tf_op jit(solution)/shard_map/all_to_all | solution.py:633
  57.3 0.0 collective-permute-done.4.kv2
  57.3 1.1 %collective-permute-start.5 = (s16[16,48,128]{2,1,0:T(8,128)(2,1)S(1)}, s16[16,48,128]{2,1,0:T(8,128)(2,1)S(1)}, u32[]{:S(2)}, u32[]{:S(2)}) collective-permute-start(s16[16,48,128]{2,1,0:T(8,128)(2,1)S(1)} %collective-permute-done.4.kv2), channel_id=1, source_target_pairs={{0,32},{32,64},{64,96},{96,128},{128,160},{160,192},{192,224},{224... | collective-permute-start | bytes 589832 | tf_op jit(solution)/shard_map/ppermute | solution.py:629
  58.4 1.7 %collective-permute-start.7 = (s16[16,48,128]{2,1,0:T(8,128)(2,1)S(1)}, s16[16,48,128]{2,1,0:T(8,128)(2,1)S(1)}, u32[]{:S(2)}, u32[]{:S(2)}) collective-permute-start(s16[16,48,128]{2,1,0:T(8,128)(2,1)S(1)} %collective-permute-done.3.kv7), channel_id=1, source_target_pairs={{0,224},{32,0},{64,32},{96,64},{128,96},{160,128},{192,160},{224,1... | collective-permute-start | bytes 589832 | tf_op jit(solution)/shard_map/ppermute | solution.py:628
  60.2 4.7 %all-to-all-done.1.bias_mine = s16[16,24,384]{2,1,0:T(8,128)(2,1)S(1)} async-done(((s16[16,24,384]{2,1,0:T(8,128)(2,1)}), s16[16,24,384]{2,1,0:T(8,128)(2,1)S(1)}, u32[]{:S(2)}, u32[]{:S(2)}) %all-to-all-start.1) | async-done | bytes 294944 | tf_op jit(solution)/shard_map/all_to_all | solution.py:633
  64.9 3.4 %collective-permute-start.9 = (s16[16,24,384]{2,1,0:T(8,128)(2,1)S(1)}, s16[16,24,384]{2,1,0:T(8,128)(2,1)S(1)}, u32[]{:S(2)}, u32[]{:S(2)}) collective-permute-start(s16[16,24,384]{2,1,0:T(8,128)(2,1)S(1)} %all-to-all-done.1.bias_mine), channel_id=1, source_target_pairs={{0,1},{1,0},{2,3},{3,2},{4,5},{5,4},{6,7},{7,6},{8,9},{9,8},{10,11... | collective-permute-start | bytes 884744 | tf_op jit(solution)/shard_map/ppermute | solution.py:635
  68.2 0.0 collective-permute-done.5.anchor.kv3
  68.3 2.3 %collective-permute-start.6 = (s16[16,48,128]{2,1,0:T(8,128)(2,1)S(1)}, s16[16,48,128]{2,1,0:T(8,128)(2,1)S(1)}, u32[]{:S(2)}, u32[]{:S(2)}) collective-permute-start(s16[16,48,128]{2,1,0:T(8,128)(2,1)S(1)} %collective-permute-done.5.anchor.kv3), channel_id=1, source_target_pairs={{0,32},{32,64},{64,96},{96,128},{128,160},{160,192},{192,224},{224... | collective-permute-start | bytes 589832 | tf_op jit(solution)/shard_map/ppermute | solution.py:631
  70.5 0.0 collective-permute-done.7.kv6
  70.5 0.7 collective-permute-start.8
  71.3 0.0 copy-start.3
  71.3 1.7 %copy-done.3 = bf16[24,384,128]{2,1,0:T(8,128)(2,1)S(1)} copy-done((bf16[24,384,128]{2,1,0:T(8,128)(2,1)S(1)}, bf16[24,384,128]{2,1,0:T(8,128)(2,1)}, u32[]{:S(2)}) %copy-start.3) | copy-done | bytes 2359320
  72.9 0.0 copy-start.1
  72.9 0.0 copy-start.2
  72.9 2.2 %pair_normal.1 = (f32[6,768,256]{2,1,0:T(8,128)S(1)}, f32[6,768,256]{2,1,0:T(8,128)S(1)}) custom-call(bf16[24,384,128]{2,1,0:T(8,128)(2,1)S(1)} %copy-done.3, s16[16,48,128]{2,1,0:T(8,128)(2,1)S(1)} %collective-permute-done.5.anchor.kv3), custom_call_target="tpu_custom_call" | custom-call | flops 1500000000 | bytes 12000000 | tf_op jit(solution)/shard_map/pair_normal/pallas_call | solution.py:638
  75.1 1.2 %collective-permute-done.6.kv4 = s16[16,48,128]{2,1,0:T(8,128)(2,1)S(1)} collective-permute-done((s16[16,48,128]{2,1,0:T(8,128)(2,1)S(1)}, s16[16,48,128]{2,1,0:T(8,128)(2,1)S(1)}, u32[]{:S(2)}, u32[]{:S(2)}) %collective-permute-start.6) | collective-permute-done | bytes 196640 | tf_op jit(solution)/shard_map/ppermute | solution.py:631
  76.3 1.0 collective-permute-done.8.kv5
  77.3 0.0 collective-permute-done.9.bias_other
  77.3 0.0 copy-done.1
  77.3 0.0 copy-done.2
  77.3 5.5 %token_attention.1 = (f32[16,24,512]{2,1,0:T(8,128)S(1)}, f32[16,24,384]{2,1,0:T(8,128)S(1)}) custom-call(s32[1]{0:T(128)} %bitcast.core_at, s32[1]{0:T(128)} %bitcast.1.head_at, s32[1]{0:T(128)} %bitcast.2.z_at, s16[16,48,256]{2,1,0:T(8,128)(2,1)S(1)} %all-to-all-done.queries, s16[16,48,128]{2,1,0:T(8,128)(2,1)S(1)} %copy-done.1, ...), custom_call_target="tpu_custom_call" | custom-call | flops 4000000000 | bytes 8000000 | tf_op jit(solution)/shard_map/token_attention/pallas_call | solution.py:651
  82.9 0.9 collective-permute-start.10
  83.7 1.6 %collective-permute-done.10.other = f32[16,24,384]{2,1,0:T(8,128)S(1)} collective-permute-done((f32[16,24,384]{2,1,0:T(8,128)S(1)}, f32[16,24,384]{2,1,0:T(8,128)S(1)}, u32[]{:S(2)}, u32[]{:S(2)}) %collective-permute-start.10) | collective-permute-done | bytes 589856 | tf_op jit(solution)/shard_map/ppermute | solution.py:674
  85.4 0.4 gradient_merge.1
  85.8 12.5 %all_to_all.15.packed = s16[16,48,256]{2,1,0:T(8,128)(2,1)S(1)} all-to-all(s16[16,48,256]{2,1,0:T(8,128)(2,1)S(1)} %gradient_merge.1), channel_id=1, replica_groups=mesh['z'=8,'g'=8,'ylo'=2,'core'=2] {'g','ylo'}, dimensions={0} | all-to-all | bytes 786432 | tf_op jit(solution)/shard_map/all_to_all | solution.py:675
  98.2 4.8 %pair_gradient.1 = (bf16[24,384,128]{2,1,0:T(8,128)(2,1)}, bf16[2,24,768]{2,1,0:T(8,128)(2,1)}) custom-call(s16[16,48,256]{2,1,0:T(8,128)(2,1)S(1)} %all_to_all.15.packed, f32[6,768,256]{2,1,0:T(8,128)S(1)} %get-tuple-element.52.normals, f32[6,768,256]{2,1,0:T(8,128)S(1)} %get-tuple-element.53.scales, bf16[16,128]{1,0:T(8,128)(2,1)S(1)} %bitcast.10), custom_call_target="tpu_custom_call" | custom-call | flops 400000000 | bytes 6000000 | tf_op jit(solution)/shard_map/pair_gradient/pallas_call | solution.py:676
  (1 shorter events, 0.0 us)
Async XLA Ops:
  2.7 12.4 %collective-permute-start = (bf16[2,64,128]{2,1,0:T(8,128)(2,1)}, bf16[2,64,128]{2,1,0:T(8,128)(2,1)S(1)}, u32[]{:S(2)}, u32[]{:S(2)}) collective-permute-start(bf16[2,64,128]{2,1,0:T(8,128)(2,1)} %get-tuple-element.29.anchor), channel_id=1, source_target_pairs={{0,4},{4,8},{8,12},{12,16},{16,20},{20,24},{24,28},{28,32},{32,36}... | collective-permute-start | bytes 98312 | tf_op jit(solution)/shard_map/ppermute | solution.py:589
  6.7 8.5 %collective-permute-start.1 = (bf16[2,64,128]{2,1,0:T(8,128)(2,1)}, bf16[2,64,128]{2,1,0:T(8,128)(2,1)S(1)}, u32[]{:S(2)}, u32[]{:S(2)}) collective-permute-start(bf16[2,64,128]{2,1,0:T(8,128)(2,1)} %get-tuple-element.30), channel_id=1, source_target_pairs={{4,0},{8,4},{12,8},{16,12},{20,16},{24,20},{28,24},{32,28},{36,32}... | collective-permute-start | bytes 98312 | tf_op jit(solution)/shard_map/ppermute | solution.py:590
  15.1 0.6 copy-start.4
  15.1 0.6 copy-start.5
  21.4 16.9 %all-to-all-start = ((s16[16,48,256]{2,1,0:T(8,128)(2,1)}), s16[16,48,256]{2,1,0:T(8,128)(2,1)S(1)}, u32[]{:S(2)}, u32[]{:S(2)}) async-start(s16[16,48,256]{2,1,0:T(8,128)(2,1)} %atom_stage.1.anchor), calls=%async_computation | async-start | bytes 786432 | tf_op jit(solution)/shard_map/all_to_all | solution.py:615
  38.3 5.8 %copy-start = (s16[16,48,128]{2,1,0:T(8,128)(2,1)}, s16[16,48,128]{2,1,0:T(8,128)(2,1)S(1)}, u32[]{:S(2)}) copy-start(s16[16,48,128]{2,1,0:T(8,128)(2,1)S(1)} %slice.3.anchor.kv0) | copy-start | bytes 589828
  38.3 13.1 %collective-permute-start.2 = (s16[16,48,128]{2,1,0:T(8,128)(2,1)S(1)}, s16[16,48,128]{2,1,0:T(8,128)(2,1)S(1)}, u32[]{:S(2)}, u32[]{:S(2)}) collective-permute-start(s16[16,48,128]{2,1,0:T(8,128)(2,1)S(1)} %slice.3.anchor.kv0), channel_id=1, source_target_pairs={{0,32},{32,64},{64,96},{96,128},{128,160},{160,192},{192,224},{224... | collective-permute-start | bytes 589832 | tf_op jit(solution)/shard_map/ppermute | solution.py:620
  40.1 11.3 %collective-permute-start.3 = (s16[16,48,128]{2,1,0:T(8,128)(2,1)S(1)}, s16[16,48,128]{2,1,0:T(8,128)(2,1)S(1)}, u32[]{:S(2)}, u32[]{:S(2)}) collective-permute-start(s16[16,48,128]{2,1,0:T(8,128)(2,1)S(1)} %slice.3.anchor.kv0), channel_id=1, source_target_pairs={{0,224},{32,0},{64,32},{96,64},{128,96},{160,128},{192,160},{224,1... | collective-permute-start | bytes 589832 | tf_op jit(solution)/shard_map/ppermute | solution.py:621
  51.4 5.9 %collective-permute-start.4 = (s16[16,48,128]{2,1,0:T(8,128)(2,1)S(1)}, s16[16,48,128]{2,1,0:T(8,128)(2,1)S(1)}, u32[]{:S(2)}, u32[]{:S(2)}) collective-permute-start(s16[16,48,128]{2,1,0:T(8,128)(2,1)S(1)} %collective-permute-done.2.kv1), channel_id=1, source_target_pairs={{0,32},{32,64},{64,96},{96,128},{128,160},{160,192},{192,224},{224... | collective-permute-start | bytes 589832 | tf_op jit(solution)/shard_map/ppermute | solution.py:627
  51.5 13.3 %all-to-all-start.1 = ((s16[16,24,384]{2,1,0:T(8,128)(2,1)}), s16[16,24,384]{2,1,0:T(8,128)(2,1)S(1)}, u32[]{:S(2)}, u32[]{:S(2)}) async-start(s16[16,24,384]{2,1,0:T(8,128)(2,1)} %get-tuple-element.49), calls=%async_computation.1 | async-start | bytes 589824 | tf_op jit(solution)/shard_map/all_to_all | solution.py:633
  57.3 10.9 %collective-permute-start.5 = (s16[16,48,128]{2,1,0:T(8,128)(2,1)S(1)}, s16[16,48,128]{2,1,0:T(8,128)(2,1)S(1)}, u32[]{:S(2)}, u32[]{:S(2)}) collective-permute-start(s16[16,48,128]{2,1,0:T(8,128)(2,1)S(1)} %collective-permute-done.4.kv2), channel_id=1, source_target_pairs={{0,32},{32,64},{64,96},{96,128},{128,160},{160,192},{192,224},{224... | collective-permute-start | bytes 589832 | tf_op jit(solution)/shard_map/ppermute | solution.py:629
  58.4 12.1 %collective-permute-start.7 = (s16[16,48,128]{2,1,0:T(8,128)(2,1)S(1)}, s16[16,48,128]{2,1,0:T(8,128)(2,1)S(1)}, u32[]{:S(2)}, u32[]{:S(2)}) collective-permute-start(s16[16,48,128]{2,1,0:T(8,128)(2,1)S(1)} %collective-permute-done.3.kv7), channel_id=1, source_target_pairs={{0,224},{32,0},{64,32},{96,64},{128,96},{160,128},{192,160},{224,1... | collective-permute-start | bytes 589832 | tf_op jit(solution)/shard_map/ppermute | solution.py:628
  64.9 12.5 %collective-permute-start.9 = (s16[16,24,384]{2,1,0:T(8,128)(2,1)S(1)}, s16[16,24,384]{2,1,0:T(8,128)(2,1)S(1)}, u32[]{:S(2)}, u32[]{:S(2)}) collective-permute-start(s16[16,24,384]{2,1,0:T(8,128)(2,1)S(1)} %all-to-all-done.1.bias_mine), channel_id=1, source_target_pairs={{0,1},{1,0},{2,3},{3,2},{4,5},{5,4},{6,7},{7,6},{8,9},{9,8},{10,11... | collective-permute-start | bytes 884744 | tf_op jit(solution)/shard_map/ppermute | solution.py:635
  68.3 8.1 %collective-permute-start.6 = (s16[16,48,128]{2,1,0:T(8,128)(2,1)S(1)}, s16[16,48,128]{2,1,0:T(8,128)(2,1)S(1)}, u32[]{:S(2)}, u32[]{:S(2)}) collective-permute-start(s16[16,48,128]{2,1,0:T(8,128)(2,1)S(1)} %collective-permute-done.5.anchor.kv3), channel_id=1, source_target_pairs={{0,32},{32,64},{64,96},{96,128},{128,160},{160,192},{192,224},{224... | collective-permute-start | bytes 589832 | tf_op jit(solution)/shard_map/ppermute | solution.py:631
  70.5 6.8 %collective-permute-start.8 = (s16[16,48,128]{2,1,0:T(8,128)(2,1)S(1)}, s16[16,48,128]{2,1,0:T(8,128)(2,1)S(1)}, u32[]{:S(2)}, u32[]{:S(2)}) collective-permute-start(s16[16,48,128]{2,1,0:T(8,128)(2,1)S(1)} %collective-permute-done.7.kv6), channel_id=1, source_target_pairs={{0,224},{32,0},{64,32},{96,64},{128,96},{160,128},{192,160},{224,1... | collective-permute-start | bytes 589832 | tf_op jit(solution)/shard_map/ppermute | solution.py:630
  71.3 1.7 %copy-start.3 = (bf16[24,384,128]{2,1,0:T(8,128)(2,1)S(1)}, bf16[24,384,128]{2,1,0:T(8,128)(2,1)}, u32[]{:S(2)}) copy-start(bf16[24,384,128]{2,1,0:T(8,128)(2,1)} %get-tuple-element.44.cond) | copy-start | bytes 7077892
  72.9 4.4 %copy-start.1 = (s16[16,48,128]{2,1,0:T(8,128)(2,1)S(1)}, s16[16,48,128]{2,1,0:T(8,128)(2,1)}, u32[]{:S(2)}) copy-start(s16[16,48,128]{2,1,0:T(8,128)(2,1)} %copy-done) | copy-start | bytes 589828
  72.9 4.4 %copy-start.2 = (bf16[128,16]{0,1:T(8,128)(2,1)S(1)}, bf16[128,16]{0,1:T(8,128)(2,1)}, u32[]{:S(2)}) copy-start(bf16[128,16]{0,1:T(8,128)(2,1)} %param.26) | copy-start | bytes 12292
  82.9 2.5 %collective-permute-start.10 = (f32[16,24,384]{2,1,0:T(8,128)S(1)}, f32[16,24,384]{2,1,0:T(8,128)S(1)}, u32[]{:S(2)}, u32[]{:S(2)}) collective-permute-start(f32[16,24,384]{2,1,0:T(8,128)S(1)} %get-tuple-element.51), channel_id=1, source_target_pairs={{0,1},{1,0},{2,3},{3,2},{4,5},{5,4},{6,7},{7,6},{8,9},{9,8},{10,11... | collective-permute-start | bytes 1769480 | tf_op jit(solution)/shard_map/ppermute | solution.py:674
